TPU v7x, 256 devices: a whole 4x4x8 slice. The times are simulated.
256 devices in a mesh: span: 4 (over x), tile: 64 (over y, z, core).
Axes of the slice: x: 4, y: 4, z: 8, core: 2. Of those that a mesh axis runs over, the one named last changes fastest.
Arguments:
- latents: bfloat16 [8, 128, 64, 384], P('span', 'tile'), may hold values from -6 to 6
- gain_first: float32 [384], replicated, may hold values from 0.1 to 1.9
- conv_first: bfloat16 [3, 3, 3, 384, 384], P(None, None, None, 'tile'), may hold values from -0.0625 to 0.0625
- bias_first: float32 [384], replicated, may hold values from -3 to 3
- gain_second: float32 [384], replicated, may hold values from 0.1 to 1.9
- conv_second: bfloat16 [3, 3, 3, 384, 384], P(None, None, None, 'tile'), may hold values from -0.0625 to 0.0625
- bias_second: float32 [384], replicated, may hold values from -3 to 3
Outputs:
- decoded: bfloat16 [8, 128, 64, 384], P('span', 'tile')
All inputs are finite; a program needn't handle non-finite values.
Results may differ from a plain program's by a relative error of at most 0.0034.
Values may be sent and summed in bfloat16 or wider, within the bound.
A program may use at most 128 MiB of HBM per device.

v0:
```python
import jax
import jax.numpy as jnp
from jax import lax
from jax.sharding import PartitionSpec as P


def from_behind(value, axis, by):
    size = lax.axis_size(axis)
    pairs = [(i, i + by) for i in range(size) if 0 <= i + by < size]
    return lax.ppermute(value, axis, pairs)


def extended(value, sides, width):
    for axis, dim in sides:
        size, length = (lax.axis_size(axis), value.shape[dim])
        up = [(i, (i + 1) % size) for i in range(size - 1)]
        down = [(j, i) for i, j in up]
        last = lax.slice_in_dim(value, length - width, length, axis=dim)
        first = lax.slice_in_dim(value, 0, width, axis=dim)
        before = lax.ppermute(last, axis, up)
        after = lax.ppermute(first, axis, down)
        value = jnp.concatenate([before, value, after], axis=dim)
    return value


def activate(values, gain):
    mean_square = jnp.mean(values * values, axis=-1, keepdims=True)
    scaled = values * lax.rsqrt(mean_square + 1e-06) * gain
    return jax.nn.silu(scaled).astype(jnp.bfloat16)


def frame_stack(active):
    history = from_behind(active, "span", 1)
    frames = jnp.concatenate([history, active], axis=0)
    padded = extended(frames, (("tile", 1),), 1)
    return jnp.pad(padded, ((0, 0), (0, 0), (1, 1), (0, 0)))


def gather_taps(padded, count, rows, cols):
    offset = padded.shape[0] - count - 2
    per_frame = []
    for frame in range(count):
        views = [
            padded[offset + frame + depth, lift : lift + rows, slide : slide + cols, :]
            for depth in range(3)
            for lift in range(3)
            for slide in range(3)
        ]
        per_frame.append(jnp.stack(views, axis=2))
    stacked = jnp.stack(per_frame, axis=0)
    return stacked.reshape(count * rows * cols, 27, padded.shape[3])


def convolve(patches, kernel, bias):
    channels = kernel.shape[4]
    piece = lax.all_gather(kernel, "tile", axis=3, tiled=True)
    width_in = piece.shape[3]
    flat = patches.reshape(patches.shape[0], 27 * width_in)
    summed = jnp.dot(
        flat, piece.reshape(27 * width_in, channels), preferred_element_type=jnp.float32
    )
    return summed + bias


def per_device(latents, gain_first, conv_first, bias_first, gain_second, conv_second, bias_second):
    count = latents.shape[0]
    rows = latents.shape[1]
    cols = latents.shape[2]
    kernel_one, kernel_two = (conv_first, conv_second)
    base = latents.astype(jnp.float32)
    active_first = activate(base, gain_first)
    hidden_first = convolve(
        gather_taps(frame_stack(active_first), count, rows, cols), kernel_one, bias_first
    )
    active_second = activate(hidden_first.reshape(latents.shape), gain_second)
    hidden_second = convolve(
        gather_taps(frame_stack(active_second), count, rows, cols), kernel_two, bias_second
    )
    return (base + hidden_second.reshape(latents.shape)).astype(jnp.bfloat16)


def solution(mesh):
    in_specs = (
        P("span", "tile", None, None),
        P(),
        P(None, None, None, "tile", None),
        P(),
        P(),
        P(None, None, None, "tile", None),
        P(),
    )
    out_specs = P("span", "tile", None, None)
    return jax.shard_map(
        per_device, mesh=mesh, in_specs=in_specs, out_specs=out_specs, check_vma=False
    )
```

profile of v0, /device:TPU:1, one launch (start us, length us, event | category | flops | bytes accessed | tf_op | source)
XLA Modules:
  0.0 215.1 jit_solution(12131984113702191359)
XLA Ops:
  6.5 0.0 all-gather.3.cloned.1.call-start
  6.5 1.6 copy.15
  8.2 0.0 all-gather.3.cloned.1.call-update
  8.2 0.0 all-gather.5.cloned.1.call-start
  8.3 1.7 copy.18
  9.9 0.0 all-gather.5.cloned.1.call-update
  9.9 1.0 fusion.11
  11.0 1.1 fusion.18
  12.1 4.0 %collective-permute-start = (bf16[2,2,64,384]{3,2,1,0:T(8,128)(2,1)S(1)}, bf16[2,2,64,384]{3,2,1,0:T(8,128)(2,1)S(1)}, u32[]{:S(2)}, u32[]{:S(2)}) collective-permute-start(bf16[2,2,64,384]{3,2,1,0:T(8,128)(2,1)S(1)} %fusion.18), channel_id=1, source_target_pairs={{0,64},{64,128},{128,192},{1,65},{65,129},{129,193},{2,66},{66,130... | collective-permute-start | bytes 589832 | tf_op jit(solution)/shard_map/ppermute | solution.py:10
  16.1 3.5 %collective-permute-done = bf16[2,2,64,384]{3,2,1,0:T(8,128)(2,1)S(1)} collective-permute-done((bf16[2,2,64,384]{3,2,1,0:T(8,128)(2,1)S(1)}, bf16[2,2,64,384]{3,2,1,0:T(8,128)(2,1)S(1)}, u32[]{:S(2)}, u32[]{:S(2)}) %collective-permute-start) | collective-permute-done | bytes 196640 | tf_op jit(solution)/shard_map/ppermute | solution.py:10
  19.7 5.0 %collective-permute-start.1 = (bf16[4,1,64,384]{3,2,1,0:T(8,128)(2,1)S(1)}, bf16[4,1,64,384]{3,2,1,0:T(8,128)(2,1)S(1)}, u32[]{:S(2)}, u32[]{:S(2)}) collective-permute-start(bf16[4,1,64,384]{3,2,1,0:T(8,128)(2,1)S(1)} %get-tuple-element.71), channel_id=1, source_target_pairs={{0,1},{1,2},{2,3},{3,4},{4,5},{5,6},{6,7},{7,8},{8,9},{9,10},{10,1... | collective-permute-start | bytes 589832 | tf_op jit(solution)/shard_map/ppermute | solution.py:20
  24.7 1.9 collective-permute-start.2
  26.6 0.7 collective-permute-done.1
  27.3 5.0 %collective-permute-done.2 = bf16[4,1,64,384]{3,2,1,0:T(8,128)(2,1)S(1)} collective-permute-done((bf16[4,1,64,384]{3,2,1,0:T(8,128)(2,1)S(1)}, bf16[4,1,64,384]{3,2,1,0:T(8,128)(2,1)S(1)}, u32[]{:S(2)}, u32[]{:S(2)}) %collective-permute-start.2) | collective-permute-done | bytes 196640 | tf_op jit(solution)/shard_map/ppermute | solution.py:21
  32.3 0.3 fusion.8
  34.0 0.6 pad_maximum_fusion
  34.6 3.4 %copy.14 = bf16[2,2,64,27,384]{4,3,2,1,0:T(8,128)(2,1)S(1)} copy(bf16[2,2,64,27,384]{4,2,1,3,0:T(8,128)(2,1)S(1)} %pad_maximum_fusion) | data formatting | bytes 10616832 | tf_op jit(solution)/shard_map/stack | solution.py:50
  38.0 4.7 %copy.20 = bf16[32,8,27,384]{3,1,2,0:T(8,128)(2,1)} copy(bf16[32,8,27,384]{3,2,1,0:T(8,128)(2,1)S(1)} %bitcast.354) | data formatting | bytes 10616832
  42.7 0.0 copy-start.2
  42.7 58.0 %all-gather.3.cloned.1.call-done = bf16[3,3,3,384,384]{4,2,1,0,3:T(4,128)(2,1)} async-done(((bf16[3,3,3,6,384]{4,2,1,0,3:T(4,128)(2,1)}), bf16[3,3,3,384,384]{4,2,1,0,3:T(4,128)(2,1)}) %all-gather.3.cloned.1.call-update) | async-done | bytes 7962640 | tf_op jit(solution)/shard_map/all_gather | solution.py:56
  100.8 8.8 %copy.16 = bf16[3,3,3,384,384]{4,3,2,1,0:T(8,128)(2,1)} copy(bf16[3,3,3,384,384]{4,2,1,0,3:T(4,128)(2,1)} %all-gather.3.cloned.1.call-done) | data formatting | bytes 15925248 | tf_op jit(solution)/shard_map/all_gather | solution.py:56
  109.5 0.0 copy-done.2
  109.5 0.0 copy-start.1
  109.5 7.5 %multiply_reduce_fusion = (f32[256]{0:T(256)S(1)}, f32[256,384]{1,0:T(8,128)S(1)}) fusion(f32[384]{0:T(512)S(1)} %copy-done.2, bf16[256,10368]{1,0:T(8,128)(2,1)} %bitcast.360, bf16[10368,384]{1,0:T(8,128)(2,1)} %bitcast.359), kind=kOutput, calls=%fused_computation.36 | convolution fusion | flops 2038726400 | bytes 13666816 | tf_op jit(solution)/shard_map/dot_general | solution.py:59
  117.0 0.1 rsqrt.21
  117.1 0.0 copy-done.1
  117.1 0.2 multiply_convert_fusion
  117.3 3.1 %collective-permute-start.3 = (bf16[2,2,64,384]{3,2,1,0:T(8,128)(2,1)S(1)}, bf16[2,2,64,384]{3,2,1,0:T(8,128)(2,1)S(1)}, u32[]{:S(2)}, u32[]{:S(2)}) collective-permute-start(bf16[2,2,64,384]{3,2,1,0:T(8,128)(2,1)S(1)} %multiply_convert_fusion), channel_id=1, source_target_pairs={{0,64},{64,128},{128,192},{1,65},{65,129},{129,193},{2,66},{66,130... | collective-permute-start | bytes 589832 | tf_op jit(solution)/shard_map/ppermute | solution.py:10
  120.4 4.0 %collective-permute-done.3 = bf16[2,2,64,384]{3,2,1,0:T(8,128)(2,1)S(1)} collective-permute-done((bf16[2,2,64,384]{3,2,1,0:T(8,128)(2,1)S(1)}, bf16[2,2,64,384]{3,2,1,0:T(8,128)(2,1)S(1)}, u32[]{:S(2)}, u32[]{:S(2)}) %collective-permute-start.3) | collective-permute-done | bytes 196640 | tf_op jit(solution)/shard_map/ppermute | solution.py:10
  124.5 3.9 %collective-permute-start.4 = (bf16[4,1,64,384]{3,2,1,0:T(8,128)(2,1)S(1)}, bf16[4,1,64,384]{3,2,1,0:T(8,128)(2,1)S(1)}, u32[]{:S(2)}, u32[]{:S(2)}) collective-permute-start(bf16[4,1,64,384]{3,2,1,0:T(8,128)(2,1)S(1)} %get-tuple-element.69), channel_id=1, source_target_pairs={{0,1},{1,2},{2,3},{3,4},{4,5},{5,6},{6,7},{7,8},{8,9},{9,10},{10,1... | collective-permute-start | bytes 589832 | tf_op jit(solution)/shard_map/ppermute | solution.py:20
  128.4 2.1 collective-permute-start.5
  130.5 56.9 %all-gather.5.cloned.1.call-done = bf16[3,3,3,384,384]{4,2,1,0,3:T(4,128)(2,1)} async-done(((bf16[3,3,3,6,384]{4,2,1,0,3:T(4,128)(2,1)}), bf16[3,3,3,384,384]{4,2,1,0,3:T(4,128)(2,1)}) %all-gather.5.cloned.1.call-update) | async-done | bytes 7962640 | tf_op jit(solution)/shard_map/all_gather | solution.py:56
  187.5 8.8 %copy.19 = bf16[3,3,3,384,384]{4,3,2,1,0:T(8,128)(2,1)} copy(bf16[3,3,3,384,384]{4,2,1,0,3:T(4,128)(2,1)} %all-gather.5.cloned.1.call-done) | data formatting | bytes 15925248 | tf_op jit(solution)/shard_map/all_gather | solution.py:56
  196.2 0.0 collective-permute-done.4
  196.2 0.0 collective-permute-done.5
  196.2 0.3 select_maximum_fusion
  197.9 0.6 pad_maximum_fusion.1
  198.5 0.0 slice-start
  198.6 3.4 %copy.17 = bf16[2,2,64,27,384]{4,3,2,1,0:T(8,128)(2,1)S(1)} copy(bf16[2,2,64,27,384]{4,2,1,3,0:T(8,128)(2,1)S(1)} %pad_maximum_fusion.1) | data formatting | bytes 10616832 | tf_op jit(solution)/shard_map/stack | solution.py:50
  201.9 0.0 slice-start.1
  201.9 0.0 copy-start.3
  201.9 2.6 %copy.21 = bf16[32,8,27,384]{3,1,2,0:T(8,128)(2,1)S(1)} copy(bf16[32,8,27,384]{3,2,1,0:T(8,128)(2,1)S(1)} %bitcast.355) | data formatting | bytes 10616832
  204.5 0.0 slice-done
  204.5 0.0 slice-done.1
  204.5 0.0 copy-done.3
  204.5 0.0 copy-start
  204.6 2.9 %convolution_add_fusion = f32[256,384]{1,0:T(8,128)S(1)} fusion(bf16[256,10368]{1,0:T(8,128)(2,1)S(1)} %bitcast.361, bf16[10368,384]{1,0:T(8,128)(2,1)S(1)} %bitcast.358, f32[384]{0:T(512)S(1)} %copy-done.3), kind=kOutput, calls=%fused_computation.5 | convolution fusion | flops 2038530048 | bytes 13665792 | tf_op jit(solution)/shard_map/dot_general | solution.py:59
  207.5 0.0 copy-done
  207.5 0.7 fusion.19
  (85 shorter events, 2.5 us)
Async XLA Ops:
  6.5 94.2 %all-gather.3.cloned.1.call-start = ((), (), s32[]{:S(2)}) async-start(), calls=%async_computation | async-start | bytes 10782720 | tf_op jit(solution)/shard_map/all_gather | solution.py:56
  8.2 179.3 %all-gather.5.cloned.1.call-start = ((), (), s32[]{:S(2)}) async-start(), calls=%async_computation.1 | async-start | bytes 10782720 | tf_op jit(solution)/shard_map/all_gather | solution.py:56
  12.1 7.5 %collective-permute-start = (bf16[2,2,64,384]{3,2,1,0:T(8,128)(2,1)S(1)}, bf16[2,2,64,384]{3,2,1,0:T(8,128)(2,1)S(1)}, u32[]{:S(2)}, u32[]{:S(2)}) collective-permute-start(bf16[2,2,64,384]{3,2,1,0:T(8,128)(2,1)S(1)} %fusion.18), channel_id=1, source_target_pairs={{0,64},{64,128},{128,192},{1,65},{65,129},{129,193},{2,66},{66,130... | collective-permute-start | bytes 589832 | tf_op jit(solution)/shard_map/ppermute | solution.py:10
  19.7 7.6 %collective-permute-start.1 = (bf16[4,1,64,384]{3,2,1,0:T(8,128)(2,1)S(1)}, bf16[4,1,64,384]{3,2,1,0:T(8,128)(2,1)S(1)}, u32[]{:S(2)}, u32[]{:S(2)}) collective-permute-start(bf16[4,1,64,384]{3,2,1,0:T(8,128)(2,1)S(1)} %get-tuple-element.71), channel_id=1, source_target_pairs={{0,1},{1,2},{2,3},{3,4},{4,5},{5,6},{6,7},{7,8},{8,9},{9,10},{10,1... | collective-permute-start | bytes 589832 | tf_op jit(solution)/shard_map/ppermute | solution.py:20
  24.7 7.6 %collective-permute-start.2 = (bf16[4,1,64,384]{3,2,1,0:T(8,128)(2,1)S(1)}, bf16[4,1,64,384]{3,2,1,0:T(8,128)(2,1)S(1)}, u32[]{:S(2)}, u32[]{:S(2)}) collective-permute-start(bf16[4,1,64,384]{3,2,1,0:T(8,128)(2,1)S(1)} %get-tuple-element.72), channel_id=1, source_target_pairs={{1,0},{2,1},{3,2},{4,3},{5,4},{6,5},{7,6},{8,7},{9,8},{10,9},{11,1... | collective-permute-start | bytes 589832 | tf_op jit(solution)/shard_map/ppermute | solution.py:21
  42.7 66.8 %copy-start.2 = (f32[384]{0:T(512)S(1)}, f32[384]{0:T(512)}, u32[]{:S(2)}) copy-start(f32[384]{0:T(512)} %param.10) | copy-start | bytes 4612
  109.5 7.6 %copy-start.1 = (f32[384]{0:T(512)S(1)}, f32[384]{0:T(512)}, u32[]{:S(2)}) copy-start(f32[384]{0:T(512)} %param.11) | copy-start | bytes 4612
  117.3 7.1 %collective-permute-start.3 = (bf16[2,2,64,384]{3,2,1,0:T(8,128)(2,1)S(1)}, bf16[2,2,64,384]{3,2,1,0:T(8,128)(2,1)S(1)}, u32[]{:S(2)}, u32[]{:S(2)}) collective-permute-start(bf16[2,2,64,384]{3,2,1,0:T(8,128)(2,1)S(1)} %multiply_convert_fusion), channel_id=1, source_target_pairs={{0,64},{64,128},{128,192},{1,65},{65,129},{129,193},{2,66},{66,130... | collective-permute-start | bytes 589832 | tf_op jit(solution)/shard_map/ppermute | solution.py:10
  124.5 71.8 %collective-permute-start.4 = (bf16[4,1,64,384]{3,2,1,0:T(8,128)(2,1)S(1)}, bf16[4,1,64,384]{3,2,1,0:T(8,128)(2,1)S(1)}, u32[]{:S(2)}, u32[]{:S(2)}) collective-permute-start(bf16[4,1,64,384]{3,2,1,0:T(8,128)(2,1)S(1)} %get-tuple-element.69), channel_id=1, source_target_pairs={{0,1},{1,2},{2,3},{3,4},{4,5},{5,6},{6,7},{7,8},{8,9},{9,10},{10,1... | collective-permute-start | bytes 589832 | tf_op jit(solution)/shard_map/ppermute | solution.py:20
  128.4 67.8 %collective-permute-start.5 = (bf16[4,1,64,384]{3,2,1,0:T(8,128)(2,1)S(1)}, bf16[4,1,64,384]{3,2,1,0:T(8,128)(2,1)S(1)}, u32[]{:S(2)}, u32[]{:S(2)}) collective-permute-start(bf16[4,1,64,384]{3,2,1,0:T(8,128)(2,1)S(1)} %get-tuple-element.70), channel_id=1, source_target_pairs={{1,0},{2,1},{3,2},{4,3},{5,4},{6,5},{7,6},{8,7},{9,8},{10,9},{11,1... | collective-permute-start | bytes 589832 | tf_op jit(solution)/shard_map/ppermute | solution.py:21
  198.5 6.0 %slice-start = ((s8[7962624]{0:T(1024)(128)(4,1)}), s8[3768320]{0:T(1024)(128)(4,1)S(1)}, s32[]{:S(2)}) async-start(s8[7962624]{0:T(1024)(128)(4,1)} %bitcast.356), calls=%async_computation.2 | async-start | bytes 7536640
  201.9 2.6 %slice-start.1 = ((s8[7962624]{0:T(1024)(128)(4,1)}), s8[4194304]{0:T(1024)(128)(4,1)S(1)}, s32[]{:S(2)}) async-start(s8[7962624]{0:T(1024)(128)(4,1)} %bitcast.356), calls=%async_computation.3 | async-start | bytes 8388608
  201.9 2.6 %copy-start.3 = (f32[384]{0:T(512)S(1)}, f32[384]{0:T(512)}, u32[]{:S(2)}) copy-start(f32[384]{0:T(512)} %param.13) | copy-start | bytes 4612
  204.5 3.0 %copy-start = (bf16[2,2,64,384]{3,2,1,0:T(8,128)(2,1)S(1)}, bf16[2,2,64,384]{3,2,1,0:T(8,128)(2,1)}, u32[]{:S(2)}) copy-start(bf16[2,2,64,384]{3,2,1,0:T(8,128)(2,1)} %param.7) | copy-start | bytes 589828
Sparse Core Ops, SparseCore 0:
  10.0 90.6 all-gather.2
  103.4 83.9 all-gather.4
where the time goes:
time: 215 us
  waiting for transfers between devices  128 us (60%)
  local copies, waits for them, and re-layouts  36.9 us (17%)
  starting transfers between devices  20 us (9%)
  between operations  14 us (7%)
  matrix products  10.4 us (5%)
  other arithmetic  5.4 us (3%)
    all_gather x2, waiting for transfers between devices, convolve(): piece = lax.all_gather(kernel, 'tile', axis=3, tiled=True)  115 us
    all_gather x2, local copies, waits for them, and re-layouts, convolve(): piece = lax.all_gather(kernel, 'tile', axis=3, tiled=True)  17.5 us
    unnamed x76, local copies, waits for them, and re-layouts  12.4 us
    dot_general x2, matrix products, convolve(): jnp.dot(flat, piece.reshape(27 * width_in, channels), preferred_element_t...  10.4 us
    ppermute x2, starting transfers between devices, extended(): before = lax.ppermute(last, axis, up)  8.92 us
    ppermute x2, waiting for transfers between devices, from_behind(): return lax.ppermute(value, axis, pairs)  7.57 us
    ppermute x2, starting transfers between devices, from_behind(): return lax.ppermute(value, axis, pairs)  7.04 us
    another operation x2, local copies, waits for them, and re-layouts, gather_taps(): stacked = jnp.stack(per_frame, axis=0)  6.71 us
  transfers between devices with their start and end apart: 8, of which 6 were waited for; matrix products, arithmetic and copies ran while one was open for 18% of the time, Pallas kernels for 0%

commit v1 on v0

v1 whole, which is shorter than its diff:
```python
import jax
import jax.numpy as jnp
import numpy as np
from jax import lax
from jax.experimental import pallas as pl
from jax.experimental.pallas import tpu as pltpu
from jax.sharding import PartitionSpec as P

MESH = pl.DeviceIdType.MESH
F32 = jnp.float32
BF16 = jnp.bfloat16

SLOTS = ((0, 1), (0, 0), (0, 2), (2, 0), (1, 1), (1, 0), (1, 2), (2, 2), (2, 1))


def one_hot_first():
    pick = np.zeros((144, 256), np.float32)
    for dy in range(3):
        for member in range(8):
            for channel in range(6):
                pick[dy * 48 + member * 6 + channel, member * 32 + dy * 6 + channel] = 1
    return pick


def one_hot_second():
    pick = np.zeros((48, 128), np.float32)
    for member in range(8):
        for channel in range(6):
            pick[member * 6 + channel, member * 16 + channel] = 1
    return pick


def silu(u):
    return u / (1.0 + jnp.exp(-u))


def kernel(
    lat, gain1, bias1, gain2, bias2, s1, s2, pick1, pick2, out,
    r1, r2, w1, w2, abuf, pbuf, hbuf, ssbuf, a2s, a2h, sendb, recvb,
    st1s, st1r, st2s, st2r, loc,
    ysend, yrecv, rsend, rrecv, bsend, brecv,
    xs, xr, ups, upr, dns, dnr, sss, ssr, h2s, h2r, fs, fr,
):
    x = lax.axis_index("span")
    t = lax.axis_index("tile")
    c = lax.rem(t, 2)
    z = lax.rem(lax.div(t, 2), 8)
    y = lax.div(t, 16)
    zi = lax.rem(z, 4)
    h = lax.div(z, 4)
    j = lax.rem(t, 8)
    g = lax.div(t, 8)

    def dev(yy, zz, cc):
        return (x, yy * 16 + zz * 2 + cc)

    def rc(src, dst, ssem, rsem, device):
        return pltpu.make_async_remote_copy(
            src_ref=src, dst_ref=dst, send_sem=ssem, recv_sem=rsem,
            device_id=device, device_id_type=MESH,
        )

    barrier = pltpu.get_barrier_semaphore()

    def hail(device):
        pl.semaphore_signal(barrier, inc=1, device_id=device, device_id_type=MESH)

    for d in range(1, 8):
        hail((x, g * 8 + lax.rem(j + d, 8)))

    @pl.when(x != y)
    def _():
        for d in range(8):
            hail((y, x * 16 + h * 8 + lax.rem(j + d, 8)))

    for d in range(1, 4):
        hail((lax.rem(x + d, 4), t))
    for d in range(1, 4):
        hail(dev(lax.rem(y + d, 4), z, c))
    zr = lax.rem(z + 1, 8)
    zl = lax.rem(z + 7, 8)
    hail(dev(y, zr, c))
    hail(dev(y, zl, c))

    @pl.when(t > 0)
    def _():
        hail((x, t - 1))

    @pl.when(t < 63)
    def _():
        hail((x, t + 1))

    w2[:, :, :, 96:128, :] = jnp.zeros((4, 4, 2, 32, 384), BF16)
    a2s[:, 0:2] = jnp.zeros((3, 2, 4, 64, 128), BF16)

    def zero_p(i, carry):
        pbuf[i, 0:2] = jnp.zeros((2, 2, 64, 256), F32)
        return carry

    lax.fori_loop(0, 4, zero_p, 0)

    def act1(i, carry):
        v = lat[i].reshape(128, 384).astype(F32)
        ms = jnp.mean(v * v, axis=-1, keepdims=True)
        u = v * lax.rsqrt(ms + 1e-6) * gain1[...]
        abuf[x, i, 1:3] = silu(u).astype(BF16).reshape(2, 64, 384)
        return carry

    lax.fori_loop(0, 2, act1, 0)

    many = jnp.where(x != y, 8, 0) + jnp.where(t > 0, 1, 0) + jnp.where(t < 63, 1, 0) + 15
    pl.semaphore_wait(barrier, many)

    def st1(d):
        jj = lax.rem(j + d, 8)
        return rc(s1.at[jj], r1.at[j], st1s.at[d], st1r.at[d], (x, g * 8 + jj))

    def st2(d):
        jj = lax.rem(j + d, 8)
        return rc(s2.at[jj], r2.at[j], st2s.at[d], st2r.at[d], (y, x * 16 + h * 8 + jj))

    def own2():
        return pltpu.make_async_copy(s2.at[j], r2.at[j], loc.at[1])

    for d in range(1, 8):
        st1(d).start()
    own1 = pltpu.make_async_copy(s1.at[j], r1.at[j], loc.at[0])
    own1.start()

    def xsend(d):
        return rc(
            abuf.at[x, :, 1:3], abuf.at[x, :, 1:3], xs.at[d], xr.at[d], (lax.rem(x + d, 4), t)
        )

    def up(src, d):
        return rc(abuf.at[src, :, 1], abuf.at[src, :, 3], ups.at[d], upr.at[d], (x, t - 1))

    def down(src, d):
        return rc(abuf.at[src, :, 2], abuf.at[src, :, 0], dns.at[d], dnr.at[d], (x, t + 1))

    def halo_send(d):
        src = lax.rem(x + 4 - d, 4)

        @pl.when(t > 0)
        def _():
            up(src, d).start()

        @pl.when(t < 63)
        def _():
            down(src, d).start()

    def xstep(d):
        src = lax.rem(x + 4 - d, 4)
        land = abuf.at[src, :, 1:3]
        rc(land, land, xs.at[d], xr.at[d], (x, t)).wait_recv()
        halo_send(d)

    def halo_wait():
        for d in range(4):
            src = lax.rem(x + 4 - d, 4)

            @pl.when(t > 0)
            def _():
                land = abuf.at[src, :, 0]
                rc(land, land, dns.at[d], dnr.at[d], (x, t)).wait_recv()

            @pl.when(t < 63)
            def _():
                land = abuf.at[src, :, 3]
                rc(land, land, ups.at[d], upr.at[d], (x, t)).wait_recv()

        @pl.when(t == 0)
        def _():
            abuf[:, :, 0] = jnp.zeros((4, 2, 64, 384), BF16)

        @pl.when(t == 63)
        def _():
            abuf[:, :, 3] = jnp.zeros((4, 2, 64, 384), BF16)

    for d in range(1, 4):
        xsend(d).start()
    for d in range(8):
        if d == 0:

            @pl.when(x != y)
            def _():
                st2(0).start()

            @pl.when(x == y)
            def _():
                own2().start()
        else:
            st2(d).start()
    halo_send(0)

    def own_slice(k):
        if k == 0:
            return w1.at[c, zi, :, y, h]
        return w2.at[y, zi, c, pl.ds(pl.multiple_of(48 * h, 16), 48), :]

    def blk(k, yy, zz, cc):
        if k == 0:
            return w1.at[cc, lax.rem(zz, 4), :, yy, lax.div(zz, 4)]
        return w2.at[yy, lax.rem(zz, 4), cc, pl.ds(pl.multiple_of(48 * lax.div(zz, 4), 16), 48), :]

    def half(k, zz, hf):
        if k == 0:
            return w1.at[0, lax.rem(zz, 4), :, 2 * hf:2 * hf + 2, lax.div(zz, 4)]
        return w2.at[2 * hf:2 * hf + 2, lax.rem(zz, 4), 0, pl.ds(pl.multiple_of(48 * lax.div(zz, 4), 16), 48), :]

    def zset(k, zz):
        if k == 0:
            return w1.at[0, lax.rem(zz, 4), :, :, lax.div(zz, 4)]
        return w2.at[:, lax.rem(zz, 4), 0, pl.ds(pl.multiple_of(48 * lax.div(zz, 4), 16), 48), :]

    def yset(k, yy):
        if k == 0:
            return w1.at[1, :, :, yy]
        return w2.at[yy, :, 1, 0:96, :]

    def yhalf(k, yy, a):
        if k == 0:
            return w1.at[1, 2 * a:2 * a + 2, :, yy]
        return w2.at[yy, 2 * a:2 * a + 2, 1, 0:96, :]

    sent_a, sent_b = [], []

    def go(group, make):
        make().start()
        group.append(make)

    def got(ref, rsem):
        rc(ref, ref, loc.at[2], rsem, (x, t)).wait_recv()

    def zz(s):
        return lax.rem(z + 8 + s, 8)

    ring_dev = (dev(y, zr, c), dev(y, zl, c))

    def a_ring(k, way, s, hf, origin):
        def make():
            ref = half(k, zz(origin), hf)
            return rc(ref, ref, rsend.at[k, way, s, hf], rrecv.at[k, way, s + 1, hf], ring_dev[way])

        go(sent_a, make)

    def a_sib(k, idx, origin):
        def make():
            ref = zset(k, zz(origin))
            return rc(ref, ref, bsend.at[k, idx], brecv.at[k, idx], dev(y, z, 1))

        go(sent_a, make)

    def b_ring(k, way, s, origin):
        def make():
            ref = blk(k, y, zz(origin), 1)
            return rc(ref, ref, rsend.at[k, way, s, 0], rrecv.at[k, way, s + 1, 0], ring_dev[way])

        go(sent_b, make)

    def b_sib(k, d):
        def make():
            ref = yset(k, lax.rem(y + d, 4))
            return rc(ref, ref, bsend.at[k, d], brecv.at[k, d], dev(y, z, 0))

        go(sent_b, make)

    def a_y(k, d):
        def make():
            ref = blk(k, y, z, 0)
            return rc(ref, ref, ysend.at[k, d], yrecv.at[k, d], dev(lax.rem(y + d, 4), z, 0))

        go(sent_a, make)

    def b_y(k, idx, origin, a, to):
        def make():
            ref = yhalf(k, lax.rem(y + origin, 4), a)
            return rc(ref, ref, ysend.at[k, idx], yrecv.at[k, idx], dev(lax.rem(y + to, 4), z, 1))

        go(sent_b, make)

    def step(k, n):
        @pl.when(c == 0)
        def _():
            if n == 0:
                for d in range(1, 4):
                    a_y(k, d)
            if n == 1:
                for d in range(1, 4):
                    got(blk(k, lax.rem(y + 4 - d, 4), z, 0), yrecv.at[k, d])
                for hf in range(2):
                    for way in range(2):
                        a_ring(k, way, 0, hf, 0)
                a_sib(k, 0, 0)
            if n in (2, 3, 4):
                s = n - 1
                for hf in range(2):
                    for way, origin in ((0, -s), (1, s)):
                        got(half(k, zz(origin), hf), rrecv.at[k, way, s, hf])
                        if s < 3 or hf == way:
                            a_ring(k, way, s, hf, origin)
                a_sib(k, 2 * s - 1, -s)
                a_sib(k, 2 * s, s)
            if n == 5:
                for way in range(2):
                    got(half(k, zz(4), way), rrecv.at[k, way, 4, way])
                a_sib(k, 7, 4)
            if n == 7:
                for d in range(4):
                    got(yset(k, lax.rem(y + d, 4)), brecv.at[k, d])

        @pl.when(c == 1)
        def _():
            if n == 0:
                for way in range(2):
                    b_ring(k, way, 0, 0)
            if n in (1, 2, 3):
                s = n
                for way, origin in ((0, -s), (1, s)):
                    got(blk(k, y, zz(origin), 1), rrecv.at[k, way, s, 0])
                    if s < 3 or way == 0:
                        b_ring(k, way, s, origin)
            if n == 4:
                got(blk(k, y, zz(4), 1), rrecv.at[k, 0, 4, 0])
                for a in range(2):
                    b_y(k, a, 0, a, 1)
                    b_y(k, 3 - a, 0, 1 - a, 3)
                b_sib(k, 0)
            if n == 5:
                below, above = lax.rem(y + 3, 4), lax.rem(y + 1, 4)
                got(yhalf(k, below, 0), yrecv.at[k, 0])
                b_y(k, 4, 3, 0, 1)
                got(yhalf(k, above, 1), yrecv.at[k, 3])
                b_y(k, 5, 1, 1, 3)
                got(yhalf(k, below, 1), yrecv.at[k, 1])
                got(yhalf(k, above, 0), yrecv.at[k, 2])
                b_sib(k, 3)
                b_sib(k, 1)
            if n == 6:
                got(yhalf(k, lax.rem(y + 2, 4), 0), yrecv.at[k, 4])
                got(yhalf(k, lax.rem(y + 2, 4), 1), yrecv.at[k, 5])
                b_sib(k, 2)
            if n == 7:
                for idx, s in enumerate((0, -1, 1, -2, 2, -3, 3, 4)):
                    got(zset(k, zz(s)), brecv.at[k, idx])

    own1.wait()
    for d in range(1, 8):
        got(r1.at[lax.rem(j + 8 - d, 8)], st1r.at[d])
    chunk = jnp.dot(pick1[...], r1[...].reshape(256, 128), preferred_element_type=F32).astype(BF16)
    for dy in range(3):
        w1[c, zi, dy, y, h] = chunk[dy * 48:dy * 48 + 48]
    step(0, 0)

    @pl.when(x != y)
    def _():
        got(r2.at[j], st2r.at[0])

    @pl.when(x == y)
    def _():
        own2().wait()

    for d in range(1, 8):
        got(r2.at[lax.rem(j + 8 - d, 8)], st2r.at[d])
    chunk2 = jnp.dot(pick2[...], r2[...].reshape(128, 384), preferred_element_type=F32).astype(BF16)
    w2[y, zi, c, pl.ds(pl.multiple_of(48 * h, 16), 48), :] = chunk2
    step(0, 1)
    step(1, 0)
    xstep(1)
    step(0, 2)
    xstep(3)
    step(0, 3)
    xstep(2)
    step(0, 4)
    step(0, 5)
    step(1, 1)
    step(0, 6)
    step(0, 7)
    halo_wait()

    def conv1(fp):
        rows = []
        for yy in range(2):
            rows.append(jnp.concatenate(
                [abuf[fp, :, yy + dy].reshape(128, 384) for dy in range(3)], axis=1))
        lhs = jnp.concatenate(rows, axis=0)

        def tile(n, carry):
            rhs = jnp.concatenate(
                [w1[0, n].reshape(1152, 128), w1[1, n].reshape(1152, 128)], axis=1)
            res = jnp.dot(lhs, rhs, preferred_element_type=F32)
            for yy in range(2):
                pbuf[n, 2 + 2 * fp:4 + 2 * fp, yy] = res[yy * 128:yy * 128 + 128].reshape(2, 64, 256)
            return carry

        lax.fori_loop(0, 4, tile, 0)

    for fp in range(4):
        conv1(fp)
        step(1, 2 + fp)

    lane = lax.broadcasted_iota(jnp.int32, (64, 128), 1)
    row = lax.broadcasted_iota(jnp.int32, (64, 128), 0)

    def shift_down(v):
        return jnp.where(row > 0, pltpu.roll(v, 1, 0), 0.0)

    def shift_up(v):
        return jnp.where(row < 63, pltpu.roll(v, 63, 0), 0.0)

    def combine(f, carry):
        for yy in range(2):
            def p(dt, n):
                return pbuf[n // 2, f + dt, yy, :, (n % 2) * 128:(n % 2) * 128 + 128]

            m1 = p(0, 0) + p(1, 3) + p(2, 6)
            a_lo = p(0, 0) + p(1, 3)
            mid = p(0, 1) + p(1, 4)
            b_hi = p(0, 2) + p(1, 5)
            m0 = pltpu.roll(jnp.where(lane >= 96, a_lo, mid), 32, 1) + pltpu.roll(p(2, 2), 96, 1)
            m2 = pltpu.roll(jnp.where(lane >= 64, mid, b_hi), 64, 1) + pltpu.roll(p(2, 5), 96, 1)
            hid = m1 + shift_down(m0) + shift_up(m2) + bias1[...]
            hbuf[f, yy] = jnp.where(lane < 96, hid, 0.0)
        return carry

    lax.fori_loop(0, 8, combine, 0)

    hv = hbuf[...].reshape(1024, 128)
    ssbuf[0] = lax.dot_general(
        jnp.ones((8, 128), F32), hv * hv, (((1,), (1,)), ((), ())),
        precision=lax.Precision.HIGHEST, preferred_element_type=F32,
    )

    def ss_send(d):
        return rc(ssbuf.at[0], ssbuf.at[d], sss.at[d], ssr.at[d], (lax.rem(x + d, 4), t))

    for d in range(1, 4):
        ss_send(d).start()
    step(1, 6)
    for d in range(1, 4):
        got(ssbuf.at[d], ssr.at[d])
    total = ssbuf[0] + ssbuf[1] + ssbuf[2] + ssbuf[3]
    ms = lax.dot_general(
        total, jnp.full((8, 128), 0.125, F32), (((0,), (0,)), ((), ())),
        precision=lax.Precision.HIGHEST, preferred_element_type=F32,
    ) * (1.0 / 384.0)
    hv = hbuf[...].reshape(1024, 128)
    hbuf[...] = (hv * lax.rsqrt(ms + 1e-6) * gain2[...]).reshape(8, 2, 64, 128)

    def spread(f, where, v):
        a2s[0, f + 2, where] = shift_down(v).astype(BF16)
        a2s[1, f + 2, where] = v.astype(BF16)
        a2s[2, f + 2, where] = shift_up(v).astype(BF16)

    def act2(f, carry):
        for yy in range(2):
            spread(f, 1 + yy, silu(hbuf[f, yy]))
        return carry

    lax.fori_loop(0, 8, act2, 0)

    def h2up():
        return rc(a2s.at[1, 2:10, 1], a2h.at[1], h2s.at[0], h2r.at[0], (x, t - 1))

    def h2down():
        return rc(a2s.at[1, 2:10, 2], a2h.at[0], h2s.at[1], h2r.at[1], (x, t + 1))

    @pl.when(t > 0)
    def _():
        h2up().start()

    @pl.when(t < 63)
    def _():
        h2down().start()

    step(1, 7)

    @pl.when(t > 0)
    def _():
        got(a2h.at[0], h2r.at[1])

    @pl.when(t == 0)
    def _():
        a2h[0] = jnp.zeros((8, 64, 128), BF16)

    @pl.when(t < 63)
    def _():
        got(a2h.at[1], h2r.at[0])

    @pl.when(t == 63)
    def _():
        a2h[1] = jnp.zeros((8, 64, 128), BF16)

    def halo2(f, carry):
        spread(f, 0, a2h[0, f].astype(F32))
        spread(f, 3, a2h[1, f].astype(F32))
        return carry

    lax.fori_loop(0, 8, halo2, 0)

    def conv2(q):
        acc = None
        for dt in range(3):
            lhs, rhs = [], []
            for dy in range(3):
                for dx in range(3):
                    tap = dt * 9 + dy * 3 + dx
                    lhs.append(a2s[dx, pl.ds(2 * q + dt, 2), dy:dy + 2].reshape(256, 128))
                    rhs.append(w2[tap // 8, (tap % 8) // 2, tap % 2])
            part = jnp.dot(
                jnp.concatenate(lhs, axis=1), jnp.concatenate(rhs, axis=0),
                preferred_element_type=F32,
            )
            acc = part if acc is None else acc + part
        return acc

    def out_send(d):
        return rc(sendb.at[d - 1], recvb.at[d - 1], fs.at[d], fr.at[d], (lax.rem(x + d, 4), t))

    for d in (2, 1, 3):
        sendb[d - 1] = conv2(lax.rem(x + d, 4)).astype(BF16).reshape(2, 2, 64, 384)
        out_send(d).start()
    mine = conv2(x) + bias2[...] + lat[...].reshape(256, 384).astype(F32)
    for d in (2, 1, 3):
        got(recvb.at[d - 1], fr.at[d])
        mine = mine + recvb[d - 1].reshape(256, 384).astype(F32)
    out[...] = mine.astype(BF16).reshape(2, 2, 64, 384)

    for d in range(1, 8):
        st1(d).wait_send()
        st2(d).wait_send()

    @pl.when(x != y)
    def _():
        st2(0).wait_send()

    for d in range(1, 4):
        xsend(d).wait_send()
        ss_send(d).wait_send()
        out_send(d).wait_send()

    @pl.when(t > 0)
    def _():
        for d in range(4):
            up(lax.rem(x + 4 - d, 4), d).wait_send()
        h2up().wait_send()

    @pl.when(t < 63)
    def _():
        for d in range(4):
            down(lax.rem(x + 4 - d, 4), d).wait_send()
        h2down().wait_send()

    @pl.when(c == 0)
    def _():
        for make in sent_a:
            make().wait_send()

    @pl.when(c == 1)
    def _():
        for make in sent_b:
            make().wait_send()


def per_device(latents, gain_first, conv_first, bias_first, gain_second, conv_second, bias_second):
    x = lax.axis_index("span")
    w = lax.dynamic_slice_in_dim(conv_first, 96 * x, 96, axis=4)
    w = jnp.stack([w[dt, :, dx] for dt, dx in SLOTS], axis=2)
    w = w.reshape(18, 864)
    w = jnp.pad(w, ((0, 14), (0, 160))).reshape(32, 8, 128)
    s1 = jnp.transpose(w, (1, 0, 2))
    v = jnp.pad(conv_second.reshape(27, 6, 384), ((0, 5), (0, 10), (0, 0)))
    s2 = lax.dynamic_slice_in_dim(v, 8 * x, 8, axis=0)

    def part(vec):
        return jnp.pad(lax.dynamic_slice_in_dim(vec, 96 * x, 96), (0, 32)).reshape(1, 128)

    vm = pl.BlockSpec(memory_space=pltpu.VMEM)
    dma = pltpu.SemaphoreType.DMA
    return pl.pallas_call(
        kernel,
        out_shape=jax.ShapeDtypeStruct((2, 2, 64, 384), BF16),
        in_specs=[vm] * 9,
        out_specs=vm,
        scratch_shapes=[
            pltpu.VMEM((8, 32, 128), BF16),
            pltpu.VMEM((8, 16, 384), BF16),
            pltpu.VMEM((2, 4, 3, 4, 2, 48, 128), BF16),
            pltpu.VMEM((4, 4, 2, 128, 384), BF16),
            pltpu.VMEM((4, 2, 4, 64, 384), BF16),
            pltpu.VMEM((4, 10, 2, 64, 256), F32),
            pltpu.VMEM((8, 2, 64, 128), F32),
            pltpu.VMEM((4, 8, 1024), F32),
            pltpu.VMEM((3, 10, 4, 64, 128), BF16),
            pltpu.VMEM((2, 8, 64, 128), BF16),
            pltpu.VMEM((3, 2, 2, 64, 384), BF16),
            pltpu.VMEM((3, 2, 2, 64, 384), BF16),
            dma((8,)), dma((8,)), dma((8,)), dma((8,)), dma((3,)),
            dma((2, 6)), dma((2, 6)), dma((2, 2, 4, 2)), dma((2, 2, 5, 2)), dma((2, 8)), dma((2, 8)),
            dma((4,)), dma((4,)), dma((4,)), dma((4,)), dma((4,)), dma((4,)),
            dma((4,)), dma((4,)), dma((2,)), dma((2,)), dma((4,)), dma((4,)),
        ],
        compiler_params=pltpu.CompilerParams(
            collective_id=0, has_side_effects=True, vmem_limit_bytes=48 * 1024 * 1024
        ),
        cost_estimate=pl.CostEstimate(flops=4_000_000_000, bytes_accessed=8_000_000, transcendentals=400_000),
    )(
        latents, gain_first.reshape(1, 384), part(bias_first), part(gain_second),
        bias_second.reshape(1, 384), s1, s2,
        jnp.asarray(one_hot_first(), BF16), jnp.asarray(one_hot_second(), BF16),
    )


def solution(mesh):
    in_specs = (
        P("span", "tile", None, None),
        P(),
        P(None, None, None, "tile", None),
        P(),
        P(),
        P(None, None, None, "tile", None),
        P(),
    )
    out_specs = P("span", "tile", None, None)
    return jax.shard_map(
        per_device, mesh=mesh, in_specs=in_specs, out_specs=out_specs, check_vma=False
    )
```

time: 215 us -> 94.4 us (0.44)
  waiting for transfers between devices: 128 us -> 0 us
  Pallas kernels: 0 us -> 81 us
  local copies, waits for them, and re-layouts: 36.9 us -> 12.4 us
  starting transfers between devices: 20 us -> 0 us
  between operations: 14 us -> 0.05 us
  matrix products: 10.4 us -> 0 us
  other arithmetic: 5.4 us -> 0 us
    all_gather x2 -> x0, waiting for transfers between devices: 115 us -> none  [convolve(): piece = lax.all_gather(kernel, 'tile', axis=3, tiled=True)]
    pallas_call x0 -> x1, Pallas kernels: none -> 81 us  [per_device(): pl.pallas_call(kernel, out_shape=jax.ShapeDtypeStruct((2, 2, 64, 384), BF...]
    ppermute x6 -> x0, starting transfers between devices: 20 us -> none  [the longest x2 8.92 us: extended(): before = lax.ppermute(last, axis, up)]
    all_gather x2 -> x0, local copies, waits for them, and re-layouts: 17.5 us -> none  [convolve(): piece = lax.all_gather(kernel, 'tile', axis=3, tiled=True)]
    ppermute x6 -> x0, waiting for transfers between devices: 13.3 us -> none  [the longest x2 7.57 us: from_behind(): return lax.ppermute(value, axis, pairs)]
    dot_general x2 -> x0, matrix products: 10.4 us -> none  [convolve(): jnp.dot(flat, piece.reshape(27 * width_in, channels), preferred_element_t...]
    another operation x6 -> x2, local copies, waits for them, and re-layouts: 6.87 us -> 0.8 us  [per_device(): w = jnp.stack([w[dt, :, dx] for dt, dx in SLOTS], axis=2)]
    unnamed x76 -> x21, local copies, waits for them, and re-layouts: 12.4 us -> 9.96 us
  transfers between devices with their start and end apart: 8 -> 0, of which waited for: 6 -> 0; matrix products, arithmetic and copies ran while one was open for 18% -> 0% of each run, Pallas kernels for 0% -> 0%
where the time goes in v1:
time: 94.4 us; the launch traced here: 93.5 us
  Pallas kernels  81 us (86%)
  local copies, waits for them, and re-layouts  12.4 us (13%)
    pallas_call x1, Pallas kernels, per_device(): pl.pallas_call(kernel, out_shape=jax.ShapeDtypeStruct((2, 2, 64, 384), BF...  81 us
    unnamed x21, local copies, waits for them, and re-layouts  9.96 us

profile of v1, /device:TPU:1, one launch (start us, length us, event | category | flops | bytes accessed | tf_op | source)
XLA Modules:
  0.0 93.5 jit_solution(11319438787853298874)
XLA Ops:
  0.0 0.8 dynamic_slice.12
  0.8 0.8 dynamic_slice.13
  1.5 0.0 copy-start.4
  1.5 0.7 copy-done.4
  2.2 0.0 copy-start.5
  2.2 0.7 copy-done.5
  2.9 0.8 constant_dynamic-update-slice_fusion.8
  3.7 0.8 constant_dynamic-update-slice_fusion.7
  4.5 0.8 constant_dynamic-update-slice_fusion.6
  5.2 0.8 constant_dynamic-update-slice_fusion.5
  6.0 0.8 constant_dynamic-update-slice_fusion.4
  6.8 0.8 constant_dynamic-update-slice_fusion.3
  7.6 0.8 constant_dynamic-update-slice_fusion.2
  8.4 0.8 constant_dynamic-update-slice_fusion.1
  9.2 0.8 constant_dynamic-update-slice_fusion
  10.0 0.0 copy-start.3
  10.0 0.1 reshape.25
  10.1 0.0 copy-start
  10.1 0.7 copy-done.3
  10.9 0.0 copy-start.1
  10.9 0.0 copy-start.2
  10.9 0.1 copy-done
  11.1 0.7 copy-done.1
  11.8 0.0 copy-done.2
  11.8 81.0 %shard_map.91 = bf16[2,2,64,384]{3,2,1,0:T(8,128)(2,1)S(1)} custom-call(bf16[2,2,64,384]{3,2,1,0:T(8,128)(2,1)S(1)} %copy-done, f32[1,384]{1,0:T(1,128)S(1)} %reshape.21.gain1, f32[1,128]{1,0:T(1,128)S(1)} %get-tuple-element.6.bias1, f32[1,128]{1,0:T(1,128)S(1)} %get-tuple-element.5.gain2, f32[1,384]{1,0:T(1,128)S(1)} %reshape.24.bias2, ...), custom_call_target="tpu_custom_call" | custom-call | flops 4000000000 | bytes 8000000 | tf_op jit(solution)/shard_map/pallas_call | solution.py:580
  92.8 0.7 copy.47
  (6 shorter events, 0.1 us)
Async XLA Ops:
  1.5 0.7 copy-start.4
  2.2 0.7 copy-start.5
  10.0 0.9 copy-start.3
  10.1 0.9 %copy-start = (bf16[2,2,64,384]{3,2,1,0:T(8,128)(2,1)S(1)}, bf16[2,2,64,384]{3,2,1,0:T(8,128)(2,1)}, u32[]{:S(2)}) copy-start(bf16[2,2,64,384]{3,2,1,0:T(8,128)(2,1)} %lat.1) | copy-start | bytes 589828
  10.9 0.9 copy-start.1
  10.9 0.9 copy-start.2

commit v2 on v1

--- a/solution.py
+++ b/solution.py
@@ -1,6 +1,5 @@
 import jax
 import jax.numpy as jnp
-import numpy as np
 from jax import lax
 from jax.experimental import pallas as pl
 from jax.experimental.pallas import tpu as pltpu
@@ -13,31 +12,15 @@
 SLOTS = ((0, 1), (0, 0), (0, 2), (2, 0), (1, 1), (1, 0), (1, 2), (2, 2), (2, 1))
 
 
-def one_hot_first():
-    pick = np.zeros((144, 256), np.float32)
-    for dy in range(3):
-        for member in range(8):
-            for channel in range(6):
-                pick[dy * 48 + member * 6 + channel, member * 32 + dy * 6 + channel] = 1
-    return pick
-
-
-def one_hot_second():
-    pick = np.zeros((48, 128), np.float32)
-    for member in range(8):
-        for channel in range(6):
-            pick[member * 6 + channel, member * 16 + channel] = 1
-    return pick
-
-
 def silu(u):
     return u / (1.0 + jnp.exp(-u))
 
 
 def kernel(
-    lat, gain1, bias1, gain2, bias2, s1, s2, pick1, pick2, out,
+    lat_hbm, gain1_hbm, bias1_hbm, gain2_hbm, bias2_hbm, k1_hbm, k2_hbm, out,
+    lat, vec, k1, k2, s1, s2, stack,
     r1, r2, w1, w2, abuf, pbuf, hbuf, ssbuf, a2s, a2h, sendb, recvb,
-    st1s, st1r, st2s, st2r, loc,
+    ins, st1s, st1r, st2s, st2r, loc,
     ysend, yrecv, rsend, rrecv, bsend, brecv,
     xs, xr, ups, upr, dns, dnr, sss, ssr, h2s, h2r, fs, fr,
 ):
@@ -60,6 +43,18 @@
             device_id=device, device_id_type=MESH,
         )
 
+    loads = [
+        pltpu.make_async_copy(k1_hbm, k1, ins.at[0]),
+        pltpu.make_async_copy(lat_hbm, lat, ins.at[1]),
+        pltpu.make_async_copy(k2_hbm, k2, ins.at[2]),
+        pltpu.make_async_copy(gain1_hbm, vec.at[0], ins.at[3]),
+        pltpu.make_async_copy(bias1_hbm, vec.at[1], ins.at[4]),
+        pltpu.make_async_copy(gain2_hbm, vec.at[2], ins.at[5]),
+        pltpu.make_async_copy(bias2_hbm, vec.at[3], ins.at[6]),
+    ]
+    for load in loads:
+        load.start()
+
     barrier = pltpu.get_barrier_semaphore()
 
     def hail(device):
@@ -77,10 +72,8 @@
         hail((lax.rem(x + d, 4), t))
     for d in range(1, 4):
         hail(dev(lax.rem(y + d, 4), z, c))
-    zr = lax.rem(z + 1, 8)
-    zl = lax.rem(z + 7, 8)
-    hail(dev(y, zr, c))
-    hail(dev(y, zl, c))
+    for d in (1, 2, 6, 7):
+        hail(dev(y, lax.rem(z + d, 8), c))
 
     @pl.when(t > 0)
     def _():
@@ -89,6 +82,49 @@
     @pl.when(t < 63)
     def _():
         hail((x, t + 1))
+
+    lane8 = lax.broadcasted_iota(jnp.int32, (8, 128), 1)
+    turn = lax.rem(384 - 96 * x, 384)
+
+    def mine96(v):
+        return pltpu.roll(v, turn, 1)[:, 0:128]
+
+    loads[0].wait()
+    pad2 = jnp.zeros((2, 384), F32)
+    tiles = []
+    for dy in range(3):
+        got_slots = []
+        for dt, dx in SLOTS:
+            got_slots.append(mine96(jnp.concatenate([k1[dt * 9 + dy * 3 + dx].astype(F32), pad2], axis=0)))
+
+        def at(n, by):
+            return pltpu.roll(got_slots[n], by, 1) if by else got_slots[n]
+
+        row = [
+            jnp.where(lane8 < 96, at(0, 0), at(1, 96)),
+            jnp.where(lane8 < 64, at(1, 96), at(2, 64)),
+            jnp.where(lane8 < 32, at(2, 64), at(3, 32)),
+            jnp.where(lane8 < 96, at(4, 0), at(5, 96)),
+            jnp.where(lane8 < 64, at(5, 96), at(6, 64)),
+            jnp.where(lane8 < 32, at(6, 64), at(7, 32)),
+            jnp.where(lane8 < 96, at(8, 0), 0.0),
+            jnp.zeros((8, 128), F32),
+        ]
+        tiles.append(row)
+    for n in range(8):
+        s1[n, 0:16] = jnp.concatenate([tiles[0][n], tiles[1][n]], axis=0).astype(BF16)
+        s1[n, 16:32] = jnp.concatenate([tiles[2][n], jnp.zeros((8, 128), F32)], axis=0).astype(BF16)
+    loads[2].wait()
+    for n in range(8):
+        tap = jnp.minimum(8 * x + n, 26)
+        s2[n] = jnp.concatenate([k2[tap].astype(F32), jnp.zeros((10, 384), F32)], axis=0).astype(BF16)
+    for load in loads[3:]:
+        load.wait()
+    loads[1].wait()
+    gain1 = vec[0:1]
+    bias2 = vec[3:4]
+    bias1 = jnp.where(lane8[0:1] < 96, mine96(jnp.broadcast_to(vec[1:2], (8, 384)))[0:1], 0.0)
+    gain2 = jnp.where(lane8[0:1] < 96, mine96(jnp.broadcast_to(vec[2:3], (8, 384)))[0:1], 0.0)
 
     w2[:, :, :, 96:128, :] = jnp.zeros((4, 4, 2, 32, 384), BF16)
     a2s[:, 0:2] = jnp.zeros((3, 2, 4, 64, 128), BF16)
@@ -102,13 +138,13 @@
     def act1(i, carry):
         v = lat[i].reshape(128, 384).astype(F32)
         ms = jnp.mean(v * v, axis=-1, keepdims=True)
-        u = v * lax.rsqrt(ms + 1e-6) * gain1[...]
+        u = v * lax.rsqrt(ms + 1e-6) * gain1
         abuf[x, i, 1:3] = silu(u).astype(BF16).reshape(2, 64, 384)
         return carry
 
     lax.fori_loop(0, 2, act1, 0)
 
-    many = jnp.where(x != y, 8, 0) + jnp.where(t > 0, 1, 0) + jnp.where(t < 63, 1, 0) + 15
+    many = jnp.where(x != y, 8, 0) + jnp.where(t > 0, 1, 0) + jnp.where(t < 63, 1, 0) + 17
     pl.semaphore_wait(barrier, many)
 
     def st1(d):
@@ -235,47 +271,51 @@
     def zz(s):
         return lax.rem(z + 8 + s, 8)
 
-    ring_dev = (dev(y, zr, c), dev(y, zl, c))
-
-    def a_ring(k, way, s, hf, origin):
+    def a_y(k, d):
         def make():
-            ref = half(k, zz(origin), hf)
-            return rc(ref, ref, rsend.at[k, way, s, hf], rrecv.at[k, way, s + 1, hf], ring_dev[way])
+            ref = blk(k, y, z, 0)
+            return rc(ref, ref, ysend.at[k, d - 1], yrecv.at[k, d - 1], dev(lax.rem(y + d, 4), z, 0))
 
         go(sent_a, make)
 
-    def a_sib(k, idx, origin):
+    WAY = {1: 0, -1: 1, 2: 2, -2: 3, 3: 4, -3: 5, 4: 6, -4: 7, 0: 8}
+
+    def a_z(k, origin, total, hf=None):
         def make():
-            ref = zset(k, zz(origin))
-            return rc(ref, ref, bsend.at[k, idx], brecv.at[k, idx], dev(y, z, 1))
+            ref = zset(k, zz(origin)) if hf is None else half(k, zz(origin), hf)
+            i = WAY[total]
+            return rc(ref, ref, rsend.at[k, i], rrecv.at[k, i], dev(y, zz(origin + total), c))
 
         go(sent_a, make)
 
-    def b_ring(k, way, s, origin):
+    def a_sib(k, s):
+        def make():
+            ref = zset(k, zz(s))
+            return rc(ref, ref, bsend.at[k, WAY[s] % 9], brecv.at[k, WAY[s] % 9], dev(y, z, 1))
+
+        go(sent_a, make)
+
+    def b_z(k, origin, total):
         def make():
             ref = blk(k, y, zz(origin), 1)
-            return rc(ref, ref, rsend.at[k, way, s, 0], rrecv.at[k, way, s + 1, 0], ring_dev[way])
+            i = WAY[total]
+            return rc(ref, ref, rsend.at[k, i], rrecv.at[k, i], dev(y, zz(origin + total), c))
 
         go(sent_b, make)
+
+    def b_y(k, s):
+        for d in range(1, 4):
+            def make(d=d):
+                ref = blk(k, y, zz(s), 1)
+                i = (d - 1) * 9 + WAY[s]
+                return rc(ref, ref, ysend.at[k, i], yrecv.at[k, i], dev(lax.rem(y + d, 4), z, 1))
+
+            go(sent_b, make)
 
     def b_sib(k, d):
         def make():
             ref = yset(k, lax.rem(y + d, 4))
             return rc(ref, ref, bsend.at[k, d], brecv.at[k, d], dev(y, z, 0))
-
-        go(sent_b, make)
-
-    def a_y(k, d):
-        def make():
-            ref = blk(k, y, z, 0)
-            return rc(ref, ref, ysend.at[k, d], yrecv.at[k, d], dev(lax.rem(y + d, 4), z, 0))
-
-        go(sent_a, make)
-
-    def b_y(k, idx, origin, a, to):
-        def make():
-            ref = yhalf(k, lax.rem(y + origin, 4), a)
-            return rc(ref, ref, ysend.at[k, idx], yrecv.at[k, idx], dev(lax.rem(y + to, 4), z, 1))
 
         go(sent_b, make)
 
@@ -287,71 +327,78 @@
                     a_y(k, d)
             if n == 1:
                 for d in range(1, 4):
-                    got(blk(k, lax.rem(y + 4 - d, 4), z, 0), yrecv.at[k, d])
-                for hf in range(2):
-                    for way in range(2):
-                        a_ring(k, way, 0, hf, 0)
-                a_sib(k, 0, 0)
-            if n in (2, 3, 4):
-                s = n - 1
-                for hf in range(2):
-                    for way, origin in ((0, -s), (1, s)):
-                        got(half(k, zz(origin), hf), rrecv.at[k, way, s, hf])
-                        if s < 3 or hf == way:
-                            a_ring(k, way, s, hf, origin)
-                a_sib(k, 2 * s - 1, -s)
-                a_sib(k, 2 * s, s)
+                    got(blk(k, lax.rem(y + 4 - d, 4), z, 0), yrecv.at[k, d - 1])
+                for total in (2, -2, 1, -1):
+                    a_z(k, 0, total)
+                a_sib(k, 0)
+            if n == 2:
+                got(zset(k, zz(-2)), rrecv.at[k, WAY[2]])
+                a_z(k, -2, 4, 0)
+                a_z(k, -2, 3)
+                got(zset(k, zz(2)), rrecv.at[k, WAY[-2]])
+                a_z(k, 2, -4, 1)
+                a_z(k, 2, -3)
+                a_sib(k, -2)
+                a_sib(k, 2)
+            if n == 3:
+                for s in (1, -1):
+                    got(zset(k, zz(-s)), rrecv.at[k, WAY[s]])
+                    a_sib(k, -s)
+            if n == 4:
+                for s in (3, -3):
+                    got(zset(k, zz(-s)), rrecv.at[k, WAY[s]])
+                    a_sib(k, -s)
+                got(half(k, zz(4), 0), rrecv.at[k, WAY[4]])
+                got(half(k, zz(4), 1), rrecv.at[k, WAY[-4]])
+                a_sib(k, 4)
             if n == 5:
-                for way in range(2):
-                    got(half(k, zz(4), way), rrecv.at[k, way, 4, way])
-                a_sib(k, 7, 4)
-            if n == 7:
                 for d in range(4):
                     got(yset(k, lax.rem(y + d, 4)), brecv.at[k, d])
 
         @pl.when(c == 1)
         def _():
+            far = 4 if k == 0 else -4
             if n == 0:
-                for way in range(2):
-                    b_ring(k, way, 0, 0)
-            if n in (1, 2, 3):
-                s = n
-                for way, origin in ((0, -s), (1, s)):
-                    got(blk(k, y, zz(origin), 1), rrecv.at[k, way, s, 0])
-                    if s < 3 or way == 0:
-                        b_ring(k, way, s, origin)
+                for total in (2, -2, 1, -1):
+                    b_z(k, 0, total)
+                b_y(k, 0)
+            if n == 1:
+                for s in (2, -2):
+                    got(blk(k, y, zz(-s), 1), rrecv.at[k, WAY[s]])
+                    if far * s > 0:
+                        b_z(k, -s, far)
+                    b_z(k, -s, 3 if s > 0 else -3)
+                b_y(k, -2)
+                b_y(k, 2)
+            if n == 2:
+                for s in (1, -1):
+                    got(blk(k, y, zz(-s), 1), rrecv.at[k, WAY[s]])
+                    b_y(k, -s)
+            if n == 3:
+                for s in (3, -3):
+                    got(blk(k, y, zz(-s), 1), rrecv.at[k, WAY[s]])
+                    b_y(k, -s)
+                got(blk(k, y, zz(4), 1), rrecv.at[k, WAY[far]])
+                b_y(k, 4)
+                b_sib(k, 0)
             if n == 4:
-                got(blk(k, y, zz(4), 1), rrecv.at[k, 0, 4, 0])
-                for a in range(2):
-                    b_y(k, a, 0, a, 1)
-                    b_y(k, 3 - a, 0, 1 - a, 3)
-                b_sib(k, 0)
+                for d in range(1, 4):
+                    for s in (0, 2, -2, 1, -1, 3, -3, 4):
+                        got(blk(k, lax.rem(y + 4 - d, 4), zz(s), 1), yrecv.at[k, (d - 1) * 9 + WAY[s]])
+                    b_sib(k, 4 - d)
             if n == 5:
-                below, above = lax.rem(y + 3, 4), lax.rem(y + 1, 4)
-                got(yhalf(k, below, 0), yrecv.at[k, 0])
-                b_y(k, 4, 3, 0, 1)
-                got(yhalf(k, above, 1), yrecv.at[k, 3])
-                b_y(k, 5, 1, 1, 3)
-                got(yhalf(k, below, 1), yrecv.at[k, 1])
-                got(yhalf(k, above, 0), yrecv.at[k, 2])
-                b_sib(k, 3)
-                b_sib(k, 1)
-            if n == 6:
-                got(yhalf(k, lax.rem(y + 2, 4), 0), yrecv.at[k, 4])
-                got(yhalf(k, lax.rem(y + 2, 4), 1), yrecv.at[k, 5])
-                b_sib(k, 2)
-            if n == 7:
-                for idx, s in enumerate((0, -1, 1, -2, 2, -3, 3, 4)):
-                    got(zset(k, zz(s)), brecv.at[k, idx])
+                for s in (0, 2, -2, 1, -1, 3, -3, 4):
+                    got(zset(k, zz(s)), brecv.at[k, WAY[s]])
 
     own1.wait()
     for d in range(1, 8):
         got(r1.at[lax.rem(j + 8 - d, 8)], st1r.at[d])
-    chunk = jnp.dot(pick1[...], r1[...].reshape(256, 128), preferred_element_type=F32).astype(BF16)
     for dy in range(3):
-        w1[c, zi, dy, y, h] = chunk[dy * 48:dy * 48 + 48]
+        for m in range(8):
+            two = r1[m, 16 * (dy // 2):16 * (dy // 2) + 16].astype(F32)
+            stack[m * 6:m * 6 + 6, 0:128] = two[(dy % 2) * 8:(dy % 2) * 8 + 6]
+        w1[c, zi, dy, y, h] = stack[:, 0:128].astype(BF16)
     step(0, 0)
-
     @pl.when(x != y)
     def _():
         got(r2.at[j], st2r.at[0])
@@ -362,20 +409,21 @@
 
     for d in range(1, 8):
         got(r2.at[lax.rem(j + 8 - d, 8)], st2r.at[d])
-    chunk2 = jnp.dot(pick2[...], r2[...].reshape(128, 384), preferred_element_type=F32).astype(BF16)
-    w2[y, zi, c, pl.ds(pl.multiple_of(48 * h, 16), 48), :] = chunk2
+    for m in range(8):
+        stack[m * 6:m * 6 + 6] = r2[m].astype(F32)[0:6]
+    w2[y, zi, c, pl.ds(pl.multiple_of(48 * h, 16), 48), :] = stack[...].astype(BF16)
+    step(1, 0)
     step(0, 1)
-    step(1, 0)
     xstep(1)
+    xstep(3)
     step(0, 2)
-    xstep(3)
+    xstep(2)
     step(0, 3)
-    xstep(2)
+    step(1, 1)
     step(0, 4)
+    step(1, 2)
+    step(1, 3)
     step(0, 5)
-    step(1, 1)
-    step(0, 6)
-    step(0, 7)
     halo_wait()
 
     def conv1(fp):
@@ -397,7 +445,8 @@
 
     for fp in range(4):
         conv1(fp)
-        step(1, 2 + fp)
+        if fp == 1:
+            step(1, 4)
 
     lane = lax.broadcasted_iota(jnp.int32, (64, 128), 1)
     row = lax.broadcasted_iota(jnp.int32, (64, 128), 0)
@@ -419,7 +468,7 @@
             b_hi = p(0, 2) + p(1, 5)
             m0 = pltpu.roll(jnp.where(lane >= 96, a_lo, mid), 32, 1) + pltpu.roll(p(2, 2), 96, 1)
             m2 = pltpu.roll(jnp.where(lane >= 64, mid, b_hi), 64, 1) + pltpu.roll(p(2, 5), 96, 1)
-            hid = m1 + shift_down(m0) + shift_up(m2) + bias1[...]
+            hid = m1 + shift_down(m0) + shift_up(m2) + bias1
             hbuf[f, yy] = jnp.where(lane < 96, hid, 0.0)
         return carry
 
@@ -436,7 +485,6 @@
 
     for d in range(1, 4):
         ss_send(d).start()
-    step(1, 6)
     for d in range(1, 4):
         got(ssbuf.at[d], ssr.at[d])
     total = ssbuf[0] + ssbuf[1] + ssbuf[2] + ssbuf[3]
@@ -445,7 +493,7 @@
         precision=lax.Precision.HIGHEST, preferred_element_type=F32,
     ) * (1.0 / 384.0)
     hv = hbuf[...].reshape(1024, 128)
-    hbuf[...] = (hv * lax.rsqrt(ms + 1e-6) * gain2[...]).reshape(8, 2, 64, 128)
+    hbuf[...] = (hv * lax.rsqrt(ms + 1e-6) * gain2).reshape(8, 2, 64, 128)
 
     def spread(f, where, v):
         a2s[0, f + 2, where] = shift_down(v).astype(BF16)
@@ -473,7 +521,7 @@
     def _():
         h2down().start()
 
-    step(1, 7)
+    step(1, 5)
 
     @pl.when(t > 0)
     def _():
@@ -520,7 +568,7 @@
     for d in (2, 1, 3):
         sendb[d - 1] = conv2(lax.rem(x + d, 4)).astype(BF16).reshape(2, 2, 64, 384)
         out_send(d).start()
-    mine = conv2(x) + bias2[...] + lat[...].reshape(256, 384).astype(F32)
+    mine = conv2(x) + bias2 + lat[...].reshape(256, 384).astype(F32)
     for d in (2, 1, 3):
         got(recvb.at[d - 1], fr.at[d])
         mine = mine + recvb[d - 1].reshape(256, 384).astype(F32)
@@ -563,26 +611,21 @@
 
 
 def per_device(latents, gain_first, conv_first, bias_first, gain_second, conv_second, bias_second):
-    x = lax.axis_index("span")
-    w = lax.dynamic_slice_in_dim(conv_first, 96 * x, 96, axis=4)
-    w = jnp.stack([w[dt, :, dx] for dt, dx in SLOTS], axis=2)
-    w = w.reshape(18, 864)
-    w = jnp.pad(w, ((0, 14), (0, 160))).reshape(32, 8, 128)
-    s1 = jnp.transpose(w, (1, 0, 2))
-    v = jnp.pad(conv_second.reshape(27, 6, 384), ((0, 5), (0, 10), (0, 0)))
-    s2 = lax.dynamic_slice_in_dim(v, 8 * x, 8, axis=0)
-
-    def part(vec):
-        return jnp.pad(lax.dynamic_slice_in_dim(vec, 96 * x, 96), (0, 32)).reshape(1, 128)
-
     vm = pl.BlockSpec(memory_space=pltpu.VMEM)
     dma = pltpu.SemaphoreType.DMA
     return pl.pallas_call(
         kernel,
         out_shape=jax.ShapeDtypeStruct((2, 2, 64, 384), BF16),
-        in_specs=[vm] * 9,
+        in_specs=[pl.BlockSpec(memory_space=pl.ANY)] * 7,
         out_specs=vm,
         scratch_shapes=[
+            pltpu.VMEM((2, 2, 64, 384), BF16),
+            pltpu.VMEM((4, 384), F32),
+            pltpu.VMEM((27, 6, 384), BF16),
+            pltpu.VMEM((27, 6, 384), BF16),
+            pltpu.VMEM((8, 32, 128), BF16),
+            pltpu.VMEM((8, 16, 384), BF16),
+            pltpu.VMEM((48, 384), F32),
             pltpu.VMEM((8, 32, 128), BF16),
             pltpu.VMEM((8, 16, 384), BF16),
             pltpu.VMEM((2, 4, 3, 4, 2, 48, 128), BF16),
@@ -595,8 +638,8 @@
             pltpu.VMEM((2, 8, 64, 128), BF16),
             pltpu.VMEM((3, 2, 2, 64, 384), BF16),
             pltpu.VMEM((3, 2, 2, 64, 384), BF16),
-            dma((8,)), dma((8,)), dma((8,)), dma((8,)), dma((3,)),
-            dma((2, 6)), dma((2, 6)), dma((2, 2, 4, 2)), dma((2, 2, 5, 2)), dma((2, 8)), dma((2, 8)),
+            dma((7,)), dma((8,)), dma((8,)), dma((8,)), dma((8,)), dma((3,)),
+            dma((2, 27)), dma((2, 27)), dma((2, 9)), dma((2, 9)), dma((2, 9)), dma((2, 9)),
             dma((4,)), dma((4,)), dma((4,)), dma((4,)), dma((4,)), dma((4,)),
             dma((4,)), dma((4,)), dma((2,)), dma((2,)), dma((4,)), dma((4,)),
         ],
@@ -605,9 +648,8 @@
         ),
         cost_estimate=pl.CostEstimate(flops=4_000_000_000, bytes_accessed=8_000_000, transcendentals=400_000),
     )(
-        latents, gain_first.reshape(1, 384), part(bias_first), part(gain_second),
-        bias_second.reshape(1, 384), s1, s2,
-        jnp.asarray(one_hot_first(), BF16), jnp.asarray(one_hot_second(), BF16),
+        latents, gain_first, bias_first, gain_second, bias_second,
+        conv_first.reshape(27, 6, 384), conv_second.reshape(27, 6, 384),
     )
 
 

time: 94.4 us -> 83.2 us (0.88)
  local copies, waits for them, and re-layouts: 12.4 us -> 6.16 us
  Pallas kernels: 81 us -> 76.7 us
    pallas_call x1, Pallas kernels: 81 us -> 76.7 us  [per_device(): pl.pallas_call(kernel, out_shape=jax.ShapeDtypeStruct((2, 2, 64, 384), BF...]
    unnamed x21 -> x15, local copies, waits for them, and re-layouts: 9.96 us -> 6.16 us
    dynamic_slice x3 -> x0, local copies, waits for them, and re-layouts: 1.54 us -> none  [the longest x2 1.51 us: part(): lax.dynamic_slice_in_dim(vec, 96 * x, 96)]
where the time goes in v2:
time: 83.2 us; the launch traced here: 82.9 us
  Pallas kernels  76.7 us (92%)
  local copies, waits for them, and re-layouts  6.16 us (7%)
    pallas_call x1, Pallas kernels, per_device(): pl.pallas_call(kernel, out_shape=jax.ShapeDtypeStruct((2, 2, 64, 384), BF...  76.7 us
    unnamed x15, local copies, waits for them, and re-layouts  6.16 us

profile of v2, /device:TPU:1, one launch (start us, length us, event | category | flops | bytes accessed | tf_op | source)
XLA Modules:
  0.0 82.9 jit_solution(3798277155053032724)
XLA Ops:
  0.0 0.0 copy-start.3
  0.0 0.7 copy-done.3
  0.7 0.0 copy-start
  0.7 0.9 %copy-done = bf16[2,2,64,384]{3,2,1,0:T(8,128)(2,1)S(1)} copy-done((bf16[2,2,64,384]{3,2,1,0:T(8,128)(2,1)S(1)}, bf16[2,2,64,384]{3,2,1,0:T(8,128)(2,1)}, u32[]{:S(2)}) %copy-start) | copy-done | bytes 196632
  1.6 0.0 copy-start.1
  1.6 0.9 %copy-done.1 = bf16[3,3,3,6,384]{4,3,2,1,0:T(8,128)(2,1)S(1)} copy-done((bf16[3,3,3,6,384]{4,3,2,1,0:T(8,128)(2,1)S(1)}, bf16[3,3,3,6,384]{4,3,2,1,0:T(8,128)(2,1)}, u32[]{:S(2)}) %copy-start.1) | copy-done | bytes 124440
  2.5 0.0 copy-start.2
  2.5 0.9 %copy-done.2 = bf16[3,3,3,6,384]{4,3,2,1,0:T(8,128)(2,1)S(1)} copy-done((bf16[3,3,3,6,384]{4,3,2,1,0:T(8,128)(2,1)S(1)}, bf16[3,3,3,6,384]{4,3,2,1,0:T(8,128)(2,1)}, u32[]{:S(2)}) %copy-start.2) | copy-done | bytes 124440
  3.4 0.0 copy-start.4
  3.4 0.7 copy-done.4
  4.1 0.0 copy-start.5
  4.1 0.7 copy-done.5
  4.8 0.0 copy-start.6
  4.8 0.7 copy-done.6
  5.5 76.7 %shard_map.73 = bf16[2,2,64,384]{3,2,1,0:T(8,128)(2,1)S(1)} custom-call(bf16[2,2,64,384]{3,2,1,0:T(8,128)(2,1)S(1)} %copy-done, f32[384]{0:T(512)S(1)} %copy-done.3, f32[384]{0:T(512)S(1)} %copy-done.4, f32[384]{0:T(512)S(1)} %copy-done.5, f32[384]{0:T(512)S(1)} %copy-done.6, bf16[27,6,384]{2,1,0:T(8,128)(2,1)S(1)} %bitcast.2, bf16[27,6,384]{2,1,0:T(8,128)(2,1)S(1)} %bitcast.3), custom_call_target="tpu_custom_call" | custom-call | flops 4000000000 | bytes 8000000 | tf_op jit(solution)/shard_map/pallas_call | solution.py:616
  82.2 0.7 copy.9
Async XLA Ops:
  0.0 0.7 copy-start.3
  0.7 0.9 %copy-start = (bf16[2,2,64,384]{3,2,1,0:T(8,128)(2,1)S(1)}, bf16[2,2,64,384]{3,2,1,0:T(8,128)(2,1)}, u32[]{:S(2)}) copy-start(bf16[2,2,64,384]{3,2,1,0:T(8,128)(2,1)} %lat_hbm.1) | copy-start | bytes 589828
  1.6 0.9 %copy-start.1 = (bf16[3,3,3,6,384]{4,3,2,1,0:T(8,128)(2,1)S(1)}, bf16[3,3,3,6,384]{4,3,2,1,0:T(8,128)(2,1)}, u32[]{:S(2)}) copy-start(bf16[3,3,3,6,384]{4,3,2,1,0:T(8,128)(2,1)} %param.9) | copy-start | bytes 373252
  2.5 0.9 %copy-start.2 = (bf16[3,3,3,6,384]{4,3,2,1,0:T(8,128)(2,1)S(1)}, bf16[3,3,3,6,384]{4,3,2,1,0:T(8,128)(2,1)}, u32[]{:S(2)}) copy-start(bf16[3,3,3,6,384]{4,3,2,1,0:T(8,128)(2,1)} %param.12) | copy-start | bytes 373252
  3.4 0.7 copy-start.4
  4.1 0.7 copy-start.5
  4.8 0.7 copy-start.6

commit v3 on v2

--- a/solution.py
+++ b/solution.py
@@ -318,6 +318,59 @@
             return rc(ref, ref, bsend.at[k, d], brecv.at[k, d], dev(y, z, 0))
 
         go(sent_b, make)
+
+    def wset(yy, cc):
+        return w2.at[yy, :, cc, 0:96, :]
+
+    def z2_send(origin, total):
+        ref = blk(1, y, zz(origin), c)
+        i = WAY[total]
+        return rc(ref, ref, rsend.at[1, i], rrecv.at[1, i], dev(y, zz(origin + total), c))
+
+    def z2_got(total):
+        got(blk(1, y, zz(-total), c), rrecv.at[1, WAY[total]])
+
+    def y2_send(d):
+        ref = wset(y, c)
+        return rc(ref, ref, ysend.at[1, d], yrecv.at[1, d], dev(lax.rem(y + d, 4), z, c))
+
+    def sib2_send(d):
+        ref = wset(lax.rem(y + d, 4), c)
+        return rc(ref, ref, bsend.at[1, d], brecv.at[1, d], dev(y, z, 1 - c))
+
+    Z2 = ((0, 2), (0, -2), (0, 1), (0, -1), (-2, 4), (-2, 3), (2, -3))
+
+    def step2(n):
+        if n == 0:
+            for origin, total in Z2[:4]:
+                z2_send(origin, total).start()
+        if n == 1:
+            z2_got(2)
+            z2_send(-2, 4).start()
+            z2_send(-2, 3).start()
+            z2_got(-2)
+            z2_send(2, -3).start()
+        if n == 2:
+            for total in (1, -1, 3, -3, 4):
+                z2_got(total)
+            for d in (2, 1, 3):
+                y2_send(d).start()
+            sib2_send(0).start()
+        if n == 3:
+            for d in (1, 3, 2):
+                got(wset(lax.rem(y + 4 - d, 4), c), yrecv.at[1, d])
+                sib2_send(4 - d).start()
+        if n == 4:
+            for d in range(4):
+                got(wset(lax.rem(y + d, 4), 1 - c), brecv.at[1, d])
+
+    def step2_sent():
+        for origin, total in Z2:
+            z2_send(origin, total).wait_send()
+        for d in range(1, 4):
+            y2_send(d).wait_send()
+        for d in range(4):
+            sib2_send(d).wait_send()
 
     def step(k, n):
         @pl.when(c == 0)
@@ -399,6 +452,8 @@
             stack[m * 6:m * 6 + 6, 0:128] = two[(dy % 2) * 8:(dy % 2) * 8 + 6]
         w1[c, zi, dy, y, h] = stack[:, 0:128].astype(BF16)
     step(0, 0)
+    step(0, 1)
+
     @pl.when(x != y)
     def _():
         got(r2.at[j], st2r.at[0])
@@ -412,19 +467,17 @@
     for m in range(8):
         stack[m * 6:m * 6 + 6] = r2[m].astype(F32)[0:6]
     w2[y, zi, c, pl.ds(pl.multiple_of(48 * h, 16), 48), :] = stack[...].astype(BF16)
-    step(1, 0)
-    step(0, 1)
+    step2(0)
+    step(0, 2)
     xstep(1)
     xstep(3)
-    step(0, 2)
+    step(0, 3)
     xstep(2)
-    step(0, 3)
-    step(1, 1)
+    step2(1)
+    step2(2)
     step(0, 4)
-    step(1, 2)
-    step(1, 3)
+    halo_wait()
     step(0, 5)
-    halo_wait()
 
     def conv1(fp):
         rows = []
@@ -445,8 +498,6 @@
 
     for fp in range(4):
         conv1(fp)
-        if fp == 1:
-            step(1, 4)
 
     lane = lax.broadcasted_iota(jnp.int32, (64, 128), 1)
     row = lax.broadcasted_iota(jnp.int32, (64, 128), 0)
@@ -521,7 +572,8 @@
     def _():
         h2down().start()
 
-    step(1, 5)
+    step2(3)
+    step2(4)
 
     @pl.when(t > 0)
     def _():
@@ -599,6 +651,8 @@
             down(lax.rem(x + 4 - d, 4), d).wait_send()
         h2down().wait_send()
 
+    step2_sent()
+
     @pl.when(c == 0)
     def _():
         for make in sent_a:
@@ -616,7 +670,7 @@
     return pl.pallas_call(
         kernel,
         out_shape=jax.ShapeDtypeStruct((2, 2, 64, 384), BF16),
-        in_specs=[pl.BlockSpec(memory_space=pl.ANY)] * 7,
+        in_specs=[pl.BlockSpec(memory_space=pltpu.HBM)] * 7,
         out_specs=vm,
         scratch_shapes=[
             pltpu.VMEM((2, 2, 64, 384), BF16),
@@ -644,7 +698,7 @@
             dma((4,)), dma((4,)), dma((2,)), dma((2,)), dma((4,)), dma((4,)),
         ],
         compiler_params=pltpu.CompilerParams(
-            collective_id=0, has_side_effects=True, vmem_limit_bytes=48 * 1024 * 1024
+            collective_id=0, has_side_effects=True, vmem_limit_bytes=63 * 1024 * 1024
         ),
         cost_estimate=pl.CostEstimate(flops=4_000_000_000, bytes_accessed=8_000_000, transcendentals=400_000),
     )(

time: 83.2 us -> 73.8 us (0.89)
  Pallas kernels: 76.7 us -> 72.1 us
  local copies, waits for them, and re-layouts: 6.16 us -> 1.62 us
    pallas_call x1, Pallas kernels: 76.7 us -> 72.1 us  [per_device(): pl.pallas_call(kernel, out_shape=jax.ShapeDtypeStruct((2, 2, 64, 384), BF...]
    unnamed x15 -> x1, local copies, waits for them, and re-layouts: 6.16 us -> 1.62 us
where the time goes in v3:
time: 73.8 us; the launch traced here: 73.7 us
  Pallas kernels  72.1 us (98%)
  local copies, waits for them, and re-layouts  1.62 us (2%)
    pallas_call x1, Pallas kernels, per_device(): pl.pallas_call(kernel, out_shape=jax.ShapeDtypeStruct((2, 2, 64, 384), BF...  72.1 us
    unnamed x1, local copies, waits for them, and re-layouts  1.62 us

profile of v3, /device:TPU:1, one launch (start us, length us, event | category | flops | bytes accessed | tf_op | source)
XLA Modules:
  0.0 73.7 jit_solution(11773816389677510276)
XLA Ops:
  0.0 72.1 %shard_map.73 = bf16[2,2,64,384]{3,2,1,0:T(8,128)(2,1)} custom-call(bf16[2,2,64,384]{3,2,1,0:T(8,128)(2,1)} %lat_hbm.1, f32[384]{0:T(512)} %gain1_hbm.1, f32[384]{0:T(512)} %bias1_hbm.1, f32[384]{0:T(512)} %gain2_hbm.1, f32[384]{0:T(512)} %bias2_hbm.1, bf16[27,6,384]{2,1,0:T(8,128)(2,1)} %bitcast.2, bf16[27,6,384]{2,1,0:T(8,128)(2,1)} %bitcast.3), custom_call_target="tpu_custom_call" | custom-call | flops 4000000000 | bytes 8000000 | tf_op jit(solution)/shard_map/pallas_call | solution.py:670
  72.1 1.6 %copy.9 = bf16[2,2,64,384]{3,2,1,0:T(8,128)(2,1)} copy(bf16[2,2,64,384]{3,2,1,0:T(8,128)(2,1)} %shard_map.73) | data formatting | bytes 393216

commit v4 on v3

--- a/solution.py
+++ b/solution.py
@@ -21,7 +21,7 @@
     lat, vec, k1, k2, s1, s2, stack,
     r1, r2, w1, w2, abuf, pbuf, hbuf, ssbuf, a2s, a2h, sendb, recvb,
     ins, st1s, st1r, st2s, st2r, loc,
-    ysend, yrecv, rsend, rrecv, bsend, brecv,
+    w1zs, w1zr, ysend, yrecv, rsend, rrecv, bsend, brecv,
     xs, xr, ups, upr, dns, dnr, sss, ssr, h2s, h2r, fs, fr,
 ):
     x = lax.axis_index("span")
@@ -60,8 +60,10 @@
     def hail(device):
         pl.semaphore_signal(barrier, inc=1, device_id=device, device_id_type=MESH)
 
-    for d in range(1, 8):
-        hail((x, g * 8 + lax.rem(j + d, 8)))
+    for e in range(4):
+        for d in range(8):
+            if e or d:
+                hail((x, lax.rem(y + e, 4) * 16 + h * 8 + lax.rem(j + d, 8)))
 
     @pl.when(x != y)
     def _():
@@ -70,8 +72,6 @@
 
     for d in range(1, 4):
         hail((lax.rem(x + d, 4), t))
-    for d in range(1, 4):
-        hail(dev(lax.rem(y + d, 4), z, c))
     for d in (1, 2, 6, 7):
         hail(dev(y, lax.rem(z + d, 8), c))
 
@@ -126,6 +126,7 @@
     bias1 = jnp.where(lane8[0:1] < 96, mine96(jnp.broadcast_to(vec[1:2], (8, 384)))[0:1], 0.0)
     gain2 = jnp.where(lane8[0:1] < 96, mine96(jnp.broadcast_to(vec[2:3], (8, 384)))[0:1], 0.0)
 
+    w1[1, 3] = jnp.zeros((3, 4, 2, 48, 128), BF16)
     w2[:, :, :, 96:128, :] = jnp.zeros((4, 4, 2, 32, 384), BF16)
     a2s[:, 0:2] = jnp.zeros((3, 2, 4, 64, 128), BF16)
 
@@ -144,12 +145,12 @@
 
     lax.fori_loop(0, 2, act1, 0)
 
-    many = jnp.where(x != y, 8, 0) + jnp.where(t > 0, 1, 0) + jnp.where(t < 63, 1, 0) + 17
+    many = jnp.where(x != y, 8, 0) + jnp.where(t > 0, 1, 0) + jnp.where(t < 63, 1, 0) + 38
     pl.semaphore_wait(barrier, many)
 
-    def st1(d):
+    def st1(e, d):
         jj = lax.rem(j + d, 8)
-        return rc(s1.at[jj], r1.at[j], st1s.at[d], st1r.at[d], (x, g * 8 + jj))
+        return rc(s1.at[jj], r1.at[y, j], st1s.at[e, d], st1r.at[e, d], (x, lax.rem(y + e, 4) * 16 + h * 8 + jj))
 
     def st2(d):
         jj = lax.rem(j + d, 8)
@@ -158,9 +159,15 @@
     def own2():
         return pltpu.make_async_copy(s2.at[j], r2.at[j], loc.at[1])
 
-    for d in range(1, 8):
-        st1(d).start()
-    own1 = pltpu.make_async_copy(s1.at[j], r1.at[j], loc.at[0])
+    for e in (2, 1, 3, 0):
+        for d in range(8):
+            if e or d:
+
+                @pl.when(lax.rem(j + d, 8) != 7)
+                def _():
+                    st1(e, d).start()
+
+    own1 = pltpu.make_async_copy(s1.at[j], r1.at[y, j], loc.at[0])
     own1.start()
 
     def xsend(d):
@@ -229,41 +236,16 @@
             st2(d).start()
     halo_send(0)
 
-    def own_slice(k):
-        if k == 0:
-            return w1.at[c, zi, :, y, h]
-        return w2.at[y, zi, c, pl.ds(pl.multiple_of(48 * h, 16), 48), :]
-
     def blk(k, yy, zz, cc):
         if k == 0:
             return w1.at[cc, lax.rem(zz, 4), :, yy, lax.div(zz, 4)]
         return w2.at[yy, lax.rem(zz, 4), cc, pl.ds(pl.multiple_of(48 * lax.div(zz, 4), 16), 48), :]
 
-    def half(k, zz, hf):
-        if k == 0:
-            return w1.at[0, lax.rem(zz, 4), :, 2 * hf:2 * hf + 2, lax.div(zz, 4)]
-        return w2.at[2 * hf:2 * hf + 2, lax.rem(zz, 4), 0, pl.ds(pl.multiple_of(48 * lax.div(zz, 4), 16), 48), :]
-
-    def zset(k, zz):
-        if k == 0:
-            return w1.at[0, lax.rem(zz, 4), :, :, lax.div(zz, 4)]
-        return w2.at[:, lax.rem(zz, 4), 0, pl.ds(pl.multiple_of(48 * lax.div(zz, 4), 16), 48), :]
-
-    def yset(k, yy):
-        if k == 0:
-            return w1.at[1, :, :, yy]
-        return w2.at[yy, :, 1, 0:96, :]
-
-    def yhalf(k, yy, a):
-        if k == 0:
-            return w1.at[1, 2 * a:2 * a + 2, :, yy]
-        return w2.at[yy, 2 * a:2 * a + 2, 1, 0:96, :]
-
-    sent_a, sent_b = [], []
-
-    def go(group, make):
-        make().start()
-        group.append(make)
+    def zset(zz):
+        return w1.at[1, lax.rem(zz, 4), :, :, lax.div(zz, 4)]
+
+    def yset(yy):
+        return w1.at[0, :, :, yy]
 
     def got(ref, rsem):
         rc(ref, ref, loc.at[2], rsem, (x, t)).wait_recv()
@@ -271,53 +253,184 @@
     def zz(s):
         return lax.rem(z + 8 + s, 8)
 
-    def a_y(k, d):
-        def make():
-            ref = blk(k, y, z, 0)
-            return rc(ref, ref, ysend.at[k, d - 1], yrecv.at[k, d - 1], dev(lax.rem(y + d, 4), z, 0))
-
-        go(sent_a, make)
-
     WAY = {1: 0, -1: 1, 2: 2, -2: 3, 3: 4, -3: 5, 4: 6, -4: 7, 0: 8}
 
-    def a_z(k, origin, total, hf=None):
-        def make():
-            ref = zset(k, zz(origin)) if hf is None else half(k, zz(origin), hf)
-            i = WAY[total]
-            return rc(ref, ref, rsend.at[k, i], rrecv.at[k, i], dev(y, zz(origin + total), c))
-
-        go(sent_a, make)
-
-    def a_sib(k, s):
-        def make():
-            ref = zset(k, zz(s))
-            return rc(ref, ref, bsend.at[k, WAY[s] % 9], brecv.at[k, WAY[s] % 9], dev(y, z, 1))
-
-        go(sent_a, make)
-
-    def b_z(k, origin, total):
-        def make():
-            ref = blk(k, y, zz(origin), 1)
-            i = WAY[total]
-            return rc(ref, ref, rsend.at[k, i], rrecv.at[k, i], dev(y, zz(origin + total), c))
-
-        go(sent_b, make)
-
-    def b_y(k, s):
-        for d in range(1, 4):
-            def make(d=d):
-                ref = blk(k, y, zz(s), 1)
-                i = (d - 1) * 9 + WAY[s]
-                return rc(ref, ref, ysend.at[k, i], yrecv.at[k, i], dev(lax.rem(y + d, 4), z, 1))
-
-            go(sent_b, make)
-
-    def b_sib(k, d):
-        def make():
-            ref = yset(k, lax.rem(y + d, 4))
-            return rc(ref, ref, bsend.at[k, d], brecv.at[k, d], dev(y, z, 0))
-
-        go(sent_b, make)
+    def yy_of(e):
+        return lax.rem(y + e, 4)
+
+    def live(origin):
+        return lax.rem(z + 8 + origin, 4) != 3
+
+    def a_z(e, origin, total):
+        ref = blk(0, yy_of(e), zz(origin), 1)
+        i = WAY[total]
+        return rc(ref, ref, w1zs.at[i, e], w1zr.at[i, e], dev(y, zz(origin + total), 1))
+
+    def a_got(e, total):
+        got(blk(0, yy_of(e), zz(-total), 1), w1zr.at[WAY[total], e])
+
+    def a_sib(s):
+        ref = zset(zz(s))
+        return rc(ref, ref, bsend.at[0, WAY[s]], brecv.at[0, WAY[s]], dev(y, z, 0))
+
+    def b_z(origin, total):
+        ref = blk(0, y, zz(origin), 0)
+        i = WAY[total]
+        return rc(ref, ref, w1zs.at[i, 0], w1zr.at[i, 0], dev(y, zz(origin + total), 0))
+
+    def b_got(total):
+        got(blk(0, y, zz(-total), 0), w1zr.at[WAY[total], 0])
+
+    def b_y(d, s):
+        ref = blk(0, y, zz(s), 0)
+        i = (d - 1) * 9 + WAY[s]
+        return rc(ref, ref, ysend.at[0, i], yrecv.at[0, i], dev(lax.rem(y + d, 4), z, 0))
+
+    def b_sib(d):
+        ref = yset(lax.rem(y + d, 4))
+        return rc(ref, ref, bsend.at[0, d], brecv.at[0, d], dev(y, z, 1))
+
+    AROUND = (2, -2, 1, -1)
+
+    def a_relays(e, total):
+        if total == 2:
+            return ((-2, 3), (-2, 4)) if e < 2 else ((-2, 3),)
+        return ((2, -3), (2, -4)) if e >= 2 else ((2, -3),)
+
+    B_RELAYS = {2: ((-2, 4), (-2, 3)), -2: ((2, -3),)}
+    OTHERS = (2, -2, 1, -1, 3, -3, 4)
+
+    def on_core(core, f):
+        @pl.when(c == core)
+        def _():
+            f()
+
+    def when_live(origin, f):
+        @pl.when(live(origin))
+        def _():
+            f()
+
+    def first(e):
+        def send_a():
+            for total in AROUND:
+                a_z(e, 0, total).start()
+
+        on_core(1, lambda: when_live(0, send_a))
+        if e == 0:
+
+            def send_b():
+                for total in AROUND:
+                    b_z(0, total).start()
+
+            on_core(0, send_b)
+
+    def step(n):
+        def core1():
+            if n == 1:
+                for total in (2, -2):
+
+                    def relay(total=total):
+                        for e in (0, 1, 3, 2):
+                            a_got(e, total)
+                            for origin, far in a_relays(e, total):
+                                a_z(e, origin, far).start()
+                        a_sib(-total).start()
+
+                    when_live(-total, relay)
+                when_live(0, lambda: a_sib(0).start())
+            if n == 2:
+                for total in (1, -1):
+
+                    def take(total=total):
+                        for e in range(4):
+                            a_got(e, total)
+                        a_sib(-total).start()
+
+                    when_live(-total, take)
+            if n == 3:
+                for total in (3, -3):
+
+                    def take(total=total):
+                        for e in range(4):
+                            a_got(e, total)
+                        a_sib(-total).start()
+
+                    when_live(-total, take)
+
+                def last():
+                    for e in range(4):
+                        a_got(e, 4 if e < 2 else -4)
+                    a_sib(4).start()
+
+                when_live(4, last)
+            if n == 5:
+                for d in range(4):
+                    got(yset(yy_of(d)), brecv.at[0, d])
+
+        def core0():
+            if n == 1:
+                for total in (2, -2):
+                    b_got(total)
+                    for origin, far in B_RELAYS[total]:
+                        b_z(origin, far).start()
+                    for d in (2, 1, 3):
+                        b_y(d, -total).start()
+            if n == 2:
+                for total in (1, -1):
+                    b_got(total)
+                    for d in (2, 1, 3):
+                        b_y(d, -total).start()
+            if n == 3:
+                for total, origin in ((3, -3), (-3, 3), (4, 4)):
+                    b_got(total)
+                    for d in (2, 1, 3):
+                        b_y(d, origin).start()
+                b_sib(0).start()
+            if n == 4:
+                for d in (1, 3, 2):
+                    for s in OTHERS:
+                        got(blk(0, lax.rem(y + 4 - d, 4), zz(s), 0), yrecv.at[0, (d - 1) * 9 + WAY[s]])
+                    b_sib(4 - d).start()
+            if n == 5:
+                for s in (0,) + OTHERS:
+                    when_live(s, lambda s=s: got(zset(zz(s)), brecv.at[0, WAY[s]]))
+
+        on_core(1, core1)
+        on_core(0, core0)
+
+    def step_sent():
+        def core1():
+            def own():
+                for e in range(4):
+                    for total in AROUND:
+                        a_z(e, 0, total).wait_send()
+
+            when_live(0, own)
+            for total in (2, -2):
+
+                def relayed(total=total):
+                    for e in range(4):
+                        for origin, far in a_relays(e, total):
+                            a_z(e, origin, far).wait_send()
+
+                when_live(-total, relayed)
+            for s in (0,) + OTHERS:
+                when_live(s, lambda s=s: a_sib(s).wait_send())
+
+        def core0():
+            for total in AROUND:
+                b_z(0, total).wait_send()
+            for total in (2, -2):
+                for origin, far in B_RELAYS[total]:
+                    b_z(origin, far).wait_send()
+            for s in OTHERS:
+                for d in range(1, 4):
+                    b_y(d, s).wait_send()
+            for d in range(4):
+                b_sib(d).wait_send()
+
+        on_core(1, core1)
+        on_core(0, core0)
 
     def wset(yy, cc):
         return w2.at[yy, :, cc, 0:96, :]
@@ -372,87 +485,23 @@
         for d in range(4):
             sib2_send(d).wait_send()
 
-    def step(k, n):
-        @pl.when(c == 0)
+    own1.wait()
+    for e in (0, 1, 3, 2):
+        src = lax.rem(y + e, 4)
+
+        @pl.when(j != 7)
         def _():
-            if n == 0:
-                for d in range(1, 4):
-                    a_y(k, d)
-            if n == 1:
-                for d in range(1, 4):
-                    got(blk(k, lax.rem(y + 4 - d, 4), z, 0), yrecv.at[k, d - 1])
-                for total in (2, -2, 1, -1):
-                    a_z(k, 0, total)
-                a_sib(k, 0)
-            if n == 2:
-                got(zset(k, zz(-2)), rrecv.at[k, WAY[2]])
-                a_z(k, -2, 4, 0)
-                a_z(k, -2, 3)
-                got(zset(k, zz(2)), rrecv.at[k, WAY[-2]])
-                a_z(k, 2, -4, 1)
-                a_z(k, 2, -3)
-                a_sib(k, -2)
-                a_sib(k, 2)
-            if n == 3:
-                for s in (1, -1):
-                    got(zset(k, zz(-s)), rrecv.at[k, WAY[s]])
-                    a_sib(k, -s)
-            if n == 4:
-                for s in (3, -3):
-                    got(zset(k, zz(-s)), rrecv.at[k, WAY[s]])
-                    a_sib(k, -s)
-                got(half(k, zz(4), 0), rrecv.at[k, WAY[4]])
-                got(half(k, zz(4), 1), rrecv.at[k, WAY[-4]])
-                a_sib(k, 4)
-            if n == 5:
-                for d in range(4):
-                    got(yset(k, lax.rem(y + d, 4)), brecv.at[k, d])
-
-        @pl.when(c == 1)
-        def _():
-            far = 4 if k == 0 else -4
-            if n == 0:
-                for total in (2, -2, 1, -1):
-                    b_z(k, 0, total)
-                b_y(k, 0)
-            if n == 1:
-                for s in (2, -2):
-                    got(blk(k, y, zz(-s), 1), rrecv.at[k, WAY[s]])
-                    if far * s > 0:
-                        b_z(k, -s, far)
-                    b_z(k, -s, 3 if s > 0 else -3)
-                b_y(k, -2)
-                b_y(k, 2)
-            if n == 2:
-                for s in (1, -1):
-                    got(blk(k, y, zz(-s), 1), rrecv.at[k, WAY[s]])
-                    b_y(k, -s)
-            if n == 3:
-                for s in (3, -3):
-                    got(blk(k, y, zz(-s), 1), rrecv.at[k, WAY[s]])
-                    b_y(k, -s)
-                got(blk(k, y, zz(4), 1), rrecv.at[k, WAY[far]])
-                b_y(k, 4)
-                b_sib(k, 0)
-            if n == 4:
-                for d in range(1, 4):
-                    for s in (0, 2, -2, 1, -1, 3, -3, 4):
-                        got(blk(k, lax.rem(y + 4 - d, 4), zz(s), 1), yrecv.at[k, (d - 1) * 9 + WAY[s]])
-                    b_sib(k, 4 - d)
-            if n == 5:
-                for s in (0, 2, -2, 1, -1, 3, -3, 4):
-                    got(zset(k, zz(s)), brecv.at[k, WAY[s]])
-
-    own1.wait()
-    for d in range(1, 8):
-        got(r1.at[lax.rem(j + 8 - d, 8)], st1r.at[d])
-    for dy in range(3):
-        for m in range(8):
-            two = r1[m, 16 * (dy // 2):16 * (dy // 2) + 16].astype(F32)
-            stack[m * 6:m * 6 + 6, 0:128] = two[(dy % 2) * 8:(dy % 2) * 8 + 6]
-        w1[c, zi, dy, y, h] = stack[:, 0:128].astype(BF16)
-    step(0, 0)
-    step(0, 1)
+            for d in range(8):
+                if e or d:
+                    got(r1.at[src, lax.rem(j + 8 - d, 8)], st1r.at[(4 - e) % 4, d])
+            for dy in range(3):
+                for m in range(8):
+                    two = r1[src, m, 16 * (dy // 2):16 * (dy // 2) + 16].astype(F32)
+                    stack[m * 6:m * 6 + 6, 0:128] = two[(dy % 2) * 8:(dy % 2) * 8 + 6]
+                w1[c, zi, dy, src, h] = stack[:, 0:128].astype(BF16)
+
+        first(e)
+    step(1)
 
     @pl.when(x != y)
     def _():
@@ -467,23 +516,23 @@
     for m in range(8):
         stack[m * 6:m * 6 + 6] = r2[m].astype(F32)[0:6]
     w2[y, zi, c, pl.ds(pl.multiple_of(48 * h, 16), 48), :] = stack[...].astype(BF16)
-    step2(0)
-    step(0, 2)
+    step(2)
     xstep(1)
     xstep(3)
-    step(0, 3)
+    step(3)
+    step2(0)
     xstep(2)
     step2(1)
     step2(2)
-    step(0, 4)
+    step(4)
     halo_wait()
-    step(0, 5)
-
-    def conv1(fp):
+    step(5)
+
+    def conv1():
         rows = []
         for yy in range(2):
             rows.append(jnp.concatenate(
-                [abuf[fp, :, yy + dy].reshape(128, 384) for dy in range(3)], axis=1))
+                [abuf[:, :, yy + dy].reshape(512, 384) for dy in range(3)], axis=1))
         lhs = jnp.concatenate(rows, axis=0)
 
         def tile(n, carry):
@@ -491,13 +540,12 @@
                 [w1[0, n].reshape(1152, 128), w1[1, n].reshape(1152, 128)], axis=1)
             res = jnp.dot(lhs, rhs, preferred_element_type=F32)
             for yy in range(2):
-                pbuf[n, 2 + 2 * fp:4 + 2 * fp, yy] = res[yy * 128:yy * 128 + 128].reshape(2, 64, 256)
+                pbuf[n, 2:10, yy] = res[yy * 512:yy * 512 + 512].reshape(8, 64, 256)
             return carry
 
         lax.fori_loop(0, 4, tile, 0)
 
-    for fp in range(4):
-        conv1(fp)
+    conv1()
 
     lane = lax.broadcasted_iota(jnp.int32, (64, 128), 1)
     row = lax.broadcasted_iota(jnp.int32, (64, 128), 0)
@@ -626,8 +674,15 @@
         mine = mine + recvb[d - 1].reshape(256, 384).astype(F32)
     out[...] = mine.astype(BF16).reshape(2, 2, 64, 384)
 
+    for e in range(4):
+        for d in range(8):
+            if e or d:
+
+                @pl.when(lax.rem(j + d, 8) != 7)
+                def _():
+                    st1(e, d).wait_send()
+
     for d in range(1, 8):
-        st1(d).wait_send()
         st2(d).wait_send()
 
     @pl.when(x != y)
@@ -653,15 +708,7 @@
 
     step2_sent()
 
-    @pl.when(c == 0)
-    def _():
-        for make in sent_a:
-            make().wait_send()
-
-    @pl.when(c == 1)
-    def _():
-        for make in sent_b:
-            make().wait_send()
+    step_sent()
 
 
 def per_device(latents, gain_first, conv_first, bias_first, gain_second, conv_second, bias_second):
@@ -680,7 +727,7 @@
             pltpu.VMEM((8, 32, 128), BF16),
             pltpu.VMEM((8, 16, 384), BF16),
             pltpu.VMEM((48, 384), F32),
-            pltpu.VMEM((8, 32, 128), BF16),
+            pltpu.VMEM((4, 8, 32, 128), BF16),
             pltpu.VMEM((8, 16, 384), BF16),
             pltpu.VMEM((2, 4, 3, 4, 2, 48, 128), BF16),
             pltpu.VMEM((4, 4, 2, 128, 384), BF16),
@@ -692,7 +739,8 @@
             pltpu.VMEM((2, 8, 64, 128), BF16),
             pltpu.VMEM((3, 2, 2, 64, 384), BF16),
             pltpu.VMEM((3, 2, 2, 64, 384), BF16),
-            dma((7,)), dma((8,)), dma((8,)), dma((8,)), dma((8,)), dma((3,)),
+            dma((7,)), dma((4, 8)), dma((4, 8)), dma((8,)), dma((8,)), dma((3,)),
+            dma((9, 4)), dma((9, 4)),
             dma((2, 27)), dma((2, 27)), dma((2, 9)), dma((2, 9)), dma((2, 9)), dma((2, 9)),
             dma((4,)), dma((4,)), dma((4,)), dma((4,)), dma((4,)), dma((4,)),
             dma((4,)), dma((4,)), dma((2,)), dma((2,)), dma((4,)), dma((4,)),

time: 73.8 us -> 71 us (0.962)
  Pallas kernels: 72.1 us -> 69.3 us
    pallas_call x1, Pallas kernels: 72.1 us -> 69.3 us  [per_device(): pl.pallas_call(kernel, out_shape=jax.ShapeDtypeStruct((2, 2, 64, 384), BF...]
where the time goes in v4:
time: 71 us; the launch traced here: 70.9 us
  Pallas kernels  69.3 us (98%)
  local copies, waits for them, and re-layouts  1.62 us (2%)
    pallas_call x1, Pallas kernels, per_device(): pl.pallas_call(kernel, out_shape=jax.ShapeDtypeStruct((2, 2, 64, 384), BF...  69.3 us
    unnamed x1, local copies, waits for them, and re-layouts  1.62 us

profile of v4, /device:TPU:1, one launch (start us, length us, event | category | flops | bytes accessed | tf_op | source)
XLA Modules:
  0.0 70.9 jit_solution(4182552626569894146)
XLA Ops:
  0.0 69.3 %shard_map.73 = bf16[2,2,64,384]{3,2,1,0:T(8,128)(2,1)} custom-call(bf16[2,2,64,384]{3,2,1,0:T(8,128)(2,1)} %lat_hbm.1, f32[384]{0:T(512)} %gain1_hbm.1, f32[384]{0:T(512)} %bias1_hbm.1, f32[384]{0:T(512)} %gain2_hbm.1, f32[384]{0:T(512)} %bias2_hbm.1, bf16[27,6,384]{2,1,0:T(8,128)(2,1)} %bitcast.2, bf16[27,6,384]{2,1,0:T(8,128)(2,1)} %bitcast.3), custom_call_target="tpu_custom_call" | custom-call | flops 4000000000 | bytes 8000000 | tf_op jit(solution)/shard_map/pallas_call | solution.py:717
  69.3 1.6 %copy.9 = bf16[2,2,64,384]{3,2,1,0:T(8,128)(2,1)} copy(bf16[2,2,64,384]{3,2,1,0:T(8,128)(2,1)} %shard_map.73) | data formatting | bytes 393216

commit v5 on v4

v5 whole, which is shorter than its diff:
```python
import jax
import jax.numpy as jnp
from jax import lax
from jax.experimental import pallas as pl
from jax.experimental.pallas import tpu as pltpu
from jax.sharding import PartitionSpec as P

MESH = pl.DeviceIdType.MESH
F32 = jnp.float32
BF16 = jnp.bfloat16

SLOTS = ((0, 1), (0, 0), (0, 2), (2, 0), (1, 1), (1, 0), (1, 2), (2, 2), (2, 1))


def silu(u):
    return u / (1.0 + jnp.exp(-u))


def kernel(
    lat_hbm, gain1_hbm, bias1_hbm, gain2_hbm, bias2_hbm, k1_hbm, k2_hbm, out,
    lat, vec, k1, k2, s1, s2, stack,
    ruler, r1, r2, w1, w2, abuf, pbuf, hbuf, ssbuf, a2s, a2h, sendb, recvb,
    ins, st1s, st1r, st2s, st2r, loc,
    w1zs, w1zr, ysend, yrecv, rsend, rrecv, bsend, brecv,
    xs, xr, ups, upr, dns, dnr, sss, ssr, h2s, h2r, fs, fr,
):
    x = lax.axis_index("span")
    t = lax.axis_index("tile")
    c = lax.rem(t, 2)
    z = lax.rem(lax.div(t, 2), 8)
    y = lax.div(t, 16)
    zi = lax.rem(z, 4)
    h = lax.div(z, 4)
    j = lax.rem(t, 8)
    g = lax.div(t, 8)

    def dev(yy, zz, cc):
        return (x, yy * 16 + zz * 2 + cc)

    def rc(src, dst, ssem, rsem, device):
        return pltpu.make_async_remote_copy(
            src_ref=src, dst_ref=dst, send_sem=ssem, recv_sem=rsem,
            device_id=device, device_id_type=MESH,
        )

    def got(ref, rsem):
        rc(ref, ref, loc.at[2], rsem, (x, t)).wait_recv()

    def gone(rows, ssem):
        size = ruler.at[0:rows]
        rc(size, size, ssem, loc.at[2], (x, t)).wait_send()

    def came(rows, rsem):
        got(ruler.at[0:rows], rsem)

    loads = [
        pltpu.make_async_copy(k1_hbm, k1, ins.at[0]),
        pltpu.make_async_copy(lat_hbm, lat, ins.at[1]),
        pltpu.make_async_copy(k2_hbm, k2, ins.at[2]),
        pltpu.make_async_copy(gain1_hbm, vec.at[0], ins.at[3]),
        pltpu.make_async_copy(bias1_hbm, vec.at[1], ins.at[4]),
        pltpu.make_async_copy(gain2_hbm, vec.at[2], ins.at[5]),
        pltpu.make_async_copy(bias2_hbm, vec.at[3], ins.at[6]),
    ]
    for load in loads:
        load.start()

    barrier = pltpu.get_barrier_semaphore()

    def hail(device):
        pl.semaphore_signal(barrier, inc=1, device_id=device, device_id_type=MESH)

    for e in range(4):
        for d in range(8):
            if e or d:
                hail((x, lax.rem(y + e, 4) * 16 + h * 8 + lax.rem(j + d, 8)))

    @pl.when(x != y)
    def _():
        for d in range(8):
            hail((y, x * 16 + h * 8 + lax.rem(j + d, 8)))

    for d in range(1, 4):
        hail((lax.rem(x + d, 4), t))
    for d in (1, 2, 6, 7):
        hail(dev(y, lax.rem(z + d, 8), c))

    @pl.when(t > 0)
    def _():
        hail((x, t - 1))

    @pl.when(t < 63)
    def _():
        hail((x, t + 1))

    lane8 = lax.broadcasted_iota(jnp.int32, (8, 128), 1)
    turn = lax.rem(384 - 96 * x, 384)

    def mine96(v):
        return pltpu.roll(v, turn, 1)[:, 0:128]

    loads[0].wait()
    pad2 = jnp.zeros((2, 384), F32)
    tiles = []
    for dy in range(3):
        got_slots = []
        for dt, dx in SLOTS:
            got_slots.append(mine96(jnp.concatenate([k1[dt * 9 + dy * 3 + dx].astype(F32), pad2], axis=0)))

        def at(n, by):
            return pltpu.roll(got_slots[n], by, 1) if by else got_slots[n]

        row = [
            jnp.where(lane8 < 96, at(0, 0), at(1, 96)),
            jnp.where(lane8 < 64, at(1, 96), at(2, 64)),
            jnp.where(lane8 < 32, at(2, 64), at(3, 32)),
            jnp.where(lane8 < 96, at(4, 0), at(5, 96)),
            jnp.where(lane8 < 64, at(5, 96), at(6, 64)),
            jnp.where(lane8 < 32, at(6, 64), at(7, 32)),
            jnp.where(lane8 < 96, at(8, 0), 0.0),
            jnp.zeros((8, 128), F32),
        ]
        tiles.append(row)
    for n in range(8):
        s1[n, 0:16] = jnp.concatenate([tiles[0][n], tiles[1][n]], axis=0).astype(BF16)
        s1[n, 16:32] = jnp.concatenate([tiles[2][n], jnp.zeros((8, 128), F32)], axis=0).astype(BF16)
    loads[2].wait()
    for n in range(8):
        tap = jnp.minimum(8 * x + n, 26)
        s2[n] = jnp.concatenate([k2[tap].astype(F32), jnp.zeros((10, 384), F32)], axis=0).astype(BF16)
    for load in loads[3:]:
        load.wait()
    loads[1].wait()
    gain1 = vec[0:1]
    bias2 = vec[3:4]
    bias1 = jnp.where(lane8[0:1] < 96, mine96(jnp.broadcast_to(vec[1:2], (8, 384)))[0:1], 0.0)
    gain2 = jnp.where(lane8[0:1] < 96, mine96(jnp.broadcast_to(vec[2:3], (8, 384)))[0:1], 0.0)

    w1[1, 3] = jnp.zeros((3, 4, 2, 48, 128), BF16)
    w2[:, :, :, 96:128, :] = jnp.zeros((4, 4, 2, 32, 384), BF16)
    a2s[:, 0:2] = jnp.zeros((3, 2, 4, 64, 128), BF16)

    def zero_p(i, carry):
        pbuf[i, 0:2] = jnp.zeros((2, 2, 64, 256), F32)
        return carry

    lax.fori_loop(0, 4, zero_p, 0)

    def act1(i, carry):
        v = lat[i].reshape(128, 384).astype(F32)
        ms = jnp.mean(v * v, axis=-1, keepdims=True)
        u = v * lax.rsqrt(ms + 1e-6) * gain1
        abuf[x, i, 1:3] = silu(u).astype(BF16).reshape(2, 64, 384)
        return carry

    lax.fori_loop(0, 2, act1, 0)

    many = jnp.where(x != y, 8, 0) + jnp.where(t > 0, 1, 0) + jnp.where(t < 63, 1, 0) + 38
    pl.semaphore_wait(barrier, many)

    def st1(e, d):
        jj = lax.rem(j + d, 8)
        return rc(s1.at[jj], r1.at[y, j], st1s.at[0], st1r.at[e], (x, lax.rem(y + e, 4) * 16 + h * 8 + jj))

    def st2(d):
        jj = lax.rem(j + d, 8)
        return rc(s2.at[jj], r2.at[j], st2s.at[0], st2r.at[0], (y, x * 16 + h * 8 + jj))

    def own2():
        return pltpu.make_async_copy(s2.at[j], r2.at[j], loc.at[1])

    for e in (2, 1, 3, 0):
        for d in range(8):
            if e or d:

                @pl.when(lax.rem(j + d, 8) != 7)
                def _():
                    st1(e, d).start()

    own1 = pltpu.make_async_copy(s1.at[j], r1.at[y, j], loc.at[0])
    own1.start()

    def xsend(d):
        return rc(
            abuf.at[x, :, 1:3], abuf.at[x, :, 1:3], xs.at[0], xr.at[d], (lax.rem(x + d, 4), t)
        )

    def up(src, d):
        return rc(abuf.at[src, :, 1], abuf.at[src, :, 3], ups.at[0], upr.at[0], (x, t - 1))

    def down(src, d):
        return rc(abuf.at[src, :, 2], abuf.at[src, :, 0], dns.at[0], dnr.at[0], (x, t + 1))

    def halo_send(d):
        src = lax.rem(x + 4 - d, 4)

        @pl.when(t > 0)
        def _():
            up(src, d).start()

        @pl.when(t < 63)
        def _():
            down(src, d).start()

    def xstep(d):
        src = lax.rem(x + 4 - d, 4)
        land = abuf.at[src, :, 1:3]
        got(land, xr.at[d])
        halo_send(d)

    def halo_wait():
        @pl.when(t > 0)
        def _():
            came(4 * 384, dnr.at[0])

        @pl.when(t < 63)
        def _():
            came(4 * 384, upr.at[0])

        @pl.when(t == 0)
        def _():
            abuf[:, :, 0] = jnp.zeros((4, 2, 64, 384), BF16)

        @pl.when(t == 63)
        def _():
            abuf[:, :, 3] = jnp.zeros((4, 2, 64, 384), BF16)

    for d in range(8):
        if d == 0:

            @pl.when(x != y)
            def _():
                st2(0).start()

            @pl.when(x == y)
            def _():
                own2().start()
        else:
            st2(d).start()
    for d in (2, 1, 3):
        xsend(d).start()
    halo_send(0)

    def blk(k, yy, zz, cc):
        if k == 0:
            return w1.at[cc, lax.rem(zz, 4), :, yy, lax.div(zz, 4)]
        return w2.at[yy, lax.rem(zz, 4), cc, pl.ds(pl.multiple_of(48 * lax.div(zz, 4), 16), 48), :]

    def zset(zz):
        return w1.at[1, lax.rem(zz, 4), :, :, lax.div(zz, 4)]

    def zz(s):
        return lax.rem(z + 8 + s, 8)

    WAY = {1: 0, -1: 1, 2: 2, -2: 3, 3: 4, -3: 5, 4: 6, -4: 7, 0: 8}
    AROUND = (2, -2, 1, -1)
    B_RELAYS = {2: ((-2, 4), (-2, 3)), -2: ((2, -3),)}

    def yy_of(e):
        return lax.rem(y + e, 4)

    def zi_of(origin):
        return lax.rem(z + 8 + origin, 4)

    def when_a(origin, f):
        @pl.when(jnp.logical_and(c == 1, zi_of(origin) == 0))
        def _():
            f()

    def when_b(origin, f):
        k = zi_of(origin)

        @pl.when(jnp.logical_or(c == 0, jnp.logical_or(k == 1, k == 2)))
        def _():
            f()

    def on_core(core, f):
        @pl.when(c == core)
        def _():
            f()

    def a_z(e, origin, total):
        ref = blk(0, yy_of(e), zz(origin), 1)
        i = WAY[total]
        k = 9 + 4 * (i - 2) + e if total in (2, -2) else i
        return rc(ref, ref, w1zs.at[0], w1zr.at[k], dev(y, zz(origin + total), 1))

    def a_got(e, total):
        got(blk(0, yy_of(e), zz(-total), 1), w1zr.at[9 + 4 * (WAY[total] - 2) + e])

    def a_relays(e, total):
        if total == 2:
            return ((-2, 3), (-2, 4)) if e < 2 else ((-2, 3),)
        return ((2, -3), (2, -4)) if e >= 2 else ((2, -3),)

    def a_sib(s):
        ref = zset(zz(s))
        return rc(ref, ref, bsend.at[0], brecv.at[0], dev(y, z, 0))

    def b_z(origin, total):
        ref = blk(0, y, zz(origin), c)
        i = WAY[total]
        return rc(ref, ref, w1zs.at[0], w1zr.at[i], dev(y, zz(origin + total), c))

    def b_got(total):
        got(blk(0, y, zz(-total), c), w1zr.at[WAY[total]])

    def b_y(d, s):
        ref = blk(0, y, zz(s), c)
        return rc(ref, ref, ysend.at[0], yrecv.at[d - 1], dev(lax.rem(y + d, 4), z, c))

    def b_sib(core, d):
        yy = lax.rem(y + d, 4)
        ref = w1.at[0, :, :, yy] if core == 0 else w1.at[1, 1:3, :, yy]
        return rc(ref, ref, bsend.at[0], brecv.at[0], dev(y, z, 1 - core))

    def first(e):
        def send_a():
            for total in AROUND:
                a_z(e, 0, total).start()

        when_a(0, send_a)
        if e == 0:

            def send_b():
                for total in AROUND:
                    b_z(0, total).start()

            when_b(0, send_b)

    def y_all(origin):
        for d in (2, 1, 3):
            b_y(d, origin).start()

    def step(n):
        if n == 1:
            for total in (2, -2):

                def relay(total=total):
                    for e in (0, 1, 3, 2):
                        a_got(e, total)
                        for origin, far in a_relays(e, total):
                            a_z(e, origin, far).start()
                    a_sib(-total).start()

                def take(total=total):
                    b_got(total)
                    for origin, far in B_RELAYS[total]:
                        b_z(origin, far).start()
                    y_all(-total)

                when_a(-total, relay)
                when_b(-total, take)
            when_a(0, lambda: a_sib(0).start())
        if n == 2 or n == 3:
            for total in ((1, -1) if n == 2 else (3, -3)):

                def whole(total=total):
                    came(4 * 144, w1zr.at[WAY[total]])
                    a_sib(-total).start()

                def take(total=total):
                    b_got(total)
                    y_all(-total)

                when_a(-total, whole)
                when_b(-total, take)
        if n == 3:

            def last():
                came(2 * 144, w1zr.at[WAY[4]])
                came(2 * 144, w1zr.at[WAY[-4]])
                a_sib(4).start()

            def take4():
                b_got(4)
                y_all(4)

            when_a(4, last)
            when_b(4, take4)
            for core in range(2):
                on_core(core, lambda core=core: b_sib(core, 0).start())
        if n == 4:

            def arrived(core, count):
                for d in (1, 3, 2):
                    came(count * 144, yrecv.at[d - 1])
                    b_sib(core, 4 - d).start()

            on_core(0, lambda: arrived(0, 7))
            own_b = jnp.logical_or(zi == 1, zi == 2)

            @pl.when(jnp.logical_and(c == 1, own_b))
            def _():
                arrived(1, 3)

            @pl.when(jnp.logical_and(c == 1, jnp.logical_not(own_b)))
            def _():
                arrived(1, 4)
        if n == 5:
            on_core(0, lambda: came(24 * 144, brecv.at[0]))
            on_core(1, lambda: came(32 * 144, brecv.at[0]))

    def step_sent():
        def core0():
            gone(7 * 144, w1zs.at[0])
            gone(21 * 144, ysend.at[0])
            gone(32 * 144, bsend.at[0])

        on_core(0, core0)
        for k, (along_z, along_y) in enumerate(((19, 12), (4, 9), (16, 9), (3, 12))):

            @pl.when(jnp.logical_and(c == 1, zi == k))
            def _():
                gone(along_z * 144, w1zs.at[0])
                gone(along_y * 144, ysend.at[0])

        on_core(1, lambda: gone(24 * 144, bsend.at[0]))

    def wset(yy, cc):
        return w2.at[yy, :, cc, 0:96, :]

    def z2_send(origin, total):
        ref = blk(1, y, zz(origin), c)
        i = WAY[total]
        return rc(ref, ref, rsend.at[0], rrecv.at[i], dev(y, zz(origin + total), c))

    def z2_got(total):
        got(blk(1, y, zz(-total), c), rrecv.at[WAY[total]])

    def y2_send(d):
        ref = wset(y, c)
        return rc(ref, ref, ysend.at[1], yrecv.at[2 + d], dev(lax.rem(y + d, 4), z, c))

    def sib2_send(d):
        ref = wset(lax.rem(y + d, 4), c)
        return rc(ref, ref, bsend.at[1], brecv.at[1], dev(y, z, 1 - c))

    Z2 = ((0, 2), (0, -2), (0, 1), (0, -1), (-2, 4), (-2, 3), (2, -3))

    def step2(n):
        if n == 0:
            for origin, total in Z2[:4]:
                z2_send(origin, total).start()
        if n == 1:
            z2_got(2)
            z2_send(-2, 4).start()
            z2_send(-2, 3).start()
            z2_got(-2)
            z2_send(2, -3).start()
        if n == 2:
            for total in (1, -1, 3, -3, 4):
                z2_got(total)
            for d in (2, 1, 3):
                y2_send(d).start()
            sib2_send(0).start()
        if n == 3:
            for d in (1, 3, 2):
                got(wset(lax.rem(y + 4 - d, 4), c), yrecv.at[2 + d])
                sib2_send(4 - d).start()
        if n == 4:
            came(32 * 144, brecv.at[1])

    def step2_sent():
        gone(7 * 144, rsend.at[0])
        gone(24 * 144, ysend.at[1])
        gone(32 * 144, bsend.at[1])

    own1.wait()
    for e in (0, 1, 3, 2):
        src = lax.rem(y + e, 4)

        @pl.when(j != 7)
        def _():
            came(8 * 32 if e else 7 * 32, st1r.at[(4 - e) % 4])
            for dy in range(3):
                for m in range(8):
                    two = r1[src, m, 16 * (dy // 2):16 * (dy // 2) + 16].astype(F32)
                    stack[m * 6:m * 6 + 6, 0:128] = two[(dy % 2) * 8:(dy % 2) * 8 + 6]
                w1[c, zi, dy, src, h] = stack[:, 0:128].astype(BF16)

        first(e)
    @pl.when(x != y)
    def _():
        came(8 * 48, st2r.at[0])

    @pl.when(x == y)
    def _():
        own2().wait()
        came(7 * 48, st2r.at[0])

    for m in range(8):
        stack[m * 6:m * 6 + 6] = r2[m].astype(F32)[0:6]
    w2[y, zi, c, pl.ds(pl.multiple_of(48 * h, 16), 48), :] = stack[...].astype(BF16)
    step2(0)
    step(1)
    step(2)
    xstep(1)
    xstep(3)
    step2(1)
    step(3)
    xstep(2)
    step2(2)
    step(4)
    halo_wait()
    step(5)

    def conv1():
        rows = []
        for yy in range(2):
            rows.append(jnp.concatenate(
                [abuf[:, :, yy + dy].reshape(512, 384) for dy in range(3)], axis=1))
        lhs = jnp.concatenate(rows, axis=0)

        def tile(n, carry):
            rhs = jnp.concatenate(
                [w1[0, n].reshape(1152, 128), w1[1, n].reshape(1152, 128)], axis=1)
            res = jnp.dot(lhs, rhs, preferred_element_type=F32)
            for yy in range(2):
                pbuf[n, 2:10, yy] = res[yy * 512:yy * 512 + 512].reshape(8, 64, 256)
            return carry

        lax.fori_loop(0, 4, tile, 0)

    conv1()

    lane = lax.broadcasted_iota(jnp.int32, (64, 128), 1)
    row = lax.broadcasted_iota(jnp.int32, (64, 128), 0)

    def shift_down(v):
        return jnp.where(row > 0, pltpu.roll(v, 1, 0), 0.0)

    def shift_up(v):
        return jnp.where(row < 63, pltpu.roll(v, 63, 0), 0.0)

    def combine(f, carry):
        both = []
        for yy in range(2):
            def p(dt, n):
                return pbuf[n // 2, f + dt, yy, :, (n % 2) * 128:(n % 2) * 128 + 128]

            m1 = p(0, 0) + p(1, 3) + p(2, 6)
            a_lo = p(0, 0) + p(1, 3)
            mid = p(0, 1) + p(1, 4)
            b_hi = p(0, 2) + p(1, 5)
            m0 = pltpu.roll(jnp.where(lane >= 96, a_lo, mid), 32, 1) + pltpu.roll(p(2, 2), 96, 1)
            m2 = pltpu.roll(jnp.where(lane >= 64, mid, b_hi), 64, 1) + pltpu.roll(p(2, 5), 96, 1)
            hid = m1 + shift_down(m0) + shift_up(m2) + bias1
            hid = jnp.where(lane < 96, hid, 0.0)
            hbuf[f, yy] = hid
            both.append(hid * hid)
        sums = jnp.sum(jnp.transpose(jnp.concatenate(both, axis=0)), axis=0, keepdims=True)
        ssbuf[0, pl.ds(f, 1)] = sums
        return carry

    lax.fori_loop(0, 8, combine, 0, unroll=2)

    def ss_send(d):
        return rc(ssbuf.at[0], ssbuf.at[d], sss.at[0], ssr.at[0], (lax.rem(x + d, 4), t))

    for d in range(1, 4):
        ss_send(d).start()
    sizes = ssbuf.at[1:4]
    got(sizes, ssr.at[0])
    ssbuf[4] = (ssbuf[0] + ssbuf[1]) + (ssbuf[2] + ssbuf[3])

    def spread(f, where, v):
        a2s[0, f + 2, where] = shift_down(v).astype(BF16)
        a2s[1, f + 2, where] = v.astype(BF16)
        a2s[2, f + 2, where] = shift_up(v).astype(BF16)

    def act2(f, carry):
        ms = jnp.transpose(jnp.broadcast_to(ssbuf[4, pl.ds(f, 1)], (128, 128))) * (1.0 / 384.0)
        u = hbuf[f].reshape(128, 128) * lax.rsqrt(ms + 1e-6) * gain2
        v = silu(u)
        for yy in range(2):
            spread(f, 1 + yy, v[64 * yy:64 * yy + 64])
        return carry

    lax.fori_loop(0, 8, act2, 0, unroll=2)

    def h2up():
        return rc(a2s.at[1, 2:10, 1], a2h.at[1], h2s.at[0], h2r.at[0], (x, t - 1))

    def h2down():
        return rc(a2s.at[1, 2:10, 2], a2h.at[0], h2s.at[1], h2r.at[1], (x, t + 1))

    @pl.when(t > 0)
    def _():
        h2up().start()

    @pl.when(t < 63)
    def _():
        h2down().start()

    step2(3)
    step2(4)

    @pl.when(t > 0)
    def _():
        got(a2h.at[0], h2r.at[1])

    @pl.when(t == 0)
    def _():
        a2h[0] = jnp.zeros((8, 64, 128), BF16)

    @pl.when(t < 63)
    def _():
        got(a2h.at[1], h2r.at[0])

    @pl.when(t == 63)
    def _():
        a2h[1] = jnp.zeros((8, 64, 128), BF16)

    def halo2(f, carry):
        spread(f, 0, a2h[0, f].astype(F32))
        spread(f, 3, a2h[1, f].astype(F32))
        return carry

    lax.fori_loop(0, 8, halo2, 0)

    def conv2(q):
        acc = None
        for dt in range(3):
            lhs, rhs = [], []
            for dy in range(3):
                for dx in range(3):
                    tap = dt * 9 + dy * 3 + dx
                    lhs.append(a2s[dx, pl.ds(2 * q + dt, 2), dy:dy + 2].reshape(256, 128))
                    rhs.append(w2[tap // 8, (tap % 8) // 2, tap % 2])
            part = jnp.dot(
                jnp.concatenate(lhs, axis=1), jnp.concatenate(rhs, axis=0),
                preferred_element_type=F32,
            )
            acc = part if acc is None else acc + part
        return acc

    def out_send(d):
        return rc(sendb.at[d - 1], recvb.at[d - 1], fs.at[0], fr.at[d], (lax.rem(x + d, 4), t))

    for d in (2, 1, 3):
        sendb[d - 1] = conv2(lax.rem(x + d, 4)).astype(BF16).reshape(2, 2, 64, 384)
        out_send(d).start()
    mine = conv2(x) + bias2 + lat[...].reshape(256, 384).astype(F32)
    for d in (2, 1, 3):
        got(recvb.at[d - 1], fr.at[d])
        mine = mine + recvb[d - 1].reshape(256, 384).astype(F32)
    out[...] = mine.astype(BF16).reshape(2, 2, 64, 384)

    @pl.when(j == 7)
    def _():
        gone(28 * 32, st1s.at[0])

    @pl.when(j != 7)
    def _():
        gone(27 * 32, st1s.at[0])

    @pl.when(x != y)
    def _():
        gone(8 * 48, st2s.at[0])

    @pl.when(x == y)
    def _():
        gone(7 * 48, st2s.at[0])

    gone(3 * 768, xs.at[0])
    rc(ssbuf.at[1:4], ssbuf.at[1:4], sss.at[0], loc.at[2], (x, t)).wait_send()
    gone(3 * 768, fs.at[0])

    @pl.when(t > 0)
    def _():
        gone(4 * 384, ups.at[0])
        h2up().wait_send()

    @pl.when(t < 63)
    def _():
        gone(4 * 384, dns.at[0])
        h2down().wait_send()

    step2_sent()

    step_sent()


def per_device(latents, gain_first, conv_first, bias_first, gain_second, conv_second, bias_second):
    vm = pl.BlockSpec(memory_space=pltpu.VMEM)
    dma = pltpu.SemaphoreType.DMA
    return pl.pallas_call(
        kernel,
        out_shape=jax.ShapeDtypeStruct((2, 2, 64, 384), BF16),
        in_specs=[pl.BlockSpec(memory_space=pltpu.HBM)] * 7,
        out_specs=vm,
        scratch_shapes=[
            pltpu.VMEM((2, 2, 64, 384), BF16),
            pltpu.VMEM((4, 384), F32),
            pltpu.VMEM((27, 6, 384), BF16),
            pltpu.VMEM((27, 6, 384), BF16),
            pltpu.VMEM((8, 32, 128), BF16),
            pltpu.VMEM((8, 16, 384), BF16),
            pltpu.VMEM((48, 384), F32),
            pltpu.VMEM((4608, 128), BF16),
            pltpu.VMEM((4, 8, 32, 128), BF16),
            pltpu.VMEM((8, 16, 384), BF16),
            pltpu.VMEM((2, 4, 3, 4, 2, 48, 128), BF16),
            pltpu.VMEM((4, 4, 2, 128, 384), BF16),
            pltpu.VMEM((4, 2, 4, 64, 384), BF16),
            pltpu.VMEM((4, 10, 2, 64, 256), F32),
            pltpu.VMEM((8, 2, 64, 128), F32),
            pltpu.VMEM((5, 8, 128), F32),
            pltpu.VMEM((3, 10, 4, 64, 128), BF16),
            pltpu.VMEM((2, 8, 64, 128), BF16),
            pltpu.VMEM((3, 2, 2, 64, 384), BF16),
            pltpu.VMEM((3, 2, 2, 64, 384), BF16),
            dma((7,)), dma((1,)), dma((4,)), dma((1,)), dma((1,)), dma((3,)),
            dma((1,)), dma((17,)), dma((2,)), dma((6,)), dma((1,)), dma((9,)), dma((2,)), dma((2,)),
            dma((1,)), dma((4,)), dma((1,)), dma((1,)), dma((1,)), dma((1,)),
            dma((1,)), dma((1,)), dma((2,)), dma((2,)), dma((1,)), dma((4,)),
        ],
        compiler_params=pltpu.CompilerParams(
            collective_id=0, has_side_effects=True, vmem_limit_bytes=63 * 1024 * 1024
        ),
        cost_estimate=pl.CostEstimate(flops=4_000_000_000, bytes_accessed=8_000_000, transcendentals=400_000),
    )(
        latents, gain_first, bias_first, gain_second, bias_second,
        conv_first.reshape(27, 6, 384), conv_second.reshape(27, 6, 384),
    )


def solution(mesh):
    in_specs = (
        P("span", "tile", None, None),
        P(),
        P(None, None, None, "tile", None),
        P(),
        P(),
        P(None, None, None, "tile", None),
        P(),
    )
    out_specs = P("span", "tile", None, None)
    return jax.shard_map(
        per_device, mesh=mesh, in_specs=in_specs, out_specs=out_specs, check_vma=False
    )
```

time: 71 us -> 67.8 us (0.955); the launches traced: 70.9 us -> 66.4 us
  Pallas kernels: 69.3 us -> 64.8 us
    pallas_call x1, Pallas kernels: 69.3 us -> 64.8 us  [per_device(): pl.pallas_call(kernel, out_shape=jax.ShapeDtypeStruct((2, 2, 64, 384), BF...]
where the time goes in v5:
time: 67.8 us; the launch traced here: 66.4 us
  Pallas kernels  64.8 us (96%)
  local copies, waits for them, and re-layouts  1.62 us (2%)
    pallas_call x1, Pallas kernels, per_device(): pl.pallas_call(kernel, out_shape=jax.ShapeDtypeStruct((2, 2, 64, 384), BF...  64.8 us
    unnamed x1, local copies, waits for them, and re-layouts  1.62 us

profile of v5, /device:TPU:1, one launch (start us, length us, event | category | flops | bytes accessed | tf_op | source)
XLA Modules:
  0.0 66.4 jit_solution(12543180734110897175)
XLA Ops:
  0.0 64.8 %shard_map.73 = bf16[2,2,64,384]{3,2,1,0:T(8,128)(2,1)} custom-call(bf16[2,2,64,384]{3,2,1,0:T(8,128)(2,1)} %lat_hbm.1, f32[384]{0:T(512)} %gain1_hbm.1, f32[384]{0:T(512)} %bias1_hbm.1, f32[384]{0:T(512)} %gain2_hbm.1, f32[384]{0:T(512)} %bias2_hbm.1, bf16[27,6,384]{2,1,0:T(8,128)(2,1)} %bitcast.2, bf16[27,6,384]{2,1,0:T(8,128)(2,1)} %bitcast.3), custom_call_target="tpu_custom_call" | custom-call | flops 4000000000 | bytes 8000000 | tf_op jit(solution)/shard_map/pallas_call | solution.py:688
  64.8 1.6 %copy.9 = bf16[2,2,64,384]{3,2,1,0:T(8,128)(2,1)} copy(bf16[2,2,64,384]{3,2,1,0:T(8,128)(2,1)} %shard_map.73) | data formatting | bytes 393216

commit v6 on v5

--- a/solution.py
+++ b/solution.py
@@ -9,6 +9,8 @@
 F32 = jnp.float32
 BF16 = jnp.bfloat16
 
+WHOLE = 1
+
 SLOTS = ((0, 1), (0, 0), (0, 2), (2, 0), (1, 1), (1, 0), (1, 2), (2, 2), (2, 1))
 
 
@@ -19,7 +21,7 @@
 def kernel(
     lat_hbm, gain1_hbm, bias1_hbm, gain2_hbm, bias2_hbm, k1_hbm, k2_hbm, out,
     lat, vec, k1, k2, s1, s2, stack,
-    ruler, r1, r2, w1, w2, abuf, pbuf, hbuf, ssbuf, a2s, a2h, sendb, recvb,
+    ruler, r1, r2, w1, w2, abuf, pbuf, hbuf, hedge, ssbuf, a2s, a2h, sendb, recvb,
     ins, st1s, st1r, st2s, st2r, loc,
     w1zs, w1zr, ysend, yrecv, rsend, rrecv, bsend, brecv,
     xs, xr, ups, upr, dns, dnr, sss, ssr, h2s, h2r, fs, fr,
@@ -87,11 +89,13 @@
 
     @pl.when(t > 0)
     def _():
-        hail((x, t - 1))
+        for d in range(4):
+            hail((lax.rem(x + d, 4), t - 1))
 
     @pl.when(t < 63)
     def _():
-        hail((x, t + 1))
+        for d in range(4):
+            hail((lax.rem(x + d, 4), t + 1))
 
     lane8 = lax.broadcasted_iota(jnp.int32, (8, 128), 1)
     turn = lax.rem(384 - 96 * x, 384)
@@ -155,7 +159,7 @@
 
     lax.fori_loop(0, 2, act1, 0)
 
-    many = jnp.where(x != y, 8, 0) + jnp.where(t > 0, 1, 0) + jnp.where(t < 63, 1, 0) + 38
+    many = jnp.where(x != y, 8, 0) + jnp.where(t > 0, 4, 0) + jnp.where(t < 63, 4, 0) + 38
     pl.semaphore_wait(barrier, many)
 
     def st1(e, d):
@@ -169,13 +173,14 @@
     def own2():
         return pltpu.make_async_copy(s2.at[j], r2.at[j], loc.at[1])
 
-    for e in (2, 1, 3, 0):
-        for d in range(8):
-            if e or d:
-
-                @pl.when(lax.rem(j + d, 8) != 7)
-                def _():
-                    st1(e, d).start()
+    for e in (2, 1, 3):
+        for k in range(WHOLE):
+            st1(e, lax.rem(9 + 2 * k - j, 8)).start()
+    for d in range(1, 8):
+
+        @pl.when(lax.rem(j + d, 8) != 7)
+        def _():
+            st1(0, d).start()
 
     own1 = pltpu.make_async_copy(s1.at[j], r1.at[y, j], loc.at[0])
     own1.start()
@@ -263,14 +268,14 @@
         return lax.rem(z + 8 + origin, 4)
 
     def when_a(origin, f):
-        @pl.when(jnp.logical_and(c == 1, zi_of(origin) == 0))
+        @pl.when(jnp.logical_and(c == 1, zi_of(origin) < WHOLE))
         def _():
             f()
 
     def when_b(origin, f):
         k = zi_of(origin)
 
-        @pl.when(jnp.logical_or(c == 0, jnp.logical_or(k == 1, k == 2)))
+        @pl.when(jnp.logical_or(c == 0, jnp.logical_and(k >= WHOLE, k <= 2)))
         def _():
             f()
 
@@ -305,14 +310,20 @@
     def b_got(total):
         got(blk(0, y, zz(-total), c), w1zr.at[WAY[total]])
 
+    UP = (0, -2, 1, 3)
+
     def b_y(d, s):
         ref = blk(0, y, zz(s), c)
-        return rc(ref, ref, ysend.at[0], yrecv.at[d - 1], dev(lax.rem(y + d, 4), z, c))
+        return rc(ref, ref, ysend.at[0], yrecv.at[0, d - 1], dev(yy_of(d), z, c))
 
     def b_sib(core, d):
         yy = lax.rem(y + d, 4)
-        ref = w1.at[0, :, :, yy] if core == 0 else w1.at[1, 1:3, :, yy]
+        ref = w1.at[0, :, :, yy] if core == 0 else w1.at[1, WHOLE:3, :, yy]
         return rc(ref, ref, bsend.at[0], brecv.at[0], dev(y, z, 1 - core))
+
+    def y_all(origin):
+        for d in (2, 1, 3):
+            b_y(d, origin).start()
 
     def first(e):
         def send_a():
@@ -325,12 +336,9 @@
             def send_b():
                 for total in AROUND:
                     b_z(0, total).start()
+                y_all(0)
 
             when_b(0, send_b)
-
-    def y_all(origin):
-        for d in (2, 1, 3):
-            b_y(d, origin).start()
 
     def step(n):
         if n == 1:
@@ -378,25 +386,19 @@
 
             when_a(4, last)
             when_b(4, take4)
-            for core in range(2):
-                on_core(core, lambda core=core: b_sib(core, 0).start())
+            on_core(0, lambda: b_sib(0, 0).start())
+            if WHOLE < 3:
+                on_core(1, lambda: b_sib(1, 0).start())
         if n == 4:
 
             def arrived(core, count):
-                for d in (1, 3, 2):
-                    came(count * 144, yrecv.at[d - 1])
-                    b_sib(core, 4 - d).start()
-
-            on_core(0, lambda: arrived(0, 7))
-            own_b = jnp.logical_or(zi == 1, zi == 2)
-
-            @pl.when(jnp.logical_and(c == 1, own_b))
-            def _():
-                arrived(1, 3)
-
-            @pl.when(jnp.logical_and(c == 1, jnp.logical_not(own_b)))
-            def _():
-                arrived(1, 4)
+                if count:
+                    for d in (1, 3, 2):
+                        came(count * 144, yrecv.at[0, d - 1])
+                        b_sib(core, 4 - d).start()
+
+            on_core(0, lambda: arrived(0, 8))
+            on_core(1, lambda: arrived(1, 2 * (3 - WHOLE)))
         if n == 5:
             on_core(0, lambda: came(24 * 144, brecv.at[0]))
             on_core(1, lambda: came(32 * 144, brecv.at[0]))
@@ -404,16 +406,22 @@
     def step_sent():
         def core0():
             gone(7 * 144, w1zs.at[0])
-            gone(21 * 144, ysend.at[0])
+            gone(24 * 144, ysend.at[0])
             gone(32 * 144, bsend.at[0])
 
         on_core(0, core0)
-        for k, (along_z, along_y) in enumerate(((19, 12), (4, 9), (16, 9), (3, 12))):
+        def sends(k, whole, block):
+            return 0 if k == 3 else whole if k < WHOLE else block
+
+        for k in range(4):
+            along_z = sends(k, 16, 4) + sends((k + 2) % 4, 12, 3)
+            along_y = 6 * (3 - WHOLE)
 
             @pl.when(jnp.logical_and(c == 1, zi == k))
             def _():
                 gone(along_z * 144, w1zs.at[0])
-                gone(along_y * 144, ysend.at[0])
+                if along_y:
+                    gone(along_y * 144, ysend.at[0])
 
         on_core(1, lambda: gone(24 * 144, bsend.at[0]))
 
@@ -428,9 +436,23 @@
     def z2_got(total):
         got(blk(1, y, zz(-total), c), rrecv.at[WAY[total]])
 
-    def y2_send(d):
-        ref = wset(y, c)
-        return rc(ref, ref, ysend.at[1], yrecv.at[2 + d], dev(lax.rem(y + d, 4), z, c))
+    def y2_one(d, origin, step):
+        ref = blk(1, yy_of(4 + origin), zz(step), c)
+        k = 18 if origin else WAY[step] + 9 * (d // 2)
+        return rc(ref, ref, ysend.at[1], yrecv.at[1, k], dev(yy_of(d), z, c))
+
+    def y2_send(origin):
+        for d in (1, 3):
+            y2_one(d, 0, origin).start()
+
+    def y2_relay(*steps):
+        for k in steps:
+            got(blk(1, yy_of(3), zz(k), c), yrecv.at[1, WAY[k]])
+            if k in UP:
+                y2_one(1, -1, k).start()
+            got(blk(1, yy_of(1), zz(k), c), yrecv.at[1, WAY[k] + 9])
+            if k not in UP:
+                y2_one(3, 1, k).start()
 
     def sib2_send(d):
         ref = wset(lax.rem(y + d, 4), c)
@@ -449,15 +471,15 @@
             z2_got(-2)
             z2_send(2, -3).start()
         if n == 2:
-            for total in (1, -1, 3, -3, 4):
+            for origin in (0, 2, -2):
+                y2_send(origin)
+            for total, origin in ((1, -1), (-1, 1), (3, -3), (-3, 3), (4, 4)):
                 z2_got(total)
-            for d in (2, 1, 3):
-                y2_send(d).start()
+                y2_send(origin)
             sib2_send(0).start()
         if n == 3:
-            for d in (1, 3, 2):
-                got(wset(lax.rem(y + 4 - d, 4), c), yrecv.at[2 + d])
-                sib2_send(4 - d).start()
+            came(8 * 144, yrecv.at[1, 18])
+            sib2_send(2).start()
         if n == 4:
             came(32 * 144, brecv.at[1])
 
@@ -470,7 +492,7 @@
     for e in (0, 1, 3, 2):
         src = lax.rem(y + e, 4)
 
-        @pl.when(j != 7)
+        @pl.when(jnp.logical_and(c == 1, zi < WHOLE) if e else j != 7)
         def _():
             came(8 * 32 if e else 7 * 32, st1r.at[(4 - e) % 4])
             for dy in range(3):
@@ -480,6 +502,7 @@
                 w1[c, zi, dy, src, h] = stack[:, 0:128].astype(BF16)
 
         first(e)
+    step(1)
     @pl.when(x != y)
     def _():
         came(8 * 48, st2r.at[0])
@@ -493,11 +516,10 @@
         stack[m * 6:m * 6 + 6] = r2[m].astype(F32)[0:6]
     w2[y, zi, c, pl.ds(pl.multiple_of(48 * h, 16), 48), :] = stack[...].astype(BF16)
     step2(0)
-    step(1)
     step(2)
+    step2(1)
     xstep(1)
     xstep(3)
-    step2(1)
     step(3)
     xstep(2)
     step2(2)
@@ -520,9 +542,16 @@
                 pbuf[n, 2:10, yy] = res[yy * 512:yy * 512 + 512].reshape(8, 64, 256)
             return carry
 
-        lax.fori_loop(0, 4, tile, 0)
+        tile(0, 0)
+        tile(1, 0)
+        y2_relay(0, 2, -2)
+        tile(2, 0)
+        tile(3, 0)
 
     conv1()
+    y2_relay(1, -1, 3, -3, 4)
+    sib2_send(1).start()
+    sib2_send(3).start()
 
     lane = lax.broadcasted_iota(jnp.int32, (64, 128), 1)
     row = lax.broadcasted_iota(jnp.int32, (64, 128), 0)
@@ -548,6 +577,7 @@
             hid = m1 + shift_down(m0) + shift_up(m2) + bias1
             hid = jnp.where(lane < 96, hid, 0.0)
             hbuf[f, yy] = hid
+            hedge[f, yy] = hid.astype(BF16)
             both.append(hid * hid)
         sums = jnp.sum(jnp.transpose(jnp.concatenate(both, axis=0)), axis=0, keepdims=True)
         ssbuf[0, pl.ds(f, 1)] = sums
@@ -558,11 +588,47 @@
     def ss_send(d):
         return rc(ssbuf.at[0], ssbuf.at[d], sss.at[0], ssr.at[0], (lax.rem(x + d, 4), t))
 
-    for d in range(1, 4):
+    def ss_up(d):
+        return rc(ssbuf.at[0], ssbuf.at[8 + d], sss.at[1], ssr.at[2], (lax.rem(x + d, 4), t - 1))
+
+    def ss_down(d):
+        return rc(ssbuf.at[0], ssbuf.at[4 + d], sss.at[2], ssr.at[1], (lax.rem(x + d, 4), t + 1))
+
+    def h2up():
+        return rc(hedge.at[:, 0], a2h.at[1], h2s.at[0], h2r.at[0], (x, t - 1))
+
+    def h2down():
+        return rc(hedge.at[:, 1], a2h.at[0], h2s.at[1], h2r.at[1], (x, t + 1))
+
+    for d in (2, 1, 3):
         ss_send(d).start()
+
+    @pl.when(t > 0)
+    def _():
+        for d in (2, 1, 3, 0):
+            ss_up(d).start()
+        h2up().start()
+
+    @pl.when(t < 63)
+    def _():
+        for d in (2, 1, 3, 0):
+            ss_down(d).start()
+        h2down().start()
+
+    @pl.when(t == 0)
+    def _():
+        a2h[0] = jnp.zeros((8, 64, 128), BF16)
+        ssbuf[4:8] = jnp.zeros((4, 8, 128), F32)
+
+    @pl.when(t == 63)
+    def _():
+        a2h[1] = jnp.zeros((8, 64, 128), BF16)
+        ssbuf[8:12] = jnp.zeros((4, 8, 128), F32)
+
+    step2(3)
     sizes = ssbuf.at[1:4]
     got(sizes, ssr.at[0])
-    ssbuf[4] = (ssbuf[0] + ssbuf[1]) + (ssbuf[2] + ssbuf[3])
+    ssbuf[12] = (ssbuf[0] + ssbuf[1]) + (ssbuf[2] + ssbuf[3])
 
     def spread(f, where, v):
         a2s[0, f + 2, where] = shift_down(v).astype(BF16)
@@ -570,7 +636,7 @@
         a2s[2, f + 2, where] = shift_up(v).astype(BF16)
 
     def act2(f, carry):
-        ms = jnp.transpose(jnp.broadcast_to(ssbuf[4, pl.ds(f, 1)], (128, 128))) * (1.0 / 384.0)
+        ms = jnp.transpose(jnp.broadcast_to(ssbuf[12, pl.ds(f, 1)], (128, 128))) * (1.0 / 384.0)
         u = hbuf[f].reshape(128, 128) * lax.rsqrt(ms + 1e-6) * gain2
         v = silu(u)
         for yy in range(2):
@@ -579,45 +645,30 @@
 
     lax.fori_loop(0, 8, act2, 0, unroll=2)
 
-    def h2up():
-        return rc(a2s.at[1, 2:10, 1], a2h.at[1], h2s.at[0], h2r.at[0], (x, t - 1))
-
-    def h2down():
-        return rc(a2s.at[1, 2:10, 2], a2h.at[0], h2s.at[1], h2r.at[1], (x, t + 1))
-
     @pl.when(t > 0)
     def _():
-        h2up().start()
+        got(ssbuf.at[4:8], ssr.at[1])
+        got(a2h.at[0], h2r.at[1])
 
     @pl.when(t < 63)
     def _():
-        h2down().start()
-
-    step2(3)
+        got(ssbuf.at[8:12], ssr.at[2])
+        got(a2h.at[1], h2r.at[0])
+
+    above = (ssbuf[4] + ssbuf[5]) + (ssbuf[6] + ssbuf[7])
+    below = (ssbuf[8] + ssbuf[9]) + (ssbuf[10] + ssbuf[11])
+    ssbuf[13] = jnp.where(lane8 >= 64, above, below)
+
+    def halo2(f, carry):
+        ms = jnp.transpose(jnp.broadcast_to(ssbuf[13, pl.ds(f, 1)], (128, 128))) * (1.0 / 384.0)
+        hv = jnp.concatenate([a2h[1, f], a2h[0, f]], axis=0).astype(F32)
+        v = silu(hv * lax.rsqrt(ms + 1e-6) * gain2)
+        spread(f, 0, v[64:128])
+        spread(f, 3, v[0:64])
+        return carry
+
+    lax.fori_loop(0, 8, halo2, 0, unroll=2)
     step2(4)
-
-    @pl.when(t > 0)
-    def _():
-        got(a2h.at[0], h2r.at[1])
-
-    @pl.when(t == 0)
-    def _():
-        a2h[0] = jnp.zeros((8, 64, 128), BF16)
-
-    @pl.when(t < 63)
-    def _():
-        got(a2h.at[1], h2r.at[0])
-
-    @pl.when(t == 63)
-    def _():
-        a2h[1] = jnp.zeros((8, 64, 128), BF16)
-
-    def halo2(f, carry):
-        spread(f, 0, a2h[0, f].astype(F32))
-        spread(f, 3, a2h[1, f].astype(F32))
-        return carry
-
-    lax.fori_loop(0, 8, halo2, 0)
 
     def conv2(q):
         acc = None
@@ -649,11 +700,11 @@
 
     @pl.when(j == 7)
     def _():
-        gone(28 * 32, st1s.at[0])
+        gone((7 + 3 * WHOLE) * 32, st1s.at[0])
 
     @pl.when(j != 7)
     def _():
-        gone(27 * 32, st1s.at[0])
+        gone((6 + 3 * WHOLE) * 32, st1s.at[0])
 
     @pl.when(x != y)
     def _():
@@ -664,17 +715,23 @@
         gone(7 * 48, st2s.at[0])
 
     gone(3 * 768, xs.at[0])
-    rc(ssbuf.at[1:4], ssbuf.at[1:4], sss.at[0], loc.at[2], (x, t)).wait_send()
+    def ss_gone(count, i):
+        size = ssbuf.at[0:count]
+        rc(size, size, sss.at[i], loc.at[2], (x, t)).wait_send()
+
+    ss_gone(3, 0)
     gone(3 * 768, fs.at[0])
 
     @pl.when(t > 0)
     def _():
         gone(4 * 384, ups.at[0])
+        ss_gone(4, 1)
         h2up().wait_send()
 
     @pl.when(t < 63)
     def _():
         gone(4 * 384, dns.at[0])
+        ss_gone(4, 2)
         h2down().wait_send()
 
     step2_sent()
@@ -706,15 +763,16 @@
             pltpu.VMEM((4, 2, 4, 64, 384), BF16),
             pltpu.VMEM((4, 10, 2, 64, 256), F32),
             pltpu.VMEM((8, 2, 64, 128), F32),
-            pltpu.VMEM((5, 8, 128), F32),
+            pltpu.VMEM((8, 2, 64, 128), BF16),
+            pltpu.VMEM((14, 8, 128), F32),
             pltpu.VMEM((3, 10, 4, 64, 128), BF16),
             pltpu.VMEM((2, 8, 64, 128), BF16),
             pltpu.VMEM((3, 2, 2, 64, 384), BF16),
             pltpu.VMEM((3, 2, 2, 64, 384), BF16),
             dma((7,)), dma((1,)), dma((4,)), dma((1,)), dma((1,)), dma((3,)),
-            dma((1,)), dma((17,)), dma((2,)), dma((6,)), dma((1,)), dma((9,)), dma((2,)), dma((2,)),
+            dma((1,)), dma((17,)), dma((2,)), dma((2, 19)), dma((1,)), dma((9,)), dma((2,)), dma((2,)),
             dma((1,)), dma((4,)), dma((1,)), dma((1,)), dma((1,)), dma((1,)),
-            dma((1,)), dma((1,)), dma((2,)), dma((2,)), dma((1,)), dma((4,)),
+            dma((3,)), dma((3,)), dma((2,)), dma((2,)), dma((1,)), dma((4,)),
         ],
         compiler_params=pltpu.CompilerParams(
             collective_id=0, has_side_effects=True, vmem_limit_bytes=63 * 1024 * 1024

time: 67.8 us -> 63.5 us (0.937); the launches traced: 66.4 us -> 63.4 us
  Pallas kernels: 64.8 us -> 61.8 us
    pallas_call x1, Pallas kernels: 64.8 us -> 61.8 us  [per_device(): pl.pallas_call(kernel, out_shape=jax.ShapeDtypeStruct((2, 2, 64, 384), BF...]
where the time goes in v6:
time: 63.5 us; the launch traced here: 63.4 us
  Pallas kernels  61.8 us (97%)
  local copies, waits for them, and re-layouts  1.62 us (3%)
    pallas_call x1, Pallas kernels, per_device(): pl.pallas_call(kernel, out_shape=jax.ShapeDtypeStruct((2, 2, 64, 384), BF...  61.8 us
    unnamed x1, local copies, waits for them, and re-layouts  1.62 us

profile of v6, /device:TPU:1, one launch (start us, length us, event | category | flops | bytes accessed | tf_op | source)
XLA Modules:
  0.0 63.4 jit_solution(2275019663062563027)
XLA Ops:
  0.0 61.8 %shard_map.73 = bf16[2,2,64,384]{3,2,1,0:T(8,128)(2,1)} custom-call(bf16[2,2,64,384]{3,2,1,0:T(8,128)(2,1)} %lat_hbm.1, f32[384]{0:T(512)} %gain1_hbm.1, f32[384]{0:T(512)} %bias1_hbm.1, f32[384]{0:T(512)} %gain2_hbm.1, f32[384]{0:T(512)} %bias2_hbm.1, bf16[27,6,384]{2,1,0:T(8,128)(2,1)} %bitcast.2, bf16[27,6,384]{2,1,0:T(8,128)(2,1)} %bitcast.3), custom_call_target="tpu_custom_call" | custom-call | flops 4000000000 | bytes 8000000 | tf_op jit(solution)/shard_map/pallas_call | solution.py:745
  61.8 1.6 %copy.9 = bf16[2,2,64,384]{3,2,1,0:T(8,128)(2,1)} copy(bf16[2,2,64,384]{3,2,1,0:T(8,128)(2,1)} %shard_map.73) | data formatting | bytes 393216

commit v7 on v6

--- a/solution.py
+++ b/solution.py
@@ -314,7 +314,7 @@
 
     def b_y(d, s):
         ref = blk(0, y, zz(s), c)
-        return rc(ref, ref, ysend.at[0], yrecv.at[0, d - 1], dev(yy_of(d), z, c))
+        return rc(ref, ref, ysend.at[0], yrecv.at[5 + d - 1], dev(yy_of(d), z, c))
 
     def b_sib(core, d):
         yy = lax.rem(y + d, 4)
@@ -394,7 +394,7 @@
             def arrived(core, count):
                 if count:
                     for d in (1, 3, 2):
-                        came(count * 144, yrecv.at[0, d - 1])
+                        came(count * 144, yrecv.at[5 + d - 1])
                         b_sib(core, 4 - d).start()
 
             on_core(0, lambda: arrived(0, 8))
@@ -436,23 +436,25 @@
     def z2_got(total):
         got(blk(1, y, zz(-total), c), rrecv.at[WAY[total]])
 
+    EARLY = (0, 2, -2)
+    LATE = (1, -1, 3, -3, 4)
+
     def y2_one(d, origin, step):
-        ref = blk(1, yy_of(4 + origin), zz(step), c)
-        k = 18 if origin else WAY[step] + 9 * (d // 2)
-        return rc(ref, ref, ysend.at[1], yrecv.at[1, k], dev(yy_of(d), z, c))
+        ref = blk(1, yy_of(4 + origin), zz(step), 0)
+        k = 4 if origin else 2 * (d // 2) + (step in LATE)
+        return rc(ref, ref, ysend.at[1], yrecv.at[k], dev(yy_of(d), z, 0))
 
     def y2_send(origin):
         for d in (1, 3):
             y2_one(d, 0, origin).start()
 
-    def y2_relay(*steps):
-        for k in steps:
-            got(blk(1, yy_of(3), zz(k), c), yrecv.at[1, WAY[k]])
-            if k in UP:
-                y2_one(1, -1, k).start()
-            got(blk(1, yy_of(1), zz(k), c), yrecv.at[1, WAY[k] + 9])
-            if k not in UP:
-                y2_one(3, 1, k).start()
+    def y2_relay(group):
+        steps = LATE if group else EARLY
+        for k, (d, back) in enumerate(((1, -1), (3, 1))):
+            came(len(steps) * 144, yrecv.at[2 * k + group])
+            for step in steps:
+                if (step in UP) == (d == 1):
+                    y2_one(d, back, step).start()
 
     def sib2_send(d):
         ref = wset(lax.rem(y + d, 4), c)
@@ -460,32 +462,96 @@
 
     Z2 = ((0, 2), (0, -2), (0, 1), (0, -1), (-2, 4), (-2, 3), (2, -3))
 
+    def col(origin):
+        zo = zz(origin)
+        return w2.at[:, lax.rem(zo, 4), 1, pl.ds(pl.multiple_of(48 * lax.div(zo, 4), 16), 48), :]
+
+    def y2_own(d):
+        ref = blk(1, y, z, 1)
+        return rc(ref, ref, ysend.at[1], yrecv.at[4], dev(yy_of(d), z, 1))
+
+    def z2_col(e, origin, total):
+        ref = blk(1, yy_of(e), zz(origin), 1)
+        i = WAY[total]
+        k = 9 + 4 * (i - 2) + e if total in (2, -2) else i
+        return rc(ref, ref, rsend.at[0], rrecv.at[k], dev(y, zz(origin + total), 1))
+
+    def col_sib(origin):
+        ref = col(origin)
+        return rc(ref, ref, bsend.at[1], brecv.at[1], dev(y, z, 0))
+
     def step2(n):
-        if n == 0:
-            for origin, total in Z2[:4]:
-                z2_send(origin, total).start()
-        if n == 1:
-            z2_got(2)
-            z2_send(-2, 4).start()
-            z2_send(-2, 3).start()
-            z2_got(-2)
-            z2_send(2, -3).start()
-        if n == 2:
-            for origin in (0, 2, -2):
-                y2_send(origin)
-            for total, origin in ((1, -1), (-1, 1), (3, -3), (-3, 3), (4, 4)):
-                z2_got(total)
-                y2_send(origin)
-            sib2_send(0).start()
-        if n == 3:
-            came(8 * 144, yrecv.at[1, 18])
-            sib2_send(2).start()
-        if n == 4:
+        def core0():
+            if n == 0:
+                for origin, total in Z2[:4]:
+                    z2_send(origin, total).start()
+            if n == 1:
+                z2_got(2)
+                z2_send(-2, 4).start()
+                z2_send(-2, 3).start()
+                z2_got(-2)
+                z2_send(2, -3).start()
+            if n == 2:
+                for origin in EARLY:
+                    y2_send(origin)
+                for total, origin in ((1, -1), (-1, 1), (3, -3), (-3, 3), (4, 4)):
+                    z2_got(total)
+                    y2_send(origin)
+                sib2_send(0).start()
+            if n == 4:
+                y2_relay(0)
+            if n == 5:
+                y2_relay(1)
+                sib2_send(1).start()
+                sib2_send(3).start()
+            if n == 6:
+                came(8 * 144, yrecv.at[4])
+                sib2_send(2).start()
+
+        def core1():
+            if n == 0:
+                for d in (2, 1, 3):
+                    y2_own(d).start()
+            if n == 1:
+                came(3 * 144, yrecv.at[4])
+                for e in (0, 1, 3, 2):
+                    for total in AROUND:
+                        z2_col(e, 0, total).start()
+                col_sib(0).start()
+            if n == 3:
+                for total in (2, -2):
+                    for e in (0, 1, 3, 2):
+                        got(blk(1, yy_of(e), zz(-total), 1), rrecv.at[9 + 4 * (WAY[total] - 2) + e])
+                        for origin, far in a_relays(e, total):
+                            z2_col(e, origin, far).start()
+                    col_sib(-total).start()
+                for total in (1, -1):
+                    came(4 * 144, rrecv.at[WAY[total]])
+                    col_sib(-total).start()
+            if n == 5:
+                for total in (3, -3):
+                    came(4 * 144, rrecv.at[WAY[total]])
+                    col_sib(-total).start()
+                came(2 * 144, rrecv.at[WAY[4]])
+                came(2 * 144, rrecv.at[WAY[-4]])
+                col_sib(4).start()
+
+        on_core(0, core0)
+        on_core(1, core1)
+        if n == 7:
             came(32 * 144, brecv.at[1])
 
     def step2_sent():
-        gone(7 * 144, rsend.at[0])
-        gone(24 * 144, ysend.at[1])
+        def core0():
+            gone(7 * 144, rsend.at[0])
+            gone(24 * 144, ysend.at[1])
+
+        def core1():
+            gone(28 * 144, rsend.at[0])
+            gone(3 * 144, ysend.at[1])
+
+        on_core(0, core0)
+        on_core(1, core1)
         gone(32 * 144, bsend.at[1])
 
     own1.wait()
@@ -517,13 +583,14 @@
     w2[y, zi, c, pl.ds(pl.multiple_of(48 * h, 16), 48), :] = stack[...].astype(BF16)
     step2(0)
     step(2)
-    step2(1)
     xstep(1)
     xstep(3)
+    step2(1)
+    xstep(2)
     step(3)
-    xstep(2)
     step2(2)
     step(4)
+    step2(3)
     halo_wait()
     step(5)
 
@@ -544,14 +611,12 @@
 
         tile(0, 0)
         tile(1, 0)
-        y2_relay(0, 2, -2)
+        step2(4)
         tile(2, 0)
         tile(3, 0)
 
     conv1()
-    y2_relay(1, -1, 3, -3, 4)
-    sib2_send(1).start()
-    sib2_send(3).start()
+    step2(5)
 
     lane = lax.broadcasted_iota(jnp.int32, (64, 128), 1)
     row = lax.broadcasted_iota(jnp.int32, (64, 128), 0)
@@ -625,7 +690,7 @@
         a2h[1] = jnp.zeros((8, 64, 128), BF16)
         ssbuf[8:12] = jnp.zeros((4, 8, 128), F32)
 
-    step2(3)
+    step2(6)
     sizes = ssbuf.at[1:4]
     got(sizes, ssr.at[0])
     ssbuf[12] = (ssbuf[0] + ssbuf[1]) + (ssbuf[2] + ssbuf[3])
@@ -668,7 +733,7 @@
         return carry
 
     lax.fori_loop(0, 8, halo2, 0, unroll=2)
-    step2(4)
+    step2(7)
 
     def conv2(q):
         acc = None
@@ -770,7 +835,7 @@
             pltpu.VMEM((3, 2, 2, 64, 384), BF16),
             pltpu.VMEM((3, 2, 2, 64, 384), BF16),
             dma((7,)), dma((1,)), dma((4,)), dma((1,)), dma((1,)), dma((3,)),
-            dma((1,)), dma((17,)), dma((2,)), dma((2, 19)), dma((1,)), dma((9,)), dma((2,)), dma((2,)),
+            dma((1,)), dma((17,)), dma((2,)), dma((8,)), dma((1,)), dma((17,)), dma((2,)), dma((2,)),
             dma((1,)), dma((4,)), dma((1,)), dma((1,)), dma((1,)), dma((1,)),
             dma((3,)), dma((3,)), dma((2,)), dma((2,)), dma((1,)), dma((4,)),
         ],

time: 63.5 us -> 61.7 us (0.972)
  Pallas kernels: 61.8 us -> 60 us
    pallas_call x1, Pallas kernels: 61.8 us -> 60 us  [per_device(): pl.pallas_call(kernel, out_shape=jax.ShapeDtypeStruct((2, 2, 64, 384), BF...]
where the time goes in v7:
time: 61.7 us; the launch traced here: 61.6 us
  Pallas kernels  60 us (97%)
  local copies, waits for them, and re-layouts  1.62 us (3%)
    pallas_call x1, Pallas kernels, per_device(): pl.pallas_call(kernel, out_shape=jax.ShapeDtypeStruct((2, 2, 64, 384), BF...  60 us
    unnamed x1, local copies, waits for them, and re-layouts  1.62 us

profile of v7, /device:TPU:1, one launch (start us, length us, event | category | flops | bytes accessed | tf_op | source)
XLA Modules:
  0.0 61.6 jit_solution(12312019283093142557)
XLA Ops:
  0.0 60.0 %shard_map.73 = bf16[2,2,64,384]{3,2,1,0:T(8,128)(2,1)} custom-call(bf16[2,2,64,384]{3,2,1,0:T(8,128)(2,1)} %lat_hbm.1, f32[384]{0:T(512)} %gain1_hbm.1, f32[384]{0:T(512)} %bias1_hbm.1, f32[384]{0:T(512)} %gain2_hbm.1, f32[384]{0:T(512)} %bias2_hbm.1, bf16[27,6,384]{2,1,0:T(8,128)(2,1)} %bitcast.2, bf16[27,6,384]{2,1,0:T(8,128)(2,1)} %bitcast.3), custom_call_target="tpu_custom_call" | custom-call | flops 4000000000 | bytes 8000000 | tf_op jit(solution)/shard_map/pallas_call | solution.py:810
  60.0 1.6 %copy.9 = bf16[2,2,64,384]{3,2,1,0:T(8,128)(2,1)} copy(bf16[2,2,64,384]{3,2,1,0:T(8,128)(2,1)} %shard_map.73) | data formatting | bytes 393216

commit v8 on v7

--- a/solution.py
+++ b/solution.py
@@ -8,8 +8,6 @@
 MESH = pl.DeviceIdType.MESH
 F32 = jnp.float32
 BF16 = jnp.bfloat16
-
-WHOLE = 1
 
 SLOTS = ((0, 1), (0, 0), (0, 2), (2, 0), (1, 1), (1, 0), (1, 2), (2, 2), (2, 1))
 
@@ -72,10 +70,10 @@
     def hail(device):
         pl.semaphore_signal(barrier, inc=1, device_id=device, device_id_type=MESH)
 
-    for e in range(4):
-        for d in range(8):
-            if e or d:
-                hail((x, lax.rem(y + e, 4) * 16 + h * 8 + lax.rem(j + d, 8)))
+    for d in range(1, 8):
+        hail((x, g * 8 + lax.rem(j + d, 8)))
+    for d in range(1, 4):
+        hail(dev(lax.rem(y + d, 4), z, c))
 
     @pl.when(x != y)
     def _():
@@ -159,12 +157,12 @@
 
     lax.fori_loop(0, 2, act1, 0)
 
-    many = jnp.where(x != y, 8, 0) + jnp.where(t > 0, 4, 0) + jnp.where(t < 63, 4, 0) + 38
+    many = jnp.where(x != y, 8, 0) + jnp.where(t > 0, 4, 0) + jnp.where(t < 63, 4, 0) + 17
     pl.semaphore_wait(barrier, many)
 
-    def st1(e, d):
+    def st1(d):
         jj = lax.rem(j + d, 8)
-        return rc(s1.at[jj], r1.at[y, j], st1s.at[0], st1r.at[e], (x, lax.rem(y + e, 4) * 16 + h * 8 + jj))
+        return rc(s1.at[jj], r1.at[j], st1s.at[0], st1r.at[0], (x, g * 8 + jj))
 
     def st2(d):
         jj = lax.rem(j + d, 8)
@@ -173,16 +171,13 @@
     def own2():
         return pltpu.make_async_copy(s2.at[j], r2.at[j], loc.at[1])
 
-    for e in (2, 1, 3):
-        for k in range(WHOLE):
-            st1(e, lax.rem(9 + 2 * k - j, 8)).start()
     for d in range(1, 8):
 
         @pl.when(lax.rem(j + d, 8) != 7)
         def _():
-            st1(0, d).start()
-
-    own1 = pltpu.make_async_copy(s1.at[j], r1.at[y, j], loc.at[0])
+            st1(d).start()
+
+    own1 = pltpu.make_async_copy(s1.at[j], r1.at[j], loc.at[0])
     own1.start()
 
     def xsend(d):
@@ -267,15 +262,10 @@
     def zi_of(origin):
         return lax.rem(z + 8 + origin, 4)
 
-    def when_a(origin, f):
-        @pl.when(jnp.logical_and(c == 1, zi_of(origin) < WHOLE))
-        def _():
-            f()
-
     def when_b(origin, f):
         k = zi_of(origin)
 
-        @pl.when(jnp.logical_or(c == 0, jnp.logical_and(k >= WHOLE, k <= 2)))
+        @pl.when(jnp.logical_or(c == 0, k <= 2))
         def _():
             f()
 
@@ -283,25 +273,12 @@
         @pl.when(c == core)
         def _():
             f()
-
-    def a_z(e, origin, total):
-        ref = blk(0, yy_of(e), zz(origin), 1)
-        i = WAY[total]
-        k = 9 + 4 * (i - 2) + e if total in (2, -2) else i
-        return rc(ref, ref, w1zs.at[0], w1zr.at[k], dev(y, zz(origin + total), 1))
-
-    def a_got(e, total):
-        got(blk(0, yy_of(e), zz(-total), 1), w1zr.at[9 + 4 * (WAY[total] - 2) + e])
 
     def a_relays(e, total):
         if total == 2:
             return ((-2, 3), (-2, 4)) if e < 2 else ((-2, 3),)
         return ((2, -3), (2, -4)) if e >= 2 else ((2, -3),)
 
-    def a_sib(s):
-        ref = zset(zz(s))
-        return rc(ref, ref, bsend.at[0], brecv.at[0], dev(y, z, 0))
-
     def b_z(origin, total):
         ref = blk(0, y, zz(origin), c)
         i = WAY[total]
@@ -318,38 +295,24 @@
 
     def b_sib(core, d):
         yy = lax.rem(y + d, 4)
-        ref = w1.at[0, :, :, yy] if core == 0 else w1.at[1, WHOLE:3, :, yy]
+        ref = w1.at[0, :, :, yy] if core == 0 else w1.at[1, 0:3, :, yy]
         return rc(ref, ref, bsend.at[0], brecv.at[0], dev(y, z, 1 - core))
 
     def y_all(origin):
         for d in (2, 1, 3):
             b_y(d, origin).start()
 
-    def first(e):
-        def send_a():
+    def first():
+        def send():
             for total in AROUND:
-                a_z(e, 0, total).start()
-
-        when_a(0, send_a)
-        if e == 0:
-
-            def send_b():
-                for total in AROUND:
-                    b_z(0, total).start()
-                y_all(0)
-
-            when_b(0, send_b)
+                b_z(0, total).start()
+            y_all(0)
+
+        when_b(0, send)
 
     def step(n):
         if n == 1:
             for total in (2, -2):
-
-                def relay(total=total):
-                    for e in (0, 1, 3, 2):
-                        a_got(e, total)
-                        for origin, far in a_relays(e, total):
-                            a_z(e, origin, far).start()
-                    a_sib(-total).start()
 
                 def take(total=total):
                     b_got(total)
@@ -357,48 +320,33 @@
                         b_z(origin, far).start()
                     y_all(-total)
 
-                when_a(-total, relay)
                 when_b(-total, take)
-            when_a(0, lambda: a_sib(0).start())
         if n == 2 or n == 3:
             for total in ((1, -1) if n == 2 else (3, -3)):
-
-                def whole(total=total):
-                    came(4 * 144, w1zr.at[WAY[total]])
-                    a_sib(-total).start()
 
                 def take(total=total):
                     b_got(total)
                     y_all(-total)
 
-                when_a(-total, whole)
                 when_b(-total, take)
         if n == 3:
-
-            def last():
-                came(2 * 144, w1zr.at[WAY[4]])
-                came(2 * 144, w1zr.at[WAY[-4]])
-                a_sib(4).start()
 
             def take4():
                 b_got(4)
                 y_all(4)
 
-            when_a(4, last)
             when_b(4, take4)
             on_core(0, lambda: b_sib(0, 0).start())
-            if WHOLE < 3:
-                on_core(1, lambda: b_sib(1, 0).start())
+            on_core(1, lambda: b_sib(1, 0).start())
         if n == 4:
 
             def arrived(core, count):
-                if count:
-                    for d in (1, 3, 2):
-                        came(count * 144, yrecv.at[5 + d - 1])
-                        b_sib(core, 4 - d).start()
+                for d in (1, 3, 2):
+                    came(count * 144, yrecv.at[5 + d - 1])
+                    b_sib(core, 4 - d).start()
 
             on_core(0, lambda: arrived(0, 8))
-            on_core(1, lambda: arrived(1, 2 * (3 - WHOLE)))
+            on_core(1, lambda: arrived(1, 6))
         if n == 5:
             on_core(0, lambda: came(24 * 144, brecv.at[0]))
             on_core(1, lambda: came(32 * 144, brecv.at[0]))
@@ -410,19 +358,13 @@
             gone(32 * 144, bsend.at[0])
 
         on_core(0, core0)
-        def sends(k, whole, block):
-            return 0 if k == 3 else whole if k < WHOLE else block
-
-        for k in range(4):
-            along_z = sends(k, 16, 4) + sends((k + 2) % 4, 12, 3)
-            along_y = 6 * (3 - WHOLE)
+        for k, along_z in enumerate((7, 4, 7, 3)):
 
             @pl.when(jnp.logical_and(c == 1, zi == k))
             def _():
                 gone(along_z * 144, w1zs.at[0])
-                if along_y:
-                    gone(along_y * 144, ysend.at[0])
-
+
+        on_core(1, lambda: gone(18 * 144, ysend.at[0]))
         on_core(1, lambda: gone(24 * 144, bsend.at[0]))
 
     def wset(yy, cc):
@@ -475,6 +417,22 @@
         i = WAY[total]
         k = 9 + 4 * (i - 2) + e if total in (2, -2) else i
         return rc(ref, ref, rsend.at[0], rrecv.at[k], dev(y, zz(origin + total), 1))
+
+    def when_used(e, origin, f):
+        @pl.when(jnp.logical_not(jnp.logical_and(yy_of(e) == 3, zi_of(origin) > 0)))
+        def _():
+            f()
+
+    def col_came(total):
+        k = WAY[total]
+
+        @pl.when(zi_of(-total) > 0)
+        def _():
+            came(3 * 144, rrecv.at[k])
+
+        @pl.when(zi_of(-total) == 0)
+        def _():
+            came(4 * 144, rrecv.at[k])
 
     def col_sib(origin):
         ref = col(origin)
@@ -515,25 +473,42 @@
             if n == 1:
                 came(3 * 144, yrecv.at[4])
                 for e in (0, 1, 3, 2):
-                    for total in AROUND:
-                        z2_col(e, 0, total).start()
+
+                    def send(e=e):
+                        for total in AROUND:
+                            z2_col(e, 0, total).start()
+
+                    when_used(e, 0, send)
                 col_sib(0).start()
             if n == 3:
                 for total in (2, -2):
                     for e in (0, 1, 3, 2):
-                        got(blk(1, yy_of(e), zz(-total), 1), rrecv.at[9 + 4 * (WAY[total] - 2) + e])
-                        for origin, far in a_relays(e, total):
-                            z2_col(e, origin, far).start()
+
+                        def relay(e=e, total=total):
+                            got(blk(1, yy_of(e), zz(-total), 1), rrecv.at[9 + 4 * (WAY[total] - 2) + e])
+                            for origin, far in a_relays(e, total):
+                                z2_col(e, origin, far).start()
+
+                        when_used(e, -total, relay)
                     col_sib(-total).start()
                 for total in (1, -1):
-                    came(4 * 144, rrecv.at[WAY[total]])
+                    col_came(total)
                     col_sib(-total).start()
             if n == 5:
                 for total in (3, -3):
-                    came(4 * 144, rrecv.at[WAY[total]])
+                    col_came(total)
                     col_sib(-total).start()
-                came(2 * 144, rrecv.at[WAY[4]])
-                came(2 * 144, rrecv.at[WAY[-4]])
+                for way, rows in ((4, (0, 1)), (-4, (2, 3))):
+                    short = jnp.logical_and(zi_of(4) > 0, jnp.logical_or(yy_of(rows[0]) == 3, yy_of(rows[1]) == 3))
+
+                    @pl.when(short)
+                    def _():
+                        came(144, rrecv.at[WAY[way]])
+
+                    @pl.when(jnp.logical_not(short))
+                    def _():
+                        came(2 * 144, rrecv.at[WAY[way]])
+
                 col_sib(4).start()
 
         on_core(0, core0)
@@ -547,7 +522,12 @@
             gone(24 * 144, ysend.at[1])
 
         def core1():
-            gone(28 * 144, rsend.at[0])
+            for k in range(4):
+
+                @pl.when(zi == k)
+                def _():
+                    gone(((16 if k == 0 else 12) + (12 if k == 2 else 9)) * 144, rsend.at[0])
+
             gone(3 * 144, ysend.at[1])
 
         on_core(0, core0)
@@ -555,19 +535,17 @@
         gone(32 * 144, bsend.at[1])
 
     own1.wait()
-    for e in (0, 1, 3, 2):
-        src = lax.rem(y + e, 4)
-
-        @pl.when(jnp.logical_and(c == 1, zi < WHOLE) if e else j != 7)
-        def _():
-            came(8 * 32 if e else 7 * 32, st1r.at[(4 - e) % 4])
-            for dy in range(3):
-                for m in range(8):
-                    two = r1[src, m, 16 * (dy // 2):16 * (dy // 2) + 16].astype(F32)
-                    stack[m * 6:m * 6 + 6, 0:128] = two[(dy % 2) * 8:(dy % 2) * 8 + 6]
-                w1[c, zi, dy, src, h] = stack[:, 0:128].astype(BF16)
-
-        first(e)
+
+    @pl.when(j != 7)
+    def _():
+        came(7 * 32, st1r.at[0])
+        for dy in range(3):
+            for m in range(8):
+                two = r1[m, 16 * (dy // 2):16 * (dy // 2) + 16].astype(F32)
+                stack[m * 6:m * 6 + 6, 0:128] = two[(dy % 2) * 8:(dy % 2) * 8 + 6]
+            w1[c, zi, dy, y, h] = stack[:, 0:128].astype(BF16)
+
+    first()
     step(1)
     @pl.when(x != y)
     def _():
@@ -732,7 +710,13 @@
         spread(f, 3, v[0:64])
         return carry
 
-    lax.fori_loop(0, 8, halo2, 0, unroll=2)
+    def halo_pair(d):
+        first_frame = 2 * lax.rem(x + d, 4)
+        for f in range(2):
+            halo2(first_frame + f, 0)
+
+    halo_pair(1)
+    halo_pair(2)
     step2(7)
 
     def conv2(q):
@@ -754,9 +738,11 @@
     def out_send(d):
         return rc(sendb.at[d - 1], recvb.at[d - 1], fs.at[0], fr.at[d], (lax.rem(x + d, 4), t))
 
-    for d in (2, 1, 3):
+    for d, ready in ((2, 3), (3, 0), (1, None)):
         sendb[d - 1] = conv2(lax.rem(x + d, 4)).astype(BF16).reshape(2, 2, 64, 384)
         out_send(d).start()
+        if ready is not None:
+            halo_pair(ready)
     mine = conv2(x) + bias2 + lat[...].reshape(256, 384).astype(F32)
     for d in (2, 1, 3):
         got(recvb.at[d - 1], fr.at[d])
@@ -765,11 +751,11 @@
 
     @pl.when(j == 7)
     def _():
-        gone((7 + 3 * WHOLE) * 32, st1s.at[0])
+        gone(7 * 32, st1s.at[0])
 
     @pl.when(j != 7)
     def _():
-        gone((6 + 3 * WHOLE) * 32, st1s.at[0])
+        gone(6 * 32, st1s.at[0])
 
     @pl.when(x != y)
     def _():
@@ -821,7 +807,7 @@
             pltpu.VMEM((8, 16, 384), BF16),
             pltpu.VMEM((48, 384), F32),
             pltpu.VMEM((4608, 128), BF16),
-            pltpu.VMEM((4, 8, 32, 128), BF16),
+            pltpu.VMEM((8, 32, 128), BF16),
             pltpu.VMEM((8, 16, 384), BF16),
             pltpu.VMEM((2, 4, 3, 4, 2, 48, 128), BF16),
             pltpu.VMEM((4, 4, 2, 128, 384), BF16),
@@ -834,8 +820,8 @@
             pltpu.VMEM((2, 8, 64, 128), BF16),
             pltpu.VMEM((3, 2, 2, 64, 384), BF16),
             pltpu.VMEM((3, 2, 2, 64, 384), BF16),
-            dma((7,)), dma((1,)), dma((4,)), dma((1,)), dma((1,)), dma((3,)),
-            dma((1,)), dma((17,)), dma((2,)), dma((8,)), dma((1,)), dma((17,)), dma((2,)), dma((2,)),
+            dma((7,)), dma((1,)), dma((1,)), dma((1,)), dma((1,)), dma((3,)),
+            dma((1,)), dma((9,)), dma((2,)), dma((8,)), dma((1,)), dma((17,)), dma((2,)), dma((2,)),
             dma((1,)), dma((4,)), dma((1,)), dma((1,)), dma((1,)), dma((1,)),
             dma((3,)), dma((3,)), dma((2,)), dma((2,)), dma((1,)), dma((4,)),
         ],

time: 61.7 us -> 59.5 us (0.964)
  Pallas kernels: 60 us -> 57.8 us
    pallas_call x1, Pallas kernels: 60 us -> 57.8 us  [per_device(): pl.pallas_call(kernel, out_shape=jax.ShapeDtypeStruct((2, 2, 64, 384), BF...]
where the time goes in v8:
time: 59.5 us; the launch traced here: 59.4 us
  Pallas kernels  57.8 us (97%)
  local copies, waits for them, and re-layouts  1.62 us (3%)
    pallas_call x1, Pallas kernels, per_device(): pl.pallas_call(kernel, out_shape=jax.ShapeDtypeStruct((2, 2, 64, 384), BF...  57.8 us
    unnamed x1, local copies, waits for them, and re-layouts  1.62 us

profile of v8, /device:TPU:1, one launch (start us, length us, event | category | flops | bytes accessed | tf_op | source)
XLA Modules:
  0.0 59.4 jit_solution(18417341629568108990)
XLA Ops:
  0.0 57.8 %shard_map.73 = bf16[2,2,64,384]{3,2,1,0:T(8,128)(2,1)} custom-call(bf16[2,2,64,384]{3,2,1,0:T(8,128)(2,1)} %lat_hbm.1, f32[384]{0:T(512)} %gain1_hbm.1, f32[384]{0:T(512)} %bias1_hbm.1, f32[384]{0:T(512)} %gain2_hbm.1, f32[384]{0:T(512)} %bias2_hbm.1, bf16[27,6,384]{2,1,0:T(8,128)(2,1)} %bitcast.2, bf16[27,6,384]{2,1,0:T(8,128)(2,1)} %bitcast.3), custom_call_target="tpu_custom_call" | custom-call | flops 4000000000 | bytes 8000000 | tf_op jit(solution)/shard_map/pallas_call | solution.py:796
  57.8 1.6 %copy.9 = bf16[2,2,64,384]{3,2,1,0:T(8,128)(2,1)} copy(bf16[2,2,64,384]{3,2,1,0:T(8,128)(2,1)} %shard_map.73) | data formatting | bytes 393216

commit v9 on v8

--- a/solution.py
+++ b/solution.py
@@ -19,7 +19,7 @@
 def kernel(
     lat_hbm, gain1_hbm, bias1_hbm, gain2_hbm, bias2_hbm, k1_hbm, k2_hbm, out,
     lat, vec, k1, k2, s1, s2, stack,
-    ruler, r1, r2, w1, w2, abuf, pbuf, hbuf, hedge, ssbuf, a2s, a2h, sendb, recvb,
+    ruler, r1, r2, w1, w2, abuf, pbuf, hbuf, hedge, ssbuf, a2s, a2h, sendb, recvb, hop, keep,
     ins, st1s, st1r, st2s, st2r, loc,
     w1zs, w1zr, ysend, yrecv, rsend, rrecv, bsend, brecv,
     xs, xr, ups, upr, dns, dnr, sss, ssr, h2s, h2r, fs, fr,
@@ -452,6 +452,7 @@
             if n == 2:
                 for origin in EARLY:
                     y2_send(origin)
+            if n == 8:
                 for total, origin in ((1, -1), (-1, 1), (3, -3), (-3, 3), (4, 4)):
                     z2_got(total)
                     y2_send(origin)
@@ -568,6 +569,7 @@
     step(3)
     step2(2)
     step(4)
+    step2(8)
     step2(3)
     halo_wait()
     step(5)
@@ -735,18 +737,34 @@
             acc = part if acc is None else acc + part
         return acc
 
-    def out_send(d):
-        return rc(sendb.at[d - 1], recvb.at[d - 1], fs.at[0], fr.at[d], (lax.rem(x + d, 4), t))
-
-    for d, ready in ((2, 3), (3, 0), (1, None)):
-        sendb[d - 1] = conv2(lax.rem(x + d, 4)).astype(BF16).reshape(2, 2, 64, 384)
-        out_send(d).start()
-        if ready is not None:
-            halo_pair(ready)
+    def far_send(k):
+        ref = sendb.at[1, k]
+        return rc(ref, hop.at[k], fs.at[0], fr.at[k], (lax.rem(x + (1, 3)[k], 4), t))
+
+    def out_send(k, f):
+        return rc(sendb.at[2 * k, f], recvb.at[k, f], fs.at[0], fr.at[2 + k], (lax.rem(x + (1, 3)[k], 4), t))
+
+    sendb[1] = conv2(lax.rem(x + 2, 4)).astype(BF16).reshape(2, 2, 64, 384)
+    for k in range(2):
+        far_send(k).start()
+    halo_pair(3)
+    part = conv2(lax.rem(x + 3, 4))
+    sendb[2, 0] = part[0:128].astype(BF16).reshape(2, 64, 384)
+    out_send(1, 0).start()
+    keep[1] = part[128:256]
+    halo_pair(0)
+    part = conv2(lax.rem(x + 1, 4))
+    sendb[0, 1] = part[128:256].astype(BF16).reshape(2, 64, 384)
+    out_send(0, 1).start()
+    keep[0] = part[0:128]
     mine = conv2(x) + bias2 + lat[...].reshape(256, 384).astype(F32)
-    for d in (2, 1, 3):
-        got(recvb.at[d - 1], fr.at[d])
-        mine = mine + recvb[d - 1].reshape(256, 384).astype(F32)
+    for k in range(2):
+        got(hop.at[k], fr.at[k])
+        sendb[2 * k, k] = (keep[k] + hop[k].reshape(128, 384).astype(F32)).astype(BF16).reshape(2, 64, 384)
+        out_send(k, k).start()
+    for k in range(2):
+        got(recvb.at[k], fr.at[2 + k])
+        mine = mine + recvb[k].reshape(256, 384).astype(F32)
     out[...] = mine.astype(BF16).reshape(2, 2, 64, 384)
 
     @pl.when(j == 7)
@@ -819,7 +837,9 @@
             pltpu.VMEM((3, 10, 4, 64, 128), BF16),
             pltpu.VMEM((2, 8, 64, 128), BF16),
             pltpu.VMEM((3, 2, 2, 64, 384), BF16),
-            pltpu.VMEM((3, 2, 2, 64, 384), BF16),
+            pltpu.VMEM((2, 2, 2, 64, 384), BF16),
+            pltpu.VMEM((2, 2, 64, 384), BF16),
+            pltpu.VMEM((2, 128, 384), F32),
             dma((7,)), dma((1,)), dma((1,)), dma((1,)), dma((1,)), dma((3,)),
             dma((1,)), dma((9,)), dma((2,)), dma((8,)), dma((1,)), dma((17,)), dma((2,)), dma((2,)),
             dma((1,)), dma((4,)), dma((1,)), dma((1,)), dma((1,)), dma((1,)),

time: 59.5 us -> 57.9 us (0.973)
  Pallas kernels: 57.8 us -> 56.1 us
    pallas_call x1, Pallas kernels: 57.8 us -> 56.1 us  [per_device(): pl.pallas_call(kernel, out_shape=jax.ShapeDtypeStruct((2, 2, 64, 384), BF...]
where the time goes in v9:
time: 57.9 us; the launch traced here: 57.7 us
  Pallas kernels  56.1 us (97%)
  local copies, waits for them, and re-layouts  1.62 us (3%)
    pallas_call x1, Pallas kernels, per_device(): pl.pallas_call(kernel, out_shape=jax.ShapeDtypeStruct((2, 2, 64, 384), BF...  56.1 us
    unnamed x1, local copies, waits for them, and re-layouts  1.62 us

profile of v9, /device:TPU:1, one launch (start us, length us, event | category | flops | bytes accessed | tf_op | source)
XLA Modules:
  0.0 57.7 jit_solution(1139112466398344616)
XLA Ops:
  0.0 56.1 %shard_map.73 = bf16[2,2,64,384]{3,2,1,0:T(8,128)(2,1)} custom-call(bf16[2,2,64,384]{3,2,1,0:T(8,128)(2,1)} %lat_hbm.1, f32[384]{0:T(512)} %gain1_hbm.1, f32[384]{0:T(512)} %bias1_hbm.1, f32[384]{0:T(512)} %gain2_hbm.1, f32[384]{0:T(512)} %bias2_hbm.1, bf16[27,6,384]{2,1,0:T(8,128)(2,1)} %bitcast.2, bf16[27,6,384]{2,1,0:T(8,128)(2,1)} %bitcast.3), custom_call_target="tpu_custom_call" | custom-call | flops 4000000000 | bytes 8000000 | tf_op jit(solution)/shard_map/pallas_call | solution.py:814
  56.1 1.6 %copy.9 = bf16[2,2,64,384]{3,2,1,0:T(8,128)(2,1)} copy(bf16[2,2,64,384]{3,2,1,0:T(8,128)(2,1)} %shard_map.73) | data formatting | bytes 393216

commit v10 on v9

--- a/solution.py
+++ b/solution.py
@@ -628,7 +628,7 @@
         ssbuf[0, pl.ds(f, 1)] = sums
         return carry
 
-    lax.fori_loop(0, 8, combine, 0, unroll=2)
+    lax.fori_loop(0, 8, combine, 0, unroll=8)
 
     def ss_send(d):
         return rc(ssbuf.at[0], ssbuf.at[d], sss.at[0], ssr.at[0], (lax.rem(x + d, 4), t))
@@ -688,7 +688,7 @@
             spread(f, 1 + yy, v[64 * yy:64 * yy + 64])
         return carry
 
-    lax.fori_loop(0, 8, act2, 0, unroll=2)
+    lax.fori_loop(0, 8, act2, 0, unroll=4)
 
     @pl.when(t > 0)
     def _():

time: 57.9 us -> 57.7 us (level)
  no operation moved by 1% of the time
where the time goes in v10:
time: 57.7 us; the launch traced here: 57.6 us
  Pallas kernels  55.9 us (97%)
  local copies, waits for them, and re-layouts  1.62 us (3%)
    pallas_call x1, Pallas kernels, per_device(): pl.pallas_call(kernel, out_shape=jax.ShapeDtypeStruct((2, 2, 64, 384), BF...  55.9 us
    unnamed x1, local copies, waits for them, and re-layouts  1.62 us

profile of v10, /device:TPU:1, one launch (start us, length us, event | category | flops | bytes accessed | tf_op | source)
XLA Modules:
  0.0 57.6 jit_solution(8786714290502554025)
XLA Ops:
  0.0 55.9 %shard_map.73 = bf16[2,2,64,384]{3,2,1,0:T(8,128)(2,1)} custom-call(bf16[2,2,64,384]{3,2,1,0:T(8,128)(2,1)} %lat_hbm.1, f32[384]{0:T(512)} %gain1_hbm.1, f32[384]{0:T(512)} %bias1_hbm.1, f32[384]{0:T(512)} %gain2_hbm.1, f32[384]{0:T(512)} %bias2_hbm.1, bf16[27,6,384]{2,1,0:T(8,128)(2,1)} %bitcast.2, bf16[27,6,384]{2,1,0:T(8,128)(2,1)} %bitcast.3), custom_call_target="tpu_custom_call" | custom-call | flops 4000000000 | bytes 8000000 | tf_op jit(solution)/shard_map/pallas_call | solution.py:814
  55.9 1.6 %copy.9 = bf16[2,2,64,384]{3,2,1,0:T(8,128)(2,1)} copy(bf16[2,2,64,384]{3,2,1,0:T(8,128)(2,1)} %shard_map.73) | data formatting | bytes 393216

commit v11 on v10

--- a/solution.py
+++ b/solution.py
@@ -688,7 +688,7 @@
             spread(f, 1 + yy, v[64 * yy:64 * yy + 64])
         return carry
 
-    lax.fori_loop(0, 8, act2, 0, unroll=4)
+    lax.fori_loop(0, 8, act2, 0, unroll=8)
 
     @pl.when(t > 0)
     def _():

time: 57.7 us -> 57.5 us (level)
  no operation moved by 1% of the time
where the time goes in v11:
time: 57.5 us; the launch traced here: 57.4 us
  Pallas kernels  55.8 us (97%)
  local copies, waits for them, and re-layouts  1.62 us (3%)
    pallas_call x1, Pallas kernels, per_device(): pl.pallas_call(kernel, out_shape=jax.ShapeDtypeStruct((2, 2, 64, 384), BF...  55.8 us
    unnamed x1, local copies, waits for them, and re-layouts  1.62 us

profile of v11, /device:TPU:1, one launch (start us, length us, event | category | flops | bytes accessed | tf_op | source)
XLA Modules:
  0.0 57.4 jit_solution(14505620289515371940)
XLA Ops:
  0.0 55.8 %shard_map.73 = bf16[2,2,64,384]{3,2,1,0:T(8,128)(2,1)} custom-call(bf16[2,2,64,384]{3,2,1,0:T(8,128)(2,1)} %lat_hbm.1, f32[384]{0:T(512)} %gain1_hbm.1, f32[384]{0:T(512)} %bias1_hbm.1, f32[384]{0:T(512)} %gain2_hbm.1, f32[384]{0:T(512)} %bias2_hbm.1, bf16[27,6,384]{2,1,0:T(8,128)(2,1)} %bitcast.2, bf16[27,6,384]{2,1,0:T(8,128)(2,1)} %bitcast.3), custom_call_target="tpu_custom_call" | custom-call | flops 4000000000 | bytes 8000000 | tf_op jit(solution)/shard_map/pallas_call | solution.py:814
  55.8 1.6 %copy.9 = bf16[2,2,64,384]{3,2,1,0:T(8,128)(2,1)} copy(bf16[2,2,64,384]{3,2,1,0:T(8,128)(2,1)} %shard_map.73) | data formatting | bytes 393216
